TPU v7x, 32 devices: a whole 2x2x4 slice. The times are simulated.
32 devices in a mesh: dp: 8 (over y, x, core), seq: 4 (over z).
Axes of the slice: x: 2, y: 2, z: 4, core: 2. Of those that a mesh axis runs over, the one named last changes fastest.
Arguments:
- cotangent: bfloat16 [8, 512, 2048], P('dp', 'seq'), may hold values from -1.75 to 1.75
- expert_ids: int32 [8, 512, 2], P('dp', 'seq'), may hold values from 0 to 15, as said below
- gate_probs: float32 [8, 512, 2], P('dp', 'seq'), may hold values from 0.05 to 1
- hidden_acts: bfloat16 [7168, 512], P('seq', 'dp'), may hold values from -6 to 6
- step_input: bfloat16 [8, 512, 256], P('dp', 'seq'), may hold values from -6 to 6
- step_proj: bfloat16 [256, 4096], replicated, may hold values from -0.375 to 0.375
- step_bias: float32 [4096], replicated, may hold values from -1 to 1
- decay_rate: float32 [16, 4096], replicated, may hold values from 0.0009765625 to 0.05
- input_coef: float32 [8, 16, 512], P('dp', None, 'seq'), may hold values from -4 to 4
- output_coef: float32 [8, 16, 512], P('dp', None, 'seq'), may hold values from -0.625 to 0.625
- grad_output: bfloat16 [8, 512, 4096], P('dp', 'seq'), may hold values from -6 to 6
- skip_weight: float32 [4096], replicated, may hold values from 0.5 to 1.5
Outputs:
- grad_down: float32 [2048, 7168], P('dp', 'seq')
- grad_x: bfloat16 [8, 512, 4096], P('dp', 'seq')
Inputs may be any that keep to these rules, and one draw needn't show every extreme that they name: `expert_ids`: each token names 2 different experts; among the tokens of one device (aligned blocks of 128 tokens of a sequence) every expert is named by exactly 16 of the pairs.
All inputs are finite; a program needn't handle non-finite values.
Results may differ from a plain program's by a relative error of at most 0.0029.
Values may be sent and summed in bfloat16 or wider, within the bound.
No kernel may reach another device: no remote copies, remote signals or barrier semaphores. Data moves between devices by JAX's collectives and lax.ppermute only.
A program may use at most 64 MiB of HBM per device.

v0:
```python
import jax
import jax.numpy as jnp
from jax import lax
from jax.sharding import PartitionSpec as P

BLOCK = 16


def from_behind(value, axis, by):
    peers = lax.axis_size(axis)
    pairs = [(i, i + by) for i in range(peers) if 0 <= i + by < peers]
    return lax.ppermute(value, axis, pairs)


def on_device(
    cotangent,
    expert_ids,
    gate_probs,
    hidden_acts,
    step_input,
    step_proj,
    step_bias,
    decay_rate,
    input_coef,
    output_coef,
    grad_output,
    skip_weight,
):
    tok_count = cotangent.shape[1]
    top_count = expert_ids.shape[2]
    pair_count = tok_count * top_count
    capacity = hidden_acts.shape[1] // lax.axis_size("seq")
    chosen = (expert_ids.reshape(pair_count) == 0).astype(jnp.int32)
    before = jnp.cumsum(chosen) - chosen
    destination = jnp.where(chosen == 1, before, capacity)
    token_of_slot = (
        jnp.zeros((capacity + 1,), jnp.int32)
        .at[destination]
        .set(jnp.arange(pair_count, dtype=jnp.int32) // top_count)[:capacity]
    )
    gate_of_slot = (
        jnp.zeros((capacity + 1,), jnp.float32)
        .at[destination]
        .set(gate_probs.reshape(pair_count))[:capacity]
    )
    picked = cotangent[0][token_of_slot]
    routed_local = (picked.astype(jnp.float32) * gate_of_slot[:, None]).astype(jnp.bfloat16)
    channels = grad_output.shape[2]
    state_size = decay_rate.shape[0]
    step_size = jax.nn.softplus(
        jnp.dot(step_input[0], step_proj, preferred_element_type=jnp.float32) + step_bias[None, :]
    )
    negative_rate = -decay_rate
    block_count = tok_count // BLOCK
    step_blocks = step_size.reshape(block_count, BLOCK, channels)
    grad_blocks = grad_output[0].reshape(block_count, BLOCK, channels)
    in_blocks = jnp.transpose(input_coef[0].reshape(state_size, block_count, BLOCK), (1, 0, 2))
    out_blocks = jnp.transpose(output_coef[0].reshape(state_size, block_count, BLOCK), (1, 0, 2))

    def block_step(state_carry, inputs):
        step_rows, grad_rows, in_cols, out_cols = inputs
        results = [None] * BLOCK
        for position in reversed(range(BLOCK)):
            out_grad = grad_rows[position].astype(jnp.float32)
            adjoint = out_cols[:, position][:, None] * out_grad[None, :] + state_carry
            results[position] = (
                step_rows[position] * jnp.sum(in_cols[:, position][:, None] * adjoint, axis=0)
                + skip_weight * out_grad
            )
            state_carry = jnp.exp(step_rows[position][None, :] * negative_rate) * adjoint
        return (state_carry, jnp.stack(results))

    outgoing, local_rows = lax.scan(
        block_step,
        jnp.zeros((state_size, channels), jnp.float32),
        (step_blocks, grad_blocks, in_blocks, out_blocks),
        reverse=True,
    )
    local_rows = local_rows.reshape(tok_count, channels)
    step_total = jnp.sum(step_size, axis=0)
    passing = jnp.exp(negative_rate * step_total[None, :])

    def relay_step(counter, pair_state):
        sending, received = pair_state
        received = from_behind(sending, "seq", -1)
        return (outgoing + passing * received, received)

    unused, incoming = lax.fori_loop(
        0, lax.axis_size("seq") - 1, relay_step, (outgoing, jnp.zeros_like(outgoing))
    )
    row_ids = lax.broadcasted_iota(jnp.int32, (tok_count, tok_count), 0)
    col_ids = lax.broadcasted_iota(jnp.int32, (tok_count, tok_count), 1)
    strict_upper = (col_ids > row_ids).astype(jnp.float32)
    later_sum = jnp.dot(
        strict_upper, step_size, precision=lax.Precision.HIGHEST, preferred_element_type=jnp.float32
    )
    carried = jnp.zeros((tok_count, channels), jnp.float32)
    for state_row in range(state_size):
        carried = (
            carried
            + input_coef[0][state_row][:, None]
            * jnp.exp(negative_rate[state_row][None, :] * later_sum)
            * incoming[state_row][None, :]
        )
    grad_x = (local_rows + step_size * carried).astype(jnp.bfloat16)[None]
    dense_term = lax.dot_general(
        lax.all_gather(routed_local, "seq", axis=0, tiled=True),
        hidden_acts,
        (((0,), (1,)), ((), ())),
        preferred_element_type=jnp.float32,
    )
    grad_down = lax.psum_scatter(dense_term, "dp", scatter_dimension=0, tiled=True)
    return (grad_down, grad_x)


def solution(mesh):
    return jax.shard_map(
        on_device,
        mesh=mesh,
        in_specs=(
            P("dp", "seq", None),
            P("dp", "seq", None),
            P("dp", "seq", None),
            P("seq", "dp"),
            P("dp", "seq", None),
            P(),
            P(),
            P(),
            P("dp", None, "seq"),
            P("dp", None, "seq"),
            P("dp", "seq", None),
            P(),
        ),
        out_specs=(P("dp", "seq"), P("dp", "seq", None)),
        check_vma=False,
    )
```

profile of v0, /device:TPU:0, one launch (start us, length us, event | category | flops | bytes accessed | tf_op | source)
XLA Modules:
  0.0 193.6 jit_solution(9008695162901316550)
XLA Ops:
  9.1 1.4 scatter_custom_fusion
  11.4 1.8 gather_fusion
  13.2 1.4 scatter_custom_fusion.1
  14.7 15.6 %all_gather.3 = bf16[64,2048]{1,0:T(8,128)(2,1)S(1)} all-gather(bf16[16,2048]{1,0:T(8,128)(2,1)S(1)} %multiply_convert_fusion), channel_id=1, replica_groups=mesh['dp'=8,'seq'=4] {'seq'}, dimensions={0}, use_global_device_ids=true | all-gather | bytes 327680 | tf_op jit(solution)/shard_map/all_gather | solution.py:107
  30.3 8.3 %fusion.29 = f32[2048,1792]{1,0:T(8,128)} fusion(bf16[64,2048]{1,0:T(8,128)(2,1)S(1)} %all_gather.3, bf16[1792,64]{0,1:T(8,128)(2,1)} %param.19), kind=kOutput, calls=%fused_computation.198 | convolution fusion | flops 469762048 | bytes 15171584 | tf_op jit(solution)/shard_map/dot_general | solution.py:106
  40.7 2.9 %fusion.28 = (f32[4096]{0:T(1024)S(1)}, f32[128,4096]{1,0:T(8,128)}) fusion(f32[4096]{0:T(1024)S(1)} %copy-done.7, bf16[256,4096]{1,0:T(8,128)(2,1)S(1)} %copy-done, bf16[1,128,256]{2,1,0:T(8,128)(2,1)S(1)} %copy-done.6), kind=kOutput, calls=%fused_computation.197 | convolution fusion | flops 272625664 | bytes 4292608 | tf_op jit(solution)/shard_map/dot_general | solution.py:51
  43.7 1.6 broadcast_in_dim.21
  45.2 99.4 %while.30 = (s32[]{:T(128)}, f32[16,4096]{1,0:T(8,128)S(1)}, f32[8,16,4096]{2,1,0:T(8,128)}, f32[8,16,4096]{2,1,0:T(8,128)}, f32[16,4096]{1,0:T(8,128)S(1)}, /*i...) while((s32[]{:T(128)}, f32[16,4096]{1,0:T(8,128)S(1)}, ...), condition=%wide.region_22.23_spmd.clone, body=%wide.region_5.22_spmd.clone.sunk | while | flops 9633811 | bytes 8400216 | solution.py:73
  46.0 2.2 %dynamic-slice_convert_fusion.17 = (f32[1,1,4096]{2,1,0:T(1,128)S(1)}, f32[1,1,4096]{2,1,0:T(1,128)S(1)}, f32[1,1,4096]{2,1,0:T(1,128)S(1)}, f32[1,1,4096]{2,1,0...) fusion(bf16[8,16,4096]{2,1,0:T(8,128)(2,1)} %get-tuple-element., ...), kind=kLoop, calls=%fused_computation.52.clone.1 | loop fusion | flops 65536 | bytes 393280 | tf_op jit(solution)/shard_map/while/body/eval_jaxpr/convert_element_type | solution.py:64
  48.2 2.0 %constant_dynamic-slice_fusion.23 = (f32[1,1,4096]{2,1,0:T(1,128)S(1)}, f32[1,1,4096]{2,1,0:T(1,128)S(1)}, f32[1,1,4096]{2,1,0:T(1,128)S(1)}, f32[1,1,4096]{2,1,...) fusion(f32[8,16,4096]{2,1,0:T(8,128)} %get-tuple-element.772, ...), kind=kLoop, calls=%fused_computation.110.clone.1 | loop fusion | bytes 393268 | tf_op jit(solution)/shard_map/while/body/eval_jaxpr/slice | solution.py:70
  58.7 2.2 %dynamic-slice_convert_fusion.17 = (f32[1,1,4096]{2,1,0:T(1,128)S(1)}, f32[1,1,4096]{2,1,0:T(1,128)S(1)}, f32[1,1,4096]{2,1,0:T(1,128)S(1)}, f32[1,1,4096]{2,1,0...) fusion(bf16[8,16,4096]{2,1,0:T(8,128)(2,1)} %get-tuple-element., ...), kind=kLoop, calls=%fused_computation.52.clone.1 | loop fusion | flops 65536 | bytes 393280 | tf_op jit(solution)/shard_map/while/body/eval_jaxpr/convert_element_type | solution.py:64
  60.9 1.9 constant_dynamic-slice_fusion.23
  71.1 2.0 %dynamic-slice_convert_fusion.17 = (f32[1,1,4096]{2,1,0:T(1,128)S(1)}, f32[1,1,4096]{2,1,0:T(1,128)S(1)}, f32[1,1,4096]{2,1,0:T(1,128)S(1)}, f32[1,1,4096]{2,1,0...) fusion(bf16[8,16,4096]{2,1,0:T(8,128)(2,1)} %get-tuple-element., ...), kind=kLoop, calls=%fused_computation.52.clone.1 | loop fusion | flops 65536 | bytes 393280 | tf_op jit(solution)/shard_map/while/body/eval_jaxpr/convert_element_type | solution.py:64
  73.1 1.8 constant_dynamic-slice_fusion.23
  83.4 2.2 %dynamic-slice_convert_fusion.17 = (f32[1,1,4096]{2,1,0:T(1,128)S(1)}, f32[1,1,4096]{2,1,0:T(1,128)S(1)}, f32[1,1,4096]{2,1,0:T(1,128)S(1)}, f32[1,1,4096]{2,1,0...) fusion(bf16[8,16,4096]{2,1,0:T(8,128)(2,1)} %get-tuple-element., ...), kind=kLoop, calls=%fused_computation.52.clone.1 | loop fusion | flops 65536 | bytes 393280 | tf_op jit(solution)/shard_map/while/body/eval_jaxpr/convert_element_type | solution.py:64
  85.6 2.0 %constant_dynamic-slice_fusion.23 = (f32[1,1,4096]{2,1,0:T(1,128)S(1)}, f32[1,1,4096]{2,1,0:T(1,128)S(1)}, f32[1,1,4096]{2,1,0:T(1,128)S(1)}, f32[1,1,4096]{2,1,...) fusion(f32[8,16,4096]{2,1,0:T(8,128)} %get-tuple-element.772, ...), kind=kLoop, calls=%fused_computation.110.clone.1 | loop fusion | bytes 393268 | tf_op jit(solution)/shard_map/while/body/eval_jaxpr/slice | solution.py:70
  96.0 1.9 dynamic-slice_convert_fusion.17
  97.9 2.0 %constant_dynamic-slice_fusion.23 = (f32[1,1,4096]{2,1,0:T(1,128)S(1)}, f32[1,1,4096]{2,1,0:T(1,128)S(1)}, f32[1,1,4096]{2,1,0:T(1,128)S(1)}, f32[1,1,4096]{2,1,...) fusion(f32[8,16,4096]{2,1,0:T(8,128)} %get-tuple-element.772, ...), kind=kLoop, calls=%fused_computation.110.clone.1 | loop fusion | bytes 393268 | tf_op jit(solution)/shard_map/while/body/eval_jaxpr/slice | solution.py:70
  108.2 1.9 dynamic-slice_convert_fusion.17
  110.1 2.0 %constant_dynamic-slice_fusion.23 = (f32[1,1,4096]{2,1,0:T(1,128)S(1)}, f32[1,1,4096]{2,1,0:T(1,128)S(1)}, f32[1,1,4096]{2,1,0:T(1,128)S(1)}, f32[1,1,4096]{2,1,...) fusion(f32[8,16,4096]{2,1,0:T(8,128)} %get-tuple-element.772, ...), kind=kLoop, calls=%fused_computation.110.clone.1 | loop fusion | bytes 393268 | tf_op jit(solution)/shard_map/while/body/eval_jaxpr/slice | solution.py:70
  120.5 2.1 %dynamic-slice_convert_fusion.17 = (f32[1,1,4096]{2,1,0:T(1,128)S(1)}, f32[1,1,4096]{2,1,0:T(1,128)S(1)}, f32[1,1,4096]{2,1,0:T(1,128)S(1)}, f32[1,1,4096]{2,1,0...) fusion(bf16[8,16,4096]{2,1,0:T(8,128)(2,1)} %get-tuple-element., ...), kind=kLoop, calls=%fused_computation.52.clone.1 | loop fusion | flops 65536 | bytes 393280 | tf_op jit(solution)/shard_map/while/body/eval_jaxpr/convert_element_type | solution.py:64
  122.7 2.2 %constant_dynamic-slice_fusion.23 = (f32[1,1,4096]{2,1,0:T(1,128)S(1)}, f32[1,1,4096]{2,1,0:T(1,128)S(1)}, f32[1,1,4096]{2,1,0:T(1,128)S(1)}, f32[1,1,4096]{2,1,...) fusion(f32[8,16,4096]{2,1,0:T(8,128)} %get-tuple-element.772, ...), kind=kLoop, calls=%fused_computation.110.clone.1 | loop fusion | bytes 393268 | tf_op jit(solution)/shard_map/while/body/eval_jaxpr/slice | solution.py:70
  133.2 1.9 dynamic-slice_convert_fusion.17
  135.1 1.9 constant_dynamic-slice_fusion.23
  144.9 27.2 %while.29 = (s32[]{:T(128)}, f32[16,4096]{1,0:T(8,128)S(1)}, f32[16,4096]{1,0:T(8,128)}, f32[16,4096]{1,0:T(8,128)S(1)}, f32[16,4096]{1,0:T(8,128)S(1)}, /*index=5*/s32[]{:T(128)}) while((s32[]{:T(128)}, f32[16,4096]{1,0:T(8,128)S(1)}, f32[16,4096]{1,0:T(8,128)}, f32[16,4096]{1,0:T(8,128)S(1)}, f32[16,4096]{1,0:T(8,128)S(1)}, ...), condition=%wide.region_25.26_spmd, body=%wide.region_24.25_spmd.sunk | while | flops 131074 | bytes 3145865 | solution.py:88
  144.9 1.3 collective-permute-start
  146.2 7.3 %collective-permute-done = f32[16,4096]{1,0:T(8,128)S(1)} collective-permute-done((f32[16,4096]{1,0:T(8,128)S(1)}, f32[16,4096]{1,0:T(8,128)S(1)}, u32[]{:S(2)}, u32[]{:S(2)}) %collective-permute-start) | collective-permute-done | bytes 262176 | tf_op jit(solution)/shard_map/while/body/eval_jaxpr/ppermute | solution.py:12
  154.3 1.3 collective-permute-start
  155.5 7.0 %collective-permute-done = f32[16,4096]{1,0:T(8,128)S(1)} collective-permute-done((f32[16,4096]{1,0:T(8,128)S(1)}, f32[16,4096]{1,0:T(8,128)S(1)}, u32[]{:S(2)}, u32[]{:S(2)}) %collective-permute-start) | collective-permute-done | bytes 262176 | tf_op jit(solution)/shard_map/while/body/eval_jaxpr/ppermute | solution.py:12
  164.5 7.0 %collective-permute-done = f32[16,4096]{1,0:T(8,128)S(1)} collective-permute-done((f32[16,4096]{1,0:T(8,128)S(1)}, f32[16,4096]{1,0:T(8,128)S(1)}, u32[]{:S(2)}, u32[]{:S(2)}) %collective-permute-start) | collective-permute-done | bytes 262176 | tf_op jit(solution)/shard_map/while/body/eval_jaxpr/ppermute | solution.py:12
  172.2 2.3 %fusion.27 = (f32[1,4096]{1,0:T(1,128)S(1)}, f32[1,4096]{1,0:T(1,128)S(1)}, f32[1,4096]{1,0:T(1,128)S(1)}, f32[1,4096]{1,0:T(1,128)S(1)}, f32[1,4096]{1,0:T(1,12...) fusion(f32[16,4096]{1,0:T(8,128)} %get-tuple-element.210), kind=kLoop, calls=%fused_computation.196 | loop fusion | bytes 524288 | tf_op jit(solution)/shard_map/slice | solution.py:103
  174.5 12.2 %fusion.21 = bf16[1,128,4096]{2,1,0:T(8,128)(2,1)} fusion(f32[128,4096]{1,0:T(8,128)} %bitcast.544, f32[4096]{0:T(1024)S(1)} %bitcast.563, f32[4096]{0:T(1024)S(1)} %bitcast.561, f32[128]{0:T(128)S(1)} %get-tuple-element.423, f32[4096]{0:T(1024)S(1)} %bitcast.564, f32[4096]{0:T(1024)S(1)} %bitcast.547, f32[128]{0:T(128)S(1)} %get-tuple-element.424, ...), kind=kOutput, calls=%fused_computation.163 | convolution fusion | flops 839925760 | bytes 5775360 | tf_op jit(solution)/shard_map/dot_general | solution.py:94
  (171 shorter events, 75.5 us)
Async XLA Ops:
  7.2 33.6 %copy-start = (bf16[256,4096]{1,0:T(8,128)(2,1)S(1)}, bf16[256,4096]{1,0:T(8,128)(2,1)}, u32[]{:S(2)}) copy-start(bf16[256,4096]{1,0:T(8,128)(2,1)} %param.21) | copy-start | bytes 6291460
  7.2 179.5 %reduce-scatter.2.cloned.1.call-start = ((), (), s32[]{:S(2)}) async-start(), calls=%async_computation.1 | async-start | bytes 16515072 | tf_op jit(solution)/shard_map/reduce_scatter | solution.py:112
  38.6 0.7 copy-start.5
  38.6 1.4 copy-start.4
  38.6 2.1 %copy-start.6 = (bf16[1,128,256]{2,1,0:T(8,128)(2,1)S(1)}, bf16[1,128,256]{2,1,0:T(8,128)(2,1)}, u32[]{:S(2)}) copy-start(bf16[1,128,256]{2,1,0:T(8,128)(2,1)} %param.20) | copy-start | bytes 196612
  38.6 2.1 %copy-start.7 = (f32[4096]{0:T(1024)S(1)}, f32[4096]{0:T(1024)}, u32[]{:S(2)}) copy-start(f32[4096]{0:T(1024)} %param.22) | copy-start | bytes 49156
  40.7 2.9 %copy-start.3 = (f32[16,4096]{1,0:T(8,128)S(1)}, f32[16,4096]{1,0:T(8,128)}, u32[]{:S(2)}) copy-start(f32[16,4096]{1,0:T(8,128)} %param.23) | copy-start | bytes 786436
  43.6 1.6 copy-start.1
  144.9 8.6 %collective-permute-start = (f32[16,4096]{1,0:T(8,128)S(1)}, f32[16,4096]{1,0:T(8,128)S(1)}, u32[]{:S(2)}, u32[]{:S(2)}) collective-permute-start(f32[16,4096]{1,0:T(8,128)S(1)} %get-tuple-element.803), channel_id=1, source_target_pairs={{1,0},{2,1},{3,2},{5,4},{6,5},{7,6},{9,8},{10,9},{11,10},{13,12},{... | collective-permute-start | bytes 786440 | tf_op jit(solution)/shard_map/while/body/eval_jaxpr/ppermute | solution.py:12
  153.6 0.7 copy-start.2
  154.3 8.3 %collective-permute-start = (f32[16,4096]{1,0:T(8,128)S(1)}, f32[16,4096]{1,0:T(8,128)S(1)}, u32[]{:S(2)}, u32[]{:S(2)}) collective-permute-start(f32[16,4096]{1,0:T(8,128)S(1)} %get-tuple-element.803), channel_id=1, source_target_pairs={{1,0},{2,1},{3,2},{5,4},{6,5},{7,6},{9,8},{10,9},{11,10},{13,12},{... | collective-permute-start | bytes 786440 | tf_op jit(solution)/shard_map/while/body/eval_jaxpr/ppermute | solution.py:12
  162.5 0.7 copy-start.2
  163.2 8.3 %collective-permute-start = (f32[16,4096]{1,0:T(8,128)S(1)}, f32[16,4096]{1,0:T(8,128)S(1)}, u32[]{:S(2)}, u32[]{:S(2)}) collective-permute-start(f32[16,4096]{1,0:T(8,128)S(1)} %get-tuple-element.803), channel_id=1, source_target_pairs={{1,0},{2,1},{3,2},{5,4},{6,5},{7,6},{9,8},{10,9},{11,10},{13,12},{... | collective-permute-start | bytes 786440 | tf_op jit(solution)/shard_map/while/body/eval_jaxpr/ppermute | solution.py:12
  171.5 0.7 copy-start.2
Sparse Core Ops, SparseCore 0:
  38.7 105.0 reduce-scatter.1
where the time goes:
time: 196 us; the launch traced here: 194 us
  other arithmetic  69.6 us (36%)
  local copies, waits for them, and re-layouts  45 us (23%)
  matrix products  23.3 us (12%)
  waiting for transfers between devices  21.3 us (11%)
  blocking collectives  15.6 us (8%)
  between operations  14.1 us (7%)
  starting transfers between devices  3.89 us (2%)
    add x40, other arithmetic, block_step(): step_rows[position]  33 us
    ppermute x3, waiting for transfers between devices, from_behind(): return lax.ppermute(value, axis, pairs)  21.2 us
    reduce_sum x32, other arithmetic, block_step(): jnp.sum(in_cols[:, position][:, None] * adjoint, axis=0)  17.9 us
    convert_element_type x8, other arithmetic, block_step(): out_grad = grad_rows[position].astype(jnp.float32)  16.3 us
    slice x8, local copies, waits for them, and re-layouts, block_step(): step_rows[position][None, :] * negative_rate  15.7 us
    all_gather x1, blocking collectives, on_device(): lax.all_gather(routed_local, 'seq', axis=0, tiled=True)  15.6 us
    dot_general x1, matrix products, on_device(): jnp.dot(strict_upper, step_size, precision=lax.Precision.HIGHEST, preferr...  12.2 us
    dot_general x1, matrix products, on_device(): lax.dot_general(lax.all_gather(routed_local, 'seq', axis=0, tiled=True),...  8.27 us
  transfers between devices with their start and end apart: 4, of which 3 were waited for; matrix products, arithmetic and copies ran while one was open for 62% of the time, Pallas kernels for 0%

commit v1 on v0

v1 whole, which is shorter than its diff:
```python
import functools
import math

import jax
import jax.numpy as jnp
from jax import lax
from jax.experimental import pallas as pl
from jax.experimental.pallas import tpu as pltpu
from jax.sharding import PartitionSpec as P

LANES=128
BLOCK=16
CT=512
VMEM_BYTES=40*2**20
LOG2E=math.log2(math.e)
f32=jnp.float32; bf16=jnp.bfloat16
def softplus(v):
    return jnp.maximum(v,0.0)+jnp.log1p(jnp.exp(-jnp.abs(v)))

def spread(src_ref, dst_ref):
    v=src_ref[...]
    for t in range(v.shape[1]):
        dst_ref[t]=jnp.broadcast_to(v[:,t:t+1],(v.shape[0],LANES))

def state_kernel(x_ref,proj_ref,bias_ref,decay_ref,outc_ref,g_ref,step_ref,msg_ref,outb,g32,stot):
    ct=pl.program_id(0)
    toks=x_ref.shape[0]; n=decay_ref.shape[0]; chunk=decay_ref.shape[1]
    chans=chunk*pl.num_programs(0)
    @pl.when(ct==0)
    def _():
        spread(outc_ref,outb)
    step=softplus(jnp.dot(x_ref[...],proj_ref[...],preferred_element_type=f32)+bias_ref[...])
    blocks=toks//BLOCK
    step_ref[...]=step.reshape(blocks,BLOCK,chunk)
    g32[...]=g_ref[...].astype(f32).reshape(blocks,BLOCK,chunk)
    total=jnp.sum(step,axis=0,keepdims=True)
    width=stot.shape[1]
    for k in range(chunk//width):
        stot[pl.ds(ct*(chunk//width)+k,1),:]=total[:,k*width:(k+1)*width]
    tiles=chunk//LANES
    rate=[decay_ref[:,q*LANES:(q+1)*LANES]*(-LOG2E) for q in range(tiles)]
    def body(b,states):
        b=blocks-1-b
        states=list(states)
        for k in reversed(range(BLOCK)):
            ob=outb[b*BLOCK+k]
            for q in range(tiles):
                sl=pl.ds(q*LANES,LANES)
                s=jnp.broadcast_to(step_ref[b,k:k+1,sl],(n,LANES))
                g=jnp.broadcast_to(g32[b,k:k+1,sl],(n,LANES))
                adj=states[q]+ob*g
                states[q]=jnp.exp2(s*rate[q])*adj
        return tuple(states)
    states=lax.fori_loop(0,toks//BLOCK,body,tuple(jnp.zeros((n,LANES),f32) for _ in range(tiles)))
    for q in range(tiles):
        msg_ref[:,pl.ds(pl.multiple_of(ct*chunk+q*LANES,LANES),LANES)]=states[q].astype(bf16)
    @pl.when(ct==pl.num_programs(0)-1)
    def _():
        s=stot[...]
        hi=s.astype(bf16)
        msg_ref[:,chans:chans+width]=hi
        msg_ref[:,chans+width:chans+2*width]=(s-hi.astype(f32)).astype(bf16)

def state_pass(x,proj,bias,decay,outc,g):
    toks,chans=g.shape; n=decay.shape[0]; width=chans//n
    return pl.pallas_call(state_kernel,grid=(chans//CT,),
        in_specs=[pl.BlockSpec(x.shape,lambda c:(0,0)),pl.BlockSpec((proj.shape[0],CT),lambda c:(0,c)),pl.BlockSpec((1,CT),lambda c:(0,c)),
                  pl.BlockSpec((n,CT),lambda c:(0,c)),pl.BlockSpec(outc.shape,lambda c:(0,0)),pl.BlockSpec((toks,CT),lambda c:(0,c))],
        out_specs=[pl.BlockSpec((toks//BLOCK,BLOCK,CT),lambda c:(0,0,c)),pl.BlockSpec((n,chans+2*width),lambda c:(0,0))],
        out_shape=[jax.ShapeDtypeStruct((toks//BLOCK,BLOCK,chans),f32),jax.ShapeDtypeStruct((n,chans+2*width),bf16)],
        scratch_shapes=[pltpu.VMEM((toks,n,LANES),f32),pltpu.VMEM((toks//BLOCK,BLOCK,CT),f32),pltpu.VMEM((n,width),f32)],
        compiler_params=pltpu.CompilerParams(vmem_limit_bytes=VMEM_BYTES),
        name="state_pass")(x,proj,bias.reshape(1,-1),decay,outc,g)


def full_kernel(step_ref,g_ref,decay_ref,outc_ref,inc_ref,skip_ref,*rest):
    *msgs,out_ref,outb,g32,picks,adjs,stots=rest
    ct=pl.program_id(0)
    toks,chunk=g_ref.shape; n=decay_ref.shape[0]
    chans=chunk*pl.num_programs(0); width=chans//n
    span=BLOCK*n
    blocks=toks//BLOCK
    @pl.when(ct==0)
    def _():
        spread(outc_ref,outb)
        sel=(lax.broadcasted_iota(jnp.int32,(n,span),1)%n==lax.broadcasted_iota(jnp.int32,(n,span),0)).astype(bf16)
        own=(lax.broadcasted_iota(jnp.int32,(toks,span),1)//n==lax.broadcasted_iota(jnp.int32,(toks,span),0)%BLOCK)
        v=inc_ref[...]
        hi=v.astype(bf16); lo=(v-hi.astype(f32)).astype(bf16)
        for part,vals in enumerate((hi,lo)):
            wide=lax.dot_general(vals,sel,(((0,),(0,)),((),())),preferred_element_type=f32)
            wide=jnp.where(own,wide,0.0).astype(bf16)
            for b in range(blocks):
                picks[b,part*BLOCK:(part+1)*BLOCK,:]=wide[b*BLOCK:(b+1)*BLOCK]
        for k,m in enumerate(msgs):
            total=m[:,chans:chans+width].astype(f32)+m[:,chans+width:chans+2*width].astype(f32)
            for row in range(n):
                stots[k,row]=total[row:row+1]
    g32[...]=g_ref[...].astype(f32).reshape(blocks,BLOCK,chunk)
    tiles=chunk//LANES
    rate=[decay_ref[:,q*LANES:(q+1)*LANES]*(-LOG2E) for q in range(tiles)]
    states=[]
    for q in range(tiles):
        lanes=pl.ds(pl.multiple_of(ct*chunk+q*LANES,LANES),LANES)
        acc=msgs[-1][:,lanes].astype(f32)
        for k in reversed(range(len(msgs)-1)):
            tot=stots[k,ct*(chunk//width)+q*LANES//width,:,(q*LANES)%width:(q*LANES)%width+LANES]
            acc=msgs[k][:,lanes].astype(f32)+jnp.exp2(jnp.broadcast_to(tot,(n,LANES))*rate[q])*acc
        states.append(acc)
    def body(i,states):
        b=blocks-1-i
        base=b*BLOCK
        states=list(states)
        for k in reversed(range(BLOCK)):
            ob=outb[base+k]
            for q in range(tiles):
                sl=pl.ds(q*LANES,LANES)
                s=jnp.broadcast_to(step_ref[b,k:k+1,sl],(n,LANES))
                g=jnp.broadcast_to(g32[b,k:k+1,sl],(n,LANES))
                adj=states[q]+ob*g
                adjs[k*n:(k+1)*n,q*LANES:(q+1)*LANES]=adj.astype(bf16)
                states[q]=jnp.exp2(s*rate[q])*adj
        both=jnp.dot(picks[b],adjs[...],preferred_element_type=f32)
        y=both[:BLOCK]+both[BLOCK:]
        rows=pl.ds(pl.multiple_of(base,BLOCK),BLOCK)
        out_ref[rows,:]=(step_ref[b]*y+skip_ref[...]*g32[b]).astype(bf16)
        return tuple(states)
    lax.fori_loop(0,blocks,body,tuple(states))

def full_pass(step,g,decay,outc,inc,skip,msgs):
    toks,chans=g.shape; n=decay.shape[0]; width=chans//n
    return pl.pallas_call(full_kernel,grid=(chans//CT,),
        in_specs=[pl.BlockSpec((toks//BLOCK,BLOCK,CT),lambda c:(0,0,c)),pl.BlockSpec((toks,CT),lambda c:(0,c)),pl.BlockSpec((n,CT),lambda c:(0,c)),
                  pl.BlockSpec(outc.shape,lambda c:(0,0)),pl.BlockSpec(inc.shape,lambda c:(0,0)),pl.BlockSpec((1,CT),lambda c:(0,c))]
                 +[pl.BlockSpec(m.shape,lambda c:(0,0)) for m in msgs],
        out_specs=pl.BlockSpec((toks,CT),lambda c:(0,c)),
        out_shape=jax.ShapeDtypeStruct((toks,chans),bf16),
        scratch_shapes=[pltpu.VMEM((toks,n,LANES),f32),pltpu.VMEM((toks//BLOCK,BLOCK,CT),f32),pltpu.VMEM((toks//BLOCK,2*BLOCK,BLOCK*n),bf16),
                        pltpu.VMEM((BLOCK*n,CT),bf16),pltpu.VMEM((len(msgs),n,1,width),f32)],
        compiler_params=pltpu.CompilerParams(vmem_limit_bytes=VMEM_BYTES),
        name="full_pass")(step,g,decay,outc,inc,skip.reshape(1,-1),*msgs)


def slot_rows(ids_ref, gate_ref, cot_ref, capacity):
    toks = ids_ref.shape[0]
    named = (ids_ref[...] == 0).astype(f32)
    chosen = jnp.sum(named, axis=1, keepdims=True)
    gate = jnp.sum(named * gate_ref[...], axis=1, keepdims=True)
    earlier = (
        lax.broadcasted_iota(jnp.int32, (toks, toks), 1) < lax.broadcasted_iota(jnp.int32, (toks, toks), 0)
    ).astype(bf16)
    before = jnp.dot(
        earlier, jnp.broadcast_to(chosen, (toks, LANES)).astype(bf16), preferred_element_type=f32
    )[:, :capacity]
    slots = lax.broadcasted_iota(jnp.int32, (toks, capacity), 1).astype(f32)
    pick = jnp.where((before == slots) & (chosen > 0.5), 1.0, 0.0).astype(bf16)
    weighted = (gate * cot_ref[...].astype(f32)).astype(bf16)
    return lax.dot_general(
        pick, weighted, (((0,), (0,)), ((), ())), preferred_element_type=f32
    ).astype(bf16)


def pack_kernel(masks, part, place_ref, ids_ref, gate_ref, cot_ref, hidden_ref, *rest):
    *outs, routed = rest
    hid, rows = hidden_ref.shape
    capacity = routed.shape[0]
    routed[...] = slot_rows(ids_ref, gate_ref, cot_ref, capacity)
    eye = (
        lax.broadcasted_iota(jnp.int32, (rows, rows), 0) == lax.broadcasted_iota(jnp.int32, (rows, rows), 1)
    ).astype(bf16)
    turned = lax.dot_general(
        eye, hidden_ref[...], (((1,), (1,)), ((), ())), preferred_element_type=f32
    ).astype(bf16)
    pair = place_ref[0] // 2
    for mask, out in zip(masks, outs):
        out[:, :hid] = turned
        target = (pair ^ (mask // 2)) * 2
        for core in range(2):
            lanes = pl.ds(pl.multiple_of((target + core) * part, LANES), part)
            out[core * capacity : (core + 1) * capacity, hid:] = routed[:, lanes]
        if 2 * capacity < rows:
            out[2 * capacity :, hid:] = jnp.zeros((rows - 2 * capacity, part), bf16)


def pack(place, ids, gate, cot, hidden, masks, part, capacity):
    hid, rows = hidden.shape
    whole = pl.BlockSpec(memory_space=pltpu.VMEM)
    return pl.pallas_call(
        functools.partial(pack_kernel, masks, part),
        in_specs=[pl.BlockSpec(memory_space=pltpu.SMEM)] + [whole] * 4,
        out_specs=[whole] * len(masks),
        out_shape=[jax.ShapeDtypeStruct((rows, hid + part), bf16)] * len(masks),
        scratch_shapes=[pltpu.VMEM((capacity, cot.shape[1]), bf16)],
        compiler_params=pltpu.CompilerParams(vmem_limit_bytes=VMEM_BYTES),
        name="pack",
    )(place, ids, gate, cot, hidden)


def mine_kernel(capacity, place_ref, *rest):
    *packs, out_ref = rest
    start = pl.multiple_of((place_ref[0] % 2) * capacity, capacity)
    for slot, block in enumerate(packs):
        out_ref[slot * capacity : (slot + 1) * capacity] = block[pl.ds(start, capacity), :]


def mine(place, packs, part, capacity):
    column = packs[0].shape[1] // part - 1
    return pl.pallas_call(
        functools.partial(mine_kernel, capacity),
        grid=(1,),
        in_specs=[pl.BlockSpec(memory_space=pltpu.SMEM)]
        + [pl.BlockSpec((2 * capacity, part), lambda c: (0, column))] * len(packs),
        out_specs=pl.BlockSpec((len(packs) * capacity, part), lambda c: (0, 0)),
        out_shape=jax.ShapeDtypeStruct((len(packs) * capacity, part), bf16),
        name="own_columns",
    )(place, *packs)


def weight_kernel(capacity, peers, place_ref, *rest):
    packs = rest[:peers]
    *parts, out_ref, rows_ref = rest[peers:]
    count = len(parts)
    rows = count * capacity

    @pl.when(pl.program_id(0) == 0)
    def _():
        for ahead, piece in enumerate(parts):
            block = lax.rem(place_ref[1] + ahead, count)
            for slot in range(peers):
                start = pl.multiple_of(slot * rows + block * capacity, capacity)
                rows_ref[pl.ds(start, capacity), :] = piece[slot * capacity : (slot + 1) * capacity]

    hidden = jnp.concatenate([block[...] for block in packs], axis=0)
    out_ref[...] = lax.dot_general(
        rows_ref[...], hidden, (((0,), (0,)), ((), ())), preferred_element_type=f32
    )


def weight_grad(place, packs, parts, part, capacity):
    peers = len(packs)
    rows = packs[0].shape[0]
    hid = packs[0].shape[1] - part
    step = hid // 2 if hid % (2 * LANES) == 0 else hid
    return pl.pallas_call(
        functools.partial(weight_kernel, capacity, peers),
        grid=(hid // step,),
        in_specs=[pl.BlockSpec(memory_space=pltpu.SMEM)]
        + [pl.BlockSpec((rows, step), lambda c: (0, c))] * peers
        + [pl.BlockSpec(p.shape, lambda c: (0, 0)) for p in parts],
        out_specs=pl.BlockSpec((part, step), lambda c: (0, c)),
        out_shape=jax.ShapeDtypeStruct((part, hid), f32),
        scratch_shapes=[pltpu.VMEM((peers * rows, part), bf16)],
        compiler_params=pltpu.CompilerParams(vmem_limit_bytes=VMEM_BYTES),
        name="weight_grad",
    )(place, *packs, *parts)


def routed_kernel(ids_ref, gate_ref, cot_ref, out_ref):
    out_ref[...] = slot_rows(ids_ref, gate_ref, cot_ref, out_ref.shape[0])


def routed_rows(ids, gate, cot, capacity):
    return pl.pallas_call(
        routed_kernel,
        out_shape=jax.ShapeDtypeStruct((capacity, cot.shape[1]), bf16),
        name="routed_rows",
    )(ids, gate, cot)


def from_ahead(value, axis, by):
    peers = lax.axis_size(axis)
    return lax.ppermute(value, axis, [(i, i - by) for i in range(by, peers)])


def around(value, axis, by):
    peers = lax.axis_size(axis)
    return lax.ppermute(value, axis, [(i, (i - by) % peers) for i in range(peers)])


def across(value, axis, mask):
    return lax.ppermute(value, axis, [(i, i ^ mask) for i in range(lax.axis_size(axis))])


def on_device(
    cotangent,
    expert_ids,
    gate_probs,
    hidden_acts,
    step_input,
    step_proj,
    step_bias,
    decay_rate,
    input_coef,
    output_coef,
    grad_output,
    skip_weight,
):
    peers = lax.axis_size("dp")
    spans = lax.axis_size("seq")
    hid, rows = hidden_acts.shape
    features = cotangent.shape[2]
    capacity = rows // spans
    part = features // peers
    place = jnp.stack([lax.axis_index("dp"), lax.axis_index("seq")]).astype(jnp.int32)
    gathers = (
        peers * rows * 2 < features * 4
        and peers & (peers - 1) == 0
        and peers > 1
        and part % LANES == 0
        and hid % part == 0
        and 2 * capacity <= rows
    )
    if gathers:
        masks = list(range(0, peers, 2))
        sent = pack(place, expert_ids[0], gate_probs[0], cotangent[0], hidden_acts, masks, part, capacity)
        near = [sent[0]] + [across(v, "dp", m) for v, m in zip(sent[1:], masks[1:])]

    step, message = state_pass(
        step_input[0], step_proj, step_bias, decay_rate, output_coef[0], grad_output[0]
    )
    messages = [from_ahead(message, "seq", by) for by in range(1, spans)]

    if gathers:
        packs = near + [across(v, "dp", 1) for v in near]
        own = mine(place, packs, part, capacity)
        parts = [own] + [around(own, "seq", by) for by in range(1, spans)]
        grad_down = weight_grad(place, packs, parts, part, capacity)
    else:
        routed = routed_rows(expert_ids[0], gate_probs[0], cotangent[0], capacity)
        dense = lax.dot_general(
            lax.all_gather(routed, "seq", axis=0, tiled=True),
            hidden_acts,
            (((0,), (1,)), ((), ())),
            preferred_element_type=f32,
        )
        grad_down = lax.psum_scatter(dense, "dp", scatter_dimension=0, tiled=True)

    grad_x = full_pass(
        step, grad_output[0], decay_rate, output_coef[0], input_coef[0], skip_weight, messages
    )[None]
    return (grad_down, grad_x)


def solution(mesh):
    return jax.shard_map(
        on_device,
        mesh=mesh,
        in_specs=(
            P("dp", "seq", None),
            P("dp", "seq", None),
            P("dp", "seq", None),
            P("seq", "dp"),
            P("dp", "seq", None),
            P(),
            P(),
            P(),
            P("dp", None, "seq"),
            P("dp", None, "seq"),
            P("dp", "seq", None),
            P(),
        ),
        out_specs=(P("dp", "seq"), P("dp", "seq", None)),
        check_vma=False,
    )
```

time: 196 us -> 86.2 us (0.44)
  the two profiles are of different devices: /device:TPU:0 before, /device:TPU:13 now
where the time goes in v1:
time: 86.2 us; the launch traced here: 85.4 us
  Pallas kernels  37.4 us (43%)
  starting transfers between devices  23 us (27%)
  local copies, waits for them, and re-layouts  12.5 us (15%)
  waiting for transfers between devices  11.4 us (13%)
  between operations  0.92 us (1%)
    pallas_call x1, Pallas kernels, full_pass(): pl.pallas_call(full_kernel, grid=(chans // CT,), in_specs=[pl.BlockSpec((...  21.4 us
    ppermute x7, starting transfers between devices, across(): lax.ppermute(value, axis, [(i, i ^ mask) for i in range(lax.axis_size(axi...  12.7 us
    unnamed x59, local copies, waits for them, and re-layouts  12.5 us
    pallas_call x1, Pallas kernels, state_pass(): pl.pallas_call(state_kernel, grid=(chans // CT,), in_specs=[pl.BlockSpec(...  10.2 us
    ppermute x3, waiting for transfers between devices, from_ahead(): return lax.ppermute(value, axis, [(i, i - by) for i in range(by, peers)])  8.4 us
    ppermute x3, starting transfers between devices, around(): lax.ppermute(value, axis, [(i, (i - by) % peers) for i in range(peers)])  5.69 us
    ppermute x3, starting transfers between devices, from_ahead(): return lax.ppermute(value, axis, [(i, i - by) for i in range(by, peers)])  4.65 us
    pallas_call x1, Pallas kernels, weight_grad(): pl.pallas_call(functools.partial(weight_kernel, capacity, peers), grid=(h...  3.22 us
  transfers between devices with their start and end apart: 13, of which 2 were waited for; matrix products, arithmetic and copies ran while one was open for 0% of the time, Pallas kernels for 39%

profile of v1, /device:TPU:13, one launch (start us, length us, event | category | flops | bytes accessed | tf_op | source)
XLA Modules:
  0.0 85.4 jit_solution(11100606968414647266)
XLA Ops:
  0.6 0.9 %copy.14 = s32[1,128,2]{2,1,0:T(8,128)S(1)} copy(s32[1,128,2]{1,2,0:T(2,128)} %param.13) | data formatting | bytes 2048 | tf_op args[1]
  1.5 0.8 copy.15
  2.3 1.2 %copy.16.hidden_ref = bf16[1792,64]{1,0:T(8,128)(2,1)S(1)} copy(bf16[1792,64]{0,1:T(8,128)(2,1)} %param.15) | data formatting | bytes 458752 | tf_op args[3]
  3.6 1.0 %copy-done.18 = bf16[1,128,2048]{2,1,0:T(8,128)(2,1)S(1)} copy-done((bf16[1,128,2048]{2,1,0:T(8,128)(2,1)S(1)}, bf16[1,128,2048]{2,1,0:T(8,128)(2,1)}, u32[]{:S(2)}) %copy-start.18) | copy-done | bytes 524312
  4.6 1.2 %pack.1 = (bf16[64,2048]{1,0:T(8,128)(2,1)S(1)}, bf16[64,2048]{1,0:T(8,128)(2,1)S(1)}, bf16[64,2048]{1,0:T(8,128)(2,1)S(1)}, bf16[64,2048]{1,0:T(8,128)(2,1)S(1)}) custom-call(s32[2]{0:T(128)S(1)} %pad_add_fusion.place_ref, s32[128,2]{1,0:T(8,128)S(1)} %bitcast.15, f32[128,2]{1,0:T(8,128)S(1)} %bitcast.16, bf16[128,2048]{1,0:T(8,128)(2,1)S(1)} %bitcast.14, ...), custom_call_target="tpu_custom_call" | custom-call | tf_op jit(solution)/shard_map/pack/pallas_call | solution.py:188
  5.8 1.3 %collective-permute-start = (bf16[64,2048]{1,0:T(8,128)(2,1)S(1)}, bf16[64,2048]{1,0:T(8,128)(2,1)S(1)}, u32[]{:S(2)}, u32[]{:S(2)}) collective-permute-start(bf16[64,2048]{1,0:T(8,128)(2,1)S(1)} %get-tuple-element.9), channel_id=1, source_target_pairs={{0,8},{4,12},{8,0},{12,4},{16,24},{20,28},{24,16},{28,20},{1,9},{5... | collective-permute-start | bytes 786440 | tf_op jit(solution)/shard_map/ppermute | solution.py:281
  7.3 1.2 %collective-permute-start.2 = (bf16[64,2048]{1,0:T(8,128)(2,1)S(1)}, bf16[64,2048]{1,0:T(8,128)(2,1)S(1)}, u32[]{:S(2)}, u32[]{:S(2)}) collective-permute-start(bf16[64,2048]{1,0:T(8,128)(2,1)S(1)} %get-tuple-element.11), channel_id=1, source_target_pairs={{0,24},{4,28},{8,16},{12,20},{16,8},{20,12},{24,0},{28,4},{1,25},{... | collective-permute-start | bytes 786440 | tf_op jit(solution)/shard_map/ppermute | solution.py:281
  8.5 1.5 %collective-permute-start.3 = (bf16[64,2048]{1,0:T(8,128)(2,1)S(1)}, bf16[64,2048]{1,0:T(8,128)(2,1)S(1)}, u32[]{:S(2)}, u32[]{:S(2)}) collective-permute-start(bf16[64,2048]{1,0:T(8,128)(2,1)S(1)} %get-tuple-element.8.rest_0_), channel_id=1, source_target_pairs={{0,4},{4,0},{8,12},{12,8},{16,20},{20,16},{24,28},{28,24},{1,5},{5... | collective-permute-start | bytes 786440 | tf_op jit(solution)/shard_map/ppermute | solution.py:281
  10.0 3.0 %collective-permute-done.rest_1_ = bf16[64,2048]{1,0:T(8,128)(2,1)S(1)} collective-permute-done((bf16[64,2048]{1,0:T(8,128)(2,1)S(1)}, bf16[64,2048]{1,0:T(8,128)(2,1)S(1)}, u32[]{:S(2)}, u32[]{:S(2)}) %collective-permute-start) | collective-permute-done | bytes 262176 | tf_op jit(solution)/shard_map/ppermute | solution.py:281
  13.1 2.7 %collective-permute-start.4 = (bf16[64,2048]{1,0:T(8,128)(2,1)S(1)}, bf16[64,2048]{1,0:T(8,128)(2,1)S(1)}, u32[]{:S(2)}, u32[]{:S(2)}) collective-permute-start(bf16[64,2048]{1,0:T(8,128)(2,1)S(1)} %collective-permute-done.rest_1_), channel_id=1, source_target_pairs={{0,4},{4,0},{8,12},{12,8},{16,20},{20,16},{24,28},{28,24},{1,5},{5... | collective-permute-start | bytes 786440 | tf_op jit(solution)/shard_map/ppermute | solution.py:281
  15.8 5.7 %collective-permute-start.5 = (bf16[64,2048]{1,0:T(8,128)(2,1)S(1)}, bf16[64,2048]{1,0:T(8,128)(2,1)S(1)}, u32[]{:S(2)}, u32[]{:S(2)}) collective-permute-start(bf16[64,2048]{1,0:T(8,128)(2,1)S(1)} %collective-permute-done.1.rest_2_), channel_id=1, source_target_pairs={{0,4},{4,0},{8,12},{12,8},{16,20},{20,16},{24,28},{28,24},{1,5},{5... | collective-permute-start | bytes 786440 | tf_op jit(solution)/shard_map/ppermute | solution.py:281
  21.5 1.6 %copy-done.1 = bf16[256,4096]{1,0:T(8,128)(2,1)S(1)} copy-done((bf16[256,4096]{1,0:T(8,128)(2,1)S(1)}, bf16[256,4096]{1,0:T(8,128)(2,1)}, u32[]{:S(2)}) %copy-start.1) | copy-done | bytes 2097176
  23.1 0.9 %copy-done.16 = f32[16,4096]{1,0:T(8,128)S(1)} copy-done((f32[16,4096]{1,0:T(8,128)S(1)}, f32[16,4096]{1,0:T(8,128)}, u32[]{:S(2)}) %copy-start.16) | copy-done | bytes 262168
  24.1 0.8 copy-done.20
  24.9 0.7 copy-done.21
  25.6 0.7 copy-done.23
  26.3 10.2 %state_pass.1 = (f32[8,16,4096]{2,1,0:T(8,128)S(1)}, bf16[16,4608]{1,0:T(8,128)(2,1)}) custom-call(bf16[128,256]{1,0:T(8,128)(2,1)S(1)} %bitcast.17, bf16[256,4096]{1,0:T(8,128)(2,1)S(1)} %copy-done.1, f32[1,4096]{1,0:T(1,128)S(1)} %bitcast.20, f32[16,4096]{1,0:T(8,128)S(1)} %copy-done.16, f32[16,128]{1,0:T(8,128)S(1)} %bitcast.18, ...), custom_call_target="tpu_custom_call" | custom-call | tf_op jit(solution)/shard_map/state_pass/pallas_call | solution.py:66
  36.5 0.7 collective-permute-start.12
  37.2 1.3 %collective-permute-start.11 = (bf16[16,4608]{1,0:T(8,128)(2,1)}, bf16[16,4608]{1,0:T(8,128)(2,1)}, u32[]{:S(2)}, u32[]{:S(2)}) collective-permute-start(bf16[16,4608]{1,0:T(8,128)(2,1)} %get-tuple-element.13), channel_id=1, source_target_pairs={{2,0},{3,1},{6,4},{7,5},{10,8},{11,9},{14,12},{15,13},{18,16},{19,... | collective-permute-start | bytes 442376 | tf_op jit(solution)/shard_map/ppermute | solution.py:272
  38.5 2.7 %collective-permute-start.10 = (bf16[16,4608]{1,0:T(8,128)(2,1)}, bf16[16,4608]{1,0:T(8,128)(2,1)}, u32[]{:S(2)}, u32[]{:S(2)}) collective-permute-start(bf16[16,4608]{1,0:T(8,128)(2,1)} %get-tuple-element.13), channel_id=1, source_target_pairs={{1,0},{2,1},{3,2},{5,4},{6,5},{7,6},{9,8},{10,9},{11,10},{13,12},{... | collective-permute-start | bytes 442376 | tf_op jit(solution)/shard_map/ppermute | solution.py:272
  41.3 0.7 copy-done.14
  42.0 1.5 %own_columns.1.rest_8_ = bf16[128,256]{1,0:T(8,128)(2,1)} custom-call(s32[2]{0:T(128)} %copy-done.26, bf16[64,2048]{1,0:T(8,128)(2,1)} %copy-done.2, bf16[64,2048]{1,0:T(8,128)(2,1)} %copy-done.4, bf16[64,2048]{1,0:T(8,128)(2,1)} %copy-done.6, bf16[64,2048]{1,0:T(8,128)(2,1)} %copy-done.8, bf16[64,2048]{1,0:T(8,128)(2,1)} %copy-done.10, ...), custom_call_target="tpu_custom_call" | custom-call | tf_op jit(solution)/shard_map/own_columns/pallas_call | solution.py:208
  43.5 2.4 %collective-permute-start.9 = (bf16[128,256]{1,0:T(8,128)(2,1)}, bf16[128,256]{1,0:T(8,128)(2,1)S(1)}, u32[]{:S(2)}, u32[]{:S(2)}) collective-permute-start(bf16[128,256]{1,0:T(8,128)(2,1)} %own_columns.1.rest_8_), channel_id=1, source_target_pairs={{0,1},{1,2},{2,3},{3,0},{4,5},{5,6},{6,7},{7,4},{8,9},{9,10},{10,1... | collective-permute-start | bytes 196616 | tf_op jit(solution)/shard_map/ppermute | solution.py:277
  45.9 1.8 %collective-permute-start.8 = (bf16[128,256]{1,0:T(8,128)(2,1)}, bf16[128,256]{1,0:T(8,128)(2,1)S(1)}, u32[]{:S(2)}, u32[]{:S(2)}) collective-permute-start(bf16[128,256]{1,0:T(8,128)(2,1)} %own_columns.1.rest_8_), channel_id=1, source_target_pairs={{0,2},{1,3},{2,0},{3,1},{4,6},{5,7},{6,4},{7,5},{8,10},{9,11},{10,... | collective-permute-start | bytes 196616 | tf_op jit(solution)/shard_map/ppermute | solution.py:277
  47.7 1.5 %collective-permute-start.7 = (bf16[128,256]{1,0:T(8,128)(2,1)}, bf16[128,256]{1,0:T(8,128)(2,1)S(1)}, u32[]{:S(2)}, u32[]{:S(2)}) collective-permute-start(bf16[128,256]{1,0:T(8,128)(2,1)} %own_columns.1.rest_8_), channel_id=1, source_target_pairs={{0,3},{1,0},{2,1},{3,2},{4,7},{5,4},{6,5},{7,6},{8,11},{9,8},{10,9... | collective-permute-start | bytes 196616 | tf_op jit(solution)/shard_map/ppermute | solution.py:277
  49.2 8.4 %collective-permute-done.10.rest_0_ = bf16[16,4608]{1,0:T(8,128)(2,1)} collective-permute-done((bf16[16,4608]{1,0:T(8,128)(2,1)}, bf16[16,4608]{1,0:T(8,128)(2,1)}, u32[]{:S(2)}, u32[]{:S(2)}) %collective-permute-start.10) | collective-permute-done | bytes 147488 | tf_op jit(solution)/shard_map/ppermute | solution.py:272
  57.6 0.9 %copy-done.17 = f32[16,4096]{1,0:T(8,128)S(1)} copy-done((f32[16,4096]{1,0:T(8,128)S(1)}, f32[16,4096]{1,0:T(8,128)}, u32[]{:S(2)}) %copy-start.17) | copy-done | bytes 262168
  58.5 0.7 copy-done.22
  59.2 0.7 copy-done.24
  59.9 0.7 copy-done.25
  60.7 21.4 %full_pass.1 = bf16[128,4096]{1,0:T(8,128)(2,1)} custom-call(f32[8,16,4096]{2,1,0:T(8,128)S(1)} %get-tuple-element.12.step_ref, bf16[128,4096]{1,0:T(8,128)(2,1)S(1)} %bitcast.13, f32[16,4096]{1,0:T(8,128)S(1)} %copy-done.17, f32[16,128]{1,0:T(8,128)S(1)} %bitcast.19, f32[16,128]{1,0:T(8,128)S(1)} %bitcast.22, f32[1,4096]{1,0:T(1,128)S(1)} %bitcast.21, ...), custom_call_target="tpu_custom_call" | custom-call | tf_op jit(solution)/shard_map/full_pass/pallas_call | solution.py:132
  82.2 3.2 %weight_grad.1 = f32[256,1792]{1,0:T(8,128)} custom-call(s32[2]{0:T(128)S(1)} %copy-done.27, bf16[64,2048]{1,0:T(8,128)(2,1)S(1)} %copy-done.3, bf16[64,2048]{1,0:T(8,128)(2,1)S(1)} %copy-done.5, bf16[64,2048]{1,0:T(8,128)(2,1)S(1)} %copy-done.7, bf16[64,2048]{1,0:T(8,128)(2,1)S(1)} %copy-done.9, bf16[64,2048]{1,0:T(8,128)(2,1)S(1)} %copy-done.11, ...), custom_call_target="tpu_custom_call" | custom-call | tf_op jit(solution)/shard_map/weight_grad/pallas_call | solution.py:244
  (59 shorter events, 0.5 us)
Async XLA Ops:
  0.6 20.9 %copy-start = (bf16[1,128,4096]{2,1,0:T(8,128)(2,1)S(1)}, bf16[1,128,4096]{2,1,0:T(8,128)(2,1)}, u32[]{:S(2)}) copy-start(bf16[1,128,4096]{2,1,0:T(8,128)(2,1)} %param.22) | copy-start | bytes 3145732
  3.6 12.2 %copy-start.26 = (s32[2]{0:T(128)}, s32[2]{0:T(128)S(1)}, u32[]{:S(2)}) copy-start(s32[2]{0:T(128)S(1)} %pad_add_fusion.place_ref) | copy-start | bytes 28
  3.6 1.0 %copy-start.18 = (bf16[1,128,2048]{2,1,0:T(8,128)(2,1)S(1)}, bf16[1,128,2048]{2,1,0:T(8,128)(2,1)}, u32[]{:S(2)}) copy-start(bf16[1,128,2048]{2,1,0:T(8,128)(2,1)} %param.12) | copy-start | bytes 1572868
  5.8 36.2 %copy-start.2 = (bf16[64,2048]{1,0:T(8,128)(2,1)}, bf16[64,2048]{1,0:T(8,128)(2,1)S(1)}, u32[]{:S(2)}) copy-start(bf16[64,2048]{1,0:T(8,128)(2,1)S(1)} %get-tuple-element.8.rest_0_) | copy-start | bytes 786436
  5.8 7.2 %collective-permute-start = (bf16[64,2048]{1,0:T(8,128)(2,1)S(1)}, bf16[64,2048]{1,0:T(8,128)(2,1)S(1)}, u32[]{:S(2)}, u32[]{:S(2)}) collective-permute-start(bf16[64,2048]{1,0:T(8,128)(2,1)S(1)} %get-tuple-element.9), channel_id=1, source_target_pairs={{0,8},{4,12},{8,0},{12,4},{16,24},{20,28},{24,16},{28,20},{1,9},{5... | collective-permute-start | bytes 786440 | tf_op jit(solution)/shard_map/ppermute | solution.py:281
  7.1 8.7 %collective-permute-start.1 = (bf16[64,2048]{1,0:T(8,128)(2,1)S(1)}, bf16[64,2048]{1,0:T(8,128)(2,1)S(1)}, u32[]{:S(2)}, u32[]{:S(2)}) collective-permute-start(bf16[64,2048]{1,0:T(8,128)(2,1)S(1)} %get-tuple-element.10), channel_id=1, source_target_pairs={{0,16},{4,20},{8,24},{12,28},{16,0},{20,4},{24,8},{28,12},{1,17},{... | collective-permute-start | bytes 786440 | tf_op jit(solution)/shard_map/ppermute | solution.py:281
  7.3 14.1 %collective-permute-start.2 = (bf16[64,2048]{1,0:T(8,128)(2,1)S(1)}, bf16[64,2048]{1,0:T(8,128)(2,1)S(1)}, u32[]{:S(2)}, u32[]{:S(2)}) collective-permute-start(bf16[64,2048]{1,0:T(8,128)(2,1)S(1)} %get-tuple-element.11), channel_id=1, source_target_pairs={{0,24},{4,28},{8,16},{12,20},{16,8},{20,12},{24,0},{28,4},{1,25},{... | collective-permute-start | bytes 786440 | tf_op jit(solution)/shard_map/ppermute | solution.py:281
  8.5 28.6 %collective-permute-start.3 = (bf16[64,2048]{1,0:T(8,128)(2,1)S(1)}, bf16[64,2048]{1,0:T(8,128)(2,1)S(1)}, u32[]{:S(2)}, u32[]{:S(2)}) collective-permute-start(bf16[64,2048]{1,0:T(8,128)(2,1)S(1)} %get-tuple-element.8.rest_0_), channel_id=1, source_target_pairs={{0,4},{4,0},{8,12},{12,8},{16,20},{20,16},{24,28},{28,24},{1,5},{5... | collective-permute-start | bytes 786440 | tf_op jit(solution)/shard_map/ppermute | solution.py:281
  13.1 24.1 %copy-start.4 = (bf16[64,2048]{1,0:T(8,128)(2,1)}, bf16[64,2048]{1,0:T(8,128)(2,1)S(1)}, u32[]{:S(2)}) copy-start(bf16[64,2048]{1,0:T(8,128)(2,1)S(1)} %collective-permute-done.rest_1_) | copy-start | bytes 786436
  13.1 25.4 %collective-permute-start.4 = (bf16[64,2048]{1,0:T(8,128)(2,1)S(1)}, bf16[64,2048]{1,0:T(8,128)(2,1)S(1)}, u32[]{:S(2)}, u32[]{:S(2)}) collective-permute-start(bf16[64,2048]{1,0:T(8,128)(2,1)S(1)} %collective-permute-done.rest_1_), channel_id=1, source_target_pairs={{0,4},{4,0},{8,12},{12,8},{16,20},{20,16},{24,28},{28,24},{1,5},{5... | collective-permute-start | bytes 786440 | tf_op jit(solution)/shard_map/ppermute | solution.py:281
  15.8 22.8 %copy-start.6 = (bf16[64,2048]{1,0:T(8,128)(2,1)}, bf16[64,2048]{1,0:T(8,128)(2,1)S(1)}, u32[]{:S(2)}) copy-start(bf16[64,2048]{1,0:T(8,128)(2,1)S(1)} %collective-permute-done.1.rest_2_) | copy-start | bytes 786436
  15.8 25.5 %collective-permute-start.5 = (bf16[64,2048]{1,0:T(8,128)(2,1)S(1)}, bf16[64,2048]{1,0:T(8,128)(2,1)S(1)}, u32[]{:S(2)}, u32[]{:S(2)}) collective-permute-start(bf16[64,2048]{1,0:T(8,128)(2,1)S(1)} %collective-permute-done.1.rest_2_), channel_id=1, source_target_pairs={{0,4},{4,0},{8,12},{12,8},{16,20},{20,16},{24,28},{28,24},{1,5},{5... | collective-permute-start | bytes 786440 | tf_op jit(solution)/shard_map/ppermute | solution.py:281
  21.4 19.8 %copy-start.8 = (bf16[64,2048]{1,0:T(8,128)(2,1)}, bf16[64,2048]{1,0:T(8,128)(2,1)S(1)}, u32[]{:S(2)}) copy-start(bf16[64,2048]{1,0:T(8,128)(2,1)S(1)} %collective-permute-done.2.rest_3_) | copy-start | bytes 786436
  21.4 20.5 %collective-permute-start.6 = (bf16[64,2048]{1,0:T(8,128)(2,1)S(1)}, bf16[64,2048]{1,0:T(8,128)(2,1)}, u32[]{:S(2)}, u32[]{:S(2)}) collective-permute-start(bf16[64,2048]{1,0:T(8,128)(2,1)S(1)} %collective-permute-done.2.rest_3_), channel_id=1, source_target_pairs={{0,4},{4,0},{8,12},{12,8},{16,20},{20,16},{24,28},{28,24},{1,5},{5... | collective-permute-start | bytes 786440 | tf_op jit(solution)/shard_map/ppermute | solution.py:281
  21.5 1.6 %copy-start.1 = (bf16[256,4096]{1,0:T(8,128)(2,1)S(1)}, bf16[256,4096]{1,0:T(8,128)(2,1)}, u32[]{:S(2)}) copy-start(bf16[256,4096]{1,0:T(8,128)(2,1)} %proj_ref.1) | copy-start | bytes 6291460
  36.5 11.2 %collective-permute-start.12 = (bf16[16,4608]{1,0:T(8,128)(2,1)}, bf16[16,4608]{1,0:T(8,128)(2,1)S(1)}, u32[]{:S(2)}, u32[]{:S(2)}) collective-permute-start(bf16[16,4608]{1,0:T(8,128)(2,1)} %get-tuple-element.13), channel_id=1, source_target_pairs={{3,0},{7,4},{11,8},{15,12},{19,16},{23,20},{27,24},{31,28}} | collective-permute-start | bytes 442376 | tf_op jit(solution)/shard_map/ppermute | solution.py:272
  37.2 4.1 %copy-start.10 = (bf16[64,2048]{1,0:T(8,128)(2,1)}, bf16[64,2048]{1,0:T(8,128)(2,1)S(1)}, u32[]{:S(2)}) copy-start(bf16[64,2048]{1,0:T(8,128)(2,1)S(1)} %collective-permute-done.3.rest_4_) | copy-start | bytes 786436
  37.2 12.0 %collective-permute-start.11 = (bf16[16,4608]{1,0:T(8,128)(2,1)}, bf16[16,4608]{1,0:T(8,128)(2,1)}, u32[]{:S(2)}, u32[]{:S(2)}) collective-permute-start(bf16[16,4608]{1,0:T(8,128)(2,1)} %get-tuple-element.13), channel_id=1, source_target_pairs={{2,0},{3,1},{6,4},{7,5},{10,8},{11,9},{14,12},{15,13},{18,16},{19,... | collective-permute-start | bytes 442376 | tf_op jit(solution)/shard_map/ppermute | solution.py:272
  38.5 2.8 %copy-start.12 = (bf16[64,2048]{1,0:T(8,128)(2,1)}, bf16[64,2048]{1,0:T(8,128)(2,1)S(1)}, u32[]{:S(2)}) copy-start(bf16[64,2048]{1,0:T(8,128)(2,1)S(1)} %collective-permute-done.4.rest_5_) | copy-start | bytes 786436
  38.5 19.0 %collective-permute-start.10 = (bf16[16,4608]{1,0:T(8,128)(2,1)}, bf16[16,4608]{1,0:T(8,128)(2,1)}, u32[]{:S(2)}, u32[]{:S(2)}) collective-permute-start(bf16[16,4608]{1,0:T(8,128)(2,1)} %get-tuple-element.13), channel_id=1, source_target_pairs={{1,0},{2,1},{3,2},{5,4},{6,5},{7,6},{9,8},{10,9},{11,10},{13,12},{... | collective-permute-start | bytes 442376 | tf_op jit(solution)/shard_map/ppermute | solution.py:272
  43.5 38.6 %collective-permute-start.9 = (bf16[128,256]{1,0:T(8,128)(2,1)}, bf16[128,256]{1,0:T(8,128)(2,1)S(1)}, u32[]{:S(2)}, u32[]{:S(2)}) collective-permute-start(bf16[128,256]{1,0:T(8,128)(2,1)} %own_columns.1.rest_8_), channel_id=1, source_target_pairs={{0,1},{1,2},{2,3},{3,0},{4,5},{5,6},{6,7},{7,4},{8,9},{9,10},{10,1... | collective-permute-start | bytes 196616 | tf_op jit(solution)/shard_map/ppermute | solution.py:277
  45.9 36.2 %collective-permute-start.8 = (bf16[128,256]{1,0:T(8,128)(2,1)}, bf16[128,256]{1,0:T(8,128)(2,1)S(1)}, u32[]{:S(2)}, u32[]{:S(2)}) collective-permute-start(bf16[128,256]{1,0:T(8,128)(2,1)} %own_columns.1.rest_8_), channel_id=1, source_target_pairs={{0,2},{1,3},{2,0},{3,1},{4,6},{5,7},{6,4},{7,5},{8,10},{9,11},{10,... | collective-permute-start | bytes 196616 | tf_op jit(solution)/shard_map/ppermute | solution.py:277
  47.7 34.4 %collective-permute-start.7 = (bf16[128,256]{1,0:T(8,128)(2,1)}, bf16[128,256]{1,0:T(8,128)(2,1)S(1)}, u32[]{:S(2)}, u32[]{:S(2)}) collective-permute-start(bf16[128,256]{1,0:T(8,128)(2,1)} %own_columns.1.rest_8_), channel_id=1, source_target_pairs={{0,3},{1,0},{2,1},{3,2},{4,7},{5,4},{6,5},{7,6},{8,11},{9,8},{10,9... | collective-permute-start | bytes 196616 | tf_op jit(solution)/shard_map/ppermute | solution.py:277
  60.6 21.5 %copy-start.3 = (bf16[64,2048]{1,0:T(8,128)(2,1)S(1)}, bf16[64,2048]{1,0:T(8,128)(2,1)}, u32[]{:S(2)}) copy-start(bf16[64,2048]{1,0:T(8,128)(2,1)} %copy-done.2) | copy-start | bytes 786436
  60.6 21.5 %copy-start.5 = (bf16[64,2048]{1,0:T(8,128)(2,1)S(1)}, bf16[64,2048]{1,0:T(8,128)(2,1)}, u32[]{:S(2)}) copy-start(bf16[64,2048]{1,0:T(8,128)(2,1)} %copy-done.4) | copy-start | bytes 786436
  60.6 21.5 %copy-start.7 = (bf16[64,2048]{1,0:T(8,128)(2,1)S(1)}, bf16[64,2048]{1,0:T(8,128)(2,1)}, u32[]{:S(2)}) copy-start(bf16[64,2048]{1,0:T(8,128)(2,1)} %copy-done.6) | copy-start | bytes 786436
  60.6 21.5 %copy-start.9 = (bf16[64,2048]{1,0:T(8,128)(2,1)S(1)}, bf16[64,2048]{1,0:T(8,128)(2,1)}, u32[]{:S(2)}) copy-start(bf16[64,2048]{1,0:T(8,128)(2,1)} %copy-done.8) | copy-start | bytes 786436
  60.6 21.5 %copy-start.11 = (bf16[64,2048]{1,0:T(8,128)(2,1)S(1)}, bf16[64,2048]{1,0:T(8,128)(2,1)}, u32[]{:S(2)}) copy-start(bf16[64,2048]{1,0:T(8,128)(2,1)} %copy-done.10) | copy-start | bytes 786436
  60.6 21.5 %copy-start.13 = (bf16[64,2048]{1,0:T(8,128)(2,1)S(1)}, bf16[64,2048]{1,0:T(8,128)(2,1)}, u32[]{:S(2)}) copy-start(bf16[64,2048]{1,0:T(8,128)(2,1)} %copy-done.12) | copy-start | bytes 786436
  60.7 21.5 %copy-start.15 = (bf16[64,2048]{1,0:T(8,128)(2,1)S(1)}, bf16[64,2048]{1,0:T(8,128)(2,1)}, u32[]{:S(2)}) copy-start(bf16[64,2048]{1,0:T(8,128)(2,1)} %copy-done.14) | copy-start | bytes 786436
  60.7 21.5 %copy-start.19 = (bf16[128,256]{1,0:T(8,128)(2,1)S(1)}, bf16[128,256]{1,0:T(8,128)(2,1)}, u32[]{:S(2)}) copy-start(bf16[128,256]{1,0:T(8,128)(2,1)} %own_columns.1.rest_8_) | copy-start | bytes 196612
  60.7 21.5 %copy-start.27 = (s32[2]{0:T(128)S(1)}, s32[2]{0:T(128)}, u32[]{:S(2)}) copy-start(s32[2]{0:T(128)} %copy-done.26) | copy-start | bytes 28
  (9 other events, 7.0 us)

commit v2 on v1

v2 whole, which is shorter than its diff:
```python
import functools
import math

import jax
import jax.numpy as jnp
from jax import lax
from jax.experimental import pallas as pl
from jax.experimental.pallas import tpu as pltpu
from jax.sharding import PartitionSpec as P

LANES = 128
BLOCK = 16
CT = 1024
CARRY_CT = 512
STATE_CT = 512
PREP_CT = 2048
HALF = 8
VMEM_BYTES = 32 * 2**20
LOG2E = math.log2(math.e)
f32 = jnp.float32
bf16 = jnp.bfloat16
WHOLE = pl.BlockSpec(memory_space=pltpu.VMEM)


def work(micros):
    return pl.CostEstimate(flops=micros * 10**7, bytes_accessed=micros * 10**4, transcendentals=0)


def softplus(v):
    return jnp.maximum(v, 0.0) + jnp.log1p(jnp.exp(-jnp.abs(v)))


def halves(v):
    high = v.astype(bf16)
    return high, (v - high.astype(f32)).astype(bf16)


def fill_picks(inc_ref, picks, token_major):
    n, toks = inc_ref.shape
    span = BLOCK * n
    col = lax.broadcasted_iota(jnp.int32, (toks, span), 1)
    state_of = lax.broadcasted_iota(jnp.int32, (n, span), 1)
    if token_major:
        own, state_of = col // n, state_of % n
    else:
        own, state_of = col % BLOCK, state_of // BLOCK
    own = own == lax.broadcasted_iota(jnp.int32, (toks, span), 0) % BLOCK
    sel = (state_of == lax.broadcasted_iota(jnp.int32, (n, span), 0)).astype(bf16)
    for part, vals in enumerate(halves(inc_ref[...])):
        wide = lax.dot_general(vals, sel, (((0,), (0,)), ((), ())), preferred_element_type=f32)
        wide = jnp.where(own, wide, 0.0).astype(bf16)
        for b in range(toks // BLOCK):
            picks[b, part * BLOCK : (part + 1) * BLOCK, :] = wide[b * BLOCK : (b + 1) * BLOCK]


def state_kernel(masks, part, place_ref, *rest):
    count = 10 if masks else 6
    sources, rest = rest[:count], rest[count:]
    (step_ref, later_ref, msg_ref, g_out, decay_out), rest = rest[:5], rest[5:]
    packs, rest = rest[: len(masks)], rest[len(masks) :]
    fetched, rest = rest[: count - 2], rest[count - 2 :]
    fetched = (*fetched[:-2], decay_out, *fetched[-2:], g_out)
    coef, sums, upto, terms0, terms1, tots, routed, small, wide = rest
    x_ref, bias_ref, decay_ref, outc_ref, proj_ref, g_ref = fetched[-6:]
    toks, chans = g_ref.shape
    n = decay_ref.shape[0]
    width = chans // n
    chunk = STATE_CT
    chunks = chans // chunk
    preps = chans // PREP_CT
    copies = [pltpu.make_async_copy(sources[k], fetched[k], small.at[k]) for k in range(count - 2)]
    for copy in copies:
        copy.start()
    columns = []
    for c in range(preps):
        at = slice(c * PREP_CT, (c + 1) * PREP_CT)
        columns.append(
            [
                pltpu.make_async_copy(sources[k].at[:, at], fetched[k].at[:, at], wide.at[k - count + 2, c])
                for k in (count - 2, count - 1)
            ]
        )
        for copy in columns[-1]:
            copy.start()

    row = lax.broadcasted_iota(jnp.int32, (toks, toks), 0)
    col = lax.broadcasted_iota(jnp.int32, (toks, toks), 1)
    for half in range(2):
        lanes = slice(half * toks, (half + 1) * toks)
        sums[:toks, lanes] = (col <= row).astype(bf16)
        sums[toks:, lanes] = (col > row).astype(bf16)
    for copy in copies:
        copy.wait()
    if masks:
        fill_packs(masks, part, place_ref, *fetched[:4], packs, routed)
    rows = lax.broadcasted_iota(jnp.int32, (n, toks), 0)
    for half, vals in enumerate(halves(outc_ref[...])):
        for m in range(n):
            coef[half * n : (half + 1) * n, m * toks : (m + 1) * toks] = jnp.where(
                rows == m, vals, jnp.zeros_like(vals)
            )

    for c in range(preps):
        at = slice(c * PREP_CT, (c + 1) * PREP_CT)
        for copy in columns[c]:
            copy.wait()
        step = softplus(jnp.dot(x_ref[...], proj_ref[:, at], preferred_element_type=f32) + bias_ref[:, at])
        step_ref[:, at] = step
        both = jnp.dot(sums[...], jnp.concatenate(halves(step), axis=0), preferred_element_type=f32)
        upto[:, at] = both[:toks].astype(bf16)
        later_ref[:, at] = both[toks:].astype(bf16)
        tots[:, at] = both[toks - 1 : toks]

    for c in range(chunks + 1):
        for m in range(n):
            if c < chunks:
                at = slice(c * chunk, (c + 1) * chunk)
                rate = jnp.broadcast_to(decay_ref[m : m + 1, at] * (-LOG2E), (BLOCK, chunk)).astype(bf16)
                for d in range(toks // BLOCK):
                    here = slice(d * BLOCK, (d + 1) * BLOCK)
                    (terms0, terms1)[c % 2][m * toks + d * BLOCK : m * toks + (d + 1) * BLOCK, :] = (
                        jnp.exp2(upto[here, at] * rate) * g_ref[here, at]
                    )
        if c > 0:
            at = slice((c - 1) * chunk, c * chunk)
            both = jnp.dot(coef[...], (terms0, terms1)[(c - 1) % 2][...], preferred_element_type=f32)
            msg_ref[:, at] = (both[:n] + both[n:]).astype(bf16)
    total = jnp.concatenate([tots[:, k * width : (k + 1) * width] for k in range(n)], axis=0)
    high, low = halves(total)
    msg_ref[:, chans : chans + width] = high
    msg_ref[:, chans + width : chans + 2 * width] = low


def state_pass(x, proj, bias, decay, outc, g, place, expert, masks, part, capacity):
    toks, chans = g.shape
    n = decay.shape[0]
    width = chans // n
    sources = [*expert, x, bias.reshape(1, -1), decay, outc, proj, g]
    kept = [v for v in sources if v is not decay and v is not g]
    if masks:
        rows, hid = expert[3].shape
        packed = [jax.ShapeDtypeStruct((rows, hid + part), bf16)] * len(masks)
        routed = (capacity, expert[2].shape[1])
    else:
        packed, routed = [], (BLOCK, LANES)
    return pl.pallas_call(
        functools.partial(state_kernel, masks, part),
        in_specs=[pl.BlockSpec(memory_space=pltpu.SMEM)] + [pl.BlockSpec(memory_space=pl.ANY)] * len(sources),
        out_specs=[WHOLE] * (5 + len(packed)),
        out_shape=[
            jax.ShapeDtypeStruct((toks, chans), f32),
            jax.ShapeDtypeStruct((toks, chans), bf16),
            jax.ShapeDtypeStruct((n, chans + 2 * width), bf16),
            jax.ShapeDtypeStruct(g.shape, g.dtype),
            jax.ShapeDtypeStruct(decay.shape, decay.dtype),
        ]
        + packed,
        scratch_shapes=[pltpu.VMEM(v.shape, v.dtype) for v in kept]
        + [
            pltpu.VMEM((2 * n, n * toks), bf16),
            pltpu.VMEM((2 * toks, 2 * toks), bf16),
            pltpu.VMEM((toks, chans), bf16),
            pltpu.VMEM((n * toks, STATE_CT), bf16),
            pltpu.VMEM((n * toks, STATE_CT), bf16),
            pltpu.VMEM((1, chans), f32),
            pltpu.VMEM(routed, bf16),
            pltpu.SemaphoreType.DMA((len(sources) - 2,)),
            pltpu.SemaphoreType.DMA((2, chans // PREP_CT)),
        ],
        compiler_params=pltpu.CompilerParams(vmem_limit_bytes=56 * 2**20),
        cost_estimate=work(8),
        name="state_pass",
    )(place, *sources)


def local_kernel(step_ref, decay_ref, outc_ref, inc_ref, skip_ref, g_ref, out_ref, outb, picks, step3, g3, adjs):
    toks, chans = g_ref.shape
    n = decay_ref.shape[0]
    tiles = CT // LANES
    blocks = toks // BLOCK
    vals = outc_ref[...]
    for t in range(toks):
        outb[t] = jnp.broadcast_to(vals[:, t : t + 1], (n, LANES))
    fill_picks(inc_ref, picks, True)

    for c in range(chans // CT):
        lanes = slice(c * CT, (c + 1) * CT)
        step3[...] = step_ref[:, lanes].reshape(blocks, BLOCK, CT)
        g3[...] = g_ref[:, lanes].astype(f32).reshape(blocks, BLOCK, CT)
        rate = [decay_ref[:, c * CT + q * LANES : c * CT + (q + 1) * LANES] * (-LOG2E) for q in range(tiles)]

        def body(i, states):
            b = blocks - 1 - i
            states = list(states)
            for k in reversed(range(BLOCK)):
                ob = outb[b * BLOCK + k]
                for q in range(tiles):
                    sl = slice(q * LANES, (q + 1) * LANES)
                    s = jnp.broadcast_to(step3[b, k : k + 1, sl], (n, LANES))
                    g = jnp.broadcast_to(g3[b, k : k + 1, sl], (n, LANES))
                    adj = states[q] + ob * g
                    adjs[b, k * n : (k + 1) * n, sl] = adj.astype(bf16)
                    states[q] = jnp.exp2(s * rate[q]) * adj
            return tuple(states)

        lax.fori_loop(0, blocks, body, tuple(jnp.zeros((n, LANES), f32) for _ in range(tiles)))
        for b in range(blocks):
            both = jnp.dot(picks[b], adjs[b], preferred_element_type=f32)
            y = both[:BLOCK] + both[BLOCK:]
            rows = slice(b * BLOCK, (b + 1) * BLOCK)
            out_ref[rows, lanes] = step_ref[rows, lanes] * y + skip_ref[:, lanes] * g_ref[rows, lanes].astype(f32)


def local_pass(step, decay, outc, inc, skip, g):
    toks, chans = g.shape
    n = decay.shape[0]
    blocks = toks // BLOCK
    return pl.pallas_call(
        local_kernel,
        in_specs=[WHOLE] * 6,
        out_specs=WHOLE,
        out_shape=jax.ShapeDtypeStruct((toks, chans), f32),
        scratch_shapes=[
            pltpu.VMEM((toks, n, LANES), f32),
            pltpu.VMEM((blocks, 2 * BLOCK, BLOCK * n), bf16),
            pltpu.VMEM((blocks, BLOCK, CT), f32),
            pltpu.VMEM((blocks, BLOCK, CT), f32),
            pltpu.VMEM((blocks, BLOCK * n, CT), bf16),
        ],
        compiler_params=pltpu.CompilerParams(vmem_limit_bytes=VMEM_BYTES),
        cost_estimate=work(13),
        name="local_pass",
    )(step, decay, outc, inc, skip.reshape(1, -1), g)


def carry_kernel(local_ref, step_ref, later_ref, decay_ref, inc_ref, *rest):
    *msgs, out_ref, picks, terms0, terms1 = rest
    toks, chans = step_ref.shape
    n = decay_ref.shape[0]
    width = chans // n
    blocks = toks // BLOCK
    chunk = CARRY_CT
    fill_picks(inc_ref, picks, False)
    totals = [
        msg[:, chans : chans + width].astype(f32) + msg[:, chans + width : chans + 2 * width].astype(f32)
        for msg in msgs[:-1]
    ]

    chunks = chans // chunk

    def prepare(c):
        lanes = slice(c * chunk, (c + 1) * chunk)
        rate = decay_ref[:, lanes] * (-LOG2E)
        state = msgs[-1][:, lanes].astype(f32)
        for k in reversed(range(len(msgs) - 1)):
            at = c * chunk
            total = [totals[k][(at + j) // width : (at + j) // width + 1, (at + j) % width : (at + j) % width + LANES] for j in range(0, chunk, LANES)]
            total = jnp.concatenate(total, axis=1)
            state = msgs[k][:, lanes].astype(f32) + jnp.exp2(total * rate) * state
        return rate, state

    for c in range(chunks + 1):
        if c < chunks:
            rate, state = prepare(c)
            terms = (terms0, terms1)[c % 2]
            lanes = slice(c * chunk, (c + 1) * chunk)
            later = later_ref[:, lanes]
        for b in range(blocks):
            if c < chunks:
                for m in range(b * n // blocks, (b + 1) * n // blocks):
                    spread_rate = jnp.broadcast_to(rate[m : m + 1], (BLOCK, chunk)).astype(bf16)
                    spread_state = jnp.broadcast_to(state[m : m + 1], (BLOCK, chunk)).astype(bf16)
                    for d in range(blocks):
                        terms[d, m * BLOCK : (m + 1) * BLOCK, :] = (
                            jnp.exp2(later[d * BLOCK : (d + 1) * BLOCK] * spread_rate) * spread_state
                        )
            if c > 0:
                done = (terms0, terms1)[(c - 1) % 2]
                at = slice((c - 1) * chunk, c * chunk)
                both = jnp.dot(picks[b], done[b], preferred_element_type=f32)
                rows = slice(b * BLOCK, (b + 1) * BLOCK)
                out_ref[rows, at] = (
                    local_ref[rows, at] + step_ref[rows, at] * (both[:BLOCK] + both[BLOCK:])
                ).astype(bf16)


def carry_pass(local, step, later, decay, inc, msgs):
    toks, chans = step.shape
    n = decay.shape[0]
    blocks = toks // BLOCK
    return pl.pallas_call(
        carry_kernel,
        in_specs=[WHOLE] * (5 + len(msgs)),
        out_specs=WHOLE,
        out_shape=jax.ShapeDtypeStruct((toks, chans), bf16),
        scratch_shapes=[
            pltpu.VMEM((blocks, 2 * BLOCK, BLOCK * n), bf16),
            pltpu.VMEM((blocks, BLOCK * n, CARRY_CT), bf16),
            pltpu.VMEM((blocks, BLOCK * n, CARRY_CT), bf16),
        ],
        compiler_params=pltpu.CompilerParams(vmem_limit_bytes=VMEM_BYTES),
        cost_estimate=work(6),
        name="carry_pass",
    )(local, step, later, decay, inc, *msgs)


def slot_rows(ids_ref, gate_ref, cot_ref, capacity):
    toks = ids_ref.shape[1]
    named = (ids_ref[...] == 0).astype(f32)
    chosen = jnp.broadcast_to(jnp.sum(named, axis=0, keepdims=True), (capacity, toks))
    gate = jnp.sum(named * gate_ref[...], axis=0, keepdims=True)
    earlier = (
        lax.broadcasted_iota(jnp.int32, (toks, toks), 0) < lax.broadcasted_iota(jnp.int32, (toks, toks), 1)
    ).astype(bf16)
    before = jnp.dot(chosen.astype(bf16), earlier, preferred_element_type=f32)
    slots = lax.broadcasted_iota(jnp.int32, (capacity, toks), 0).astype(f32)
    pick = jnp.where((before == slots) & (chosen > 0.5), 1.0, 0.0)
    weight = jnp.sum(pick * gate, axis=1, keepdims=True)
    rows = jnp.dot(pick.astype(bf16), cot_ref[...], preferred_element_type=f32)
    return (weight * rows).astype(bf16)


def fill_packs(masks, part, place_ref, ids_ref, gate_ref, cot_ref, hidden_ref, outs, routed):
    rows, hid = hidden_ref.shape
    capacity = routed.shape[0]
    routed[...] = slot_rows(ids_ref, gate_ref, cot_ref, capacity)
    pair = place_ref[0] // 2
    for mask, out in zip(masks, outs):
        out[:, :hid] = hidden_ref[...]
        target = (pair ^ (mask // 2)) * 2
        for core in range(2):
            lanes = pl.ds(pl.multiple_of((target + core) * part, LANES), part)
            out[core * capacity : (core + 1) * capacity, hid:] = routed[:, lanes]
        if 2 * capacity < rows:
            out[2 * capacity :, hid:] = jnp.zeros((rows - 2 * capacity, part), bf16)


def mine_kernel(capacity, place_ref, *rest):
    *packs, out_ref = rest
    start = pl.multiple_of((place_ref[0] % 2) * capacity, capacity)
    part = out_ref.shape[1]
    for slot, block in enumerate(packs):
        hid = block.shape[1] - part
        out_ref[slot * capacity : (slot + 1) * capacity] = block[pl.ds(start, capacity), hid:]


def mine(place, packs, part, capacity):
    return pl.pallas_call(
        functools.partial(mine_kernel, capacity),
        in_specs=[pl.BlockSpec(memory_space=pltpu.SMEM)] + [WHOLE] * len(packs),
        out_specs=WHOLE,
        out_shape=jax.ShapeDtypeStruct((len(packs) * capacity, part), bf16),
        compiler_params=pltpu.CompilerParams(vmem_limit_bytes=2 * 2**20),
        cost_estimate=work(1),
        name="own_columns",
    )(place, *packs)


def weight_kernel(capacity, peers, place_ref, *rest):
    packs = rest[:peers]
    *parts, out_ref, rows_ref = rest[peers:]
    count = len(parts)
    rows = count * capacity

    @pl.when(pl.program_id(0) == 0)
    def _():
        for ahead, piece in enumerate(parts):
            block = lax.rem(place_ref[1] + ahead, count)
            for slot in range(peers):
                start = pl.multiple_of(slot * rows + block * capacity, capacity)
                rows_ref[pl.ds(start, capacity), :] = piece[slot * capacity : (slot + 1) * capacity]

    hidden = jnp.concatenate([block[...] for block in packs], axis=0)
    out_ref[...] = lax.dot_general(
        rows_ref[...], hidden, (((0,), (0,)), ((), ())), preferred_element_type=f32
    )


def weight_grad(place, packs, parts, part, capacity):
    peers = len(packs)
    rows = packs[0].shape[0]
    hid = packs[0].shape[1] - part
    step = hid // 2 if hid % (2 * LANES) == 0 else hid
    return pl.pallas_call(
        functools.partial(weight_kernel, capacity, peers),
        grid=(hid // step,),
        in_specs=[pl.BlockSpec(memory_space=pltpu.SMEM)]
        + [pl.BlockSpec((rows, step), lambda c: (0, c))] * peers
        + [pl.BlockSpec(p.shape, lambda c: (0, 0)) for p in parts],
        out_specs=pl.BlockSpec((part, step), lambda c: (0, c)),
        out_shape=jax.ShapeDtypeStruct((part, hid), f32),
        scratch_shapes=[pltpu.VMEM((peers * rows, part), bf16)],
        compiler_params=pltpu.CompilerParams(vmem_limit_bytes=16 * 2**20),
        cost_estimate=work(3),
        name="weight_grad",
    )(place, *packs, *parts)


def routed_kernel(ids_ref, gate_ref, cot_ref, out_ref):
    out_ref[...] = slot_rows(ids_ref, gate_ref, cot_ref, out_ref.shape[0])


def routed_rows(ids, gate, cot, capacity):
    return pl.pallas_call(
        routed_kernel,
        out_shape=jax.ShapeDtypeStruct((capacity, cot.shape[1]), bf16),
        compiler_params=pltpu.CompilerParams(vmem_limit_bytes=8 * 2**20),
        cost_estimate=work(1),
        name="routed_rows",
    )(ids, gate, cot)


def from_ahead(value, axis, by):
    peers = lax.axis_size(axis)
    return lax.ppermute(value, axis, [(i, i - by) for i in range(by, peers)])


def around(value, axis, by):
    peers = lax.axis_size(axis)
    return lax.ppermute(value, axis, [(i, (i - by) % peers) for i in range(peers)])


def across(value, axis, mask):
    return lax.ppermute(value, axis, [(i, i ^ mask) for i in range(lax.axis_size(axis))])


def on_device(
    cotangent,
    expert_ids,
    gate_probs,
    hidden_acts,
    step_input,
    step_proj,
    step_bias,
    decay_rate,
    input_coef,
    output_coef,
    grad_output,
    skip_weight,
):
    peers = lax.axis_size("dp")
    spans = lax.axis_size("seq")
    hid, rows = hidden_acts.shape
    features = cotangent.shape[2]
    capacity = rows // spans
    part = features // peers
    place = jnp.stack([lax.axis_index("dp"), lax.axis_index("seq")]).astype(jnp.int32)
    gathers = (
        peers * rows * 2 < features * 4
        and peers & (peers - 1) == 0
        and peers > 1
        and part % LANES == 0
        and hid % part == 0
        and 2 * capacity <= rows
    )
    masks = list(range(0, peers, 2)) if gathers else []
    expert = [expert_ids[0].T, gate_probs[0].T, cotangent[0], hidden_acts.T] if gathers else []
    step, later, message, grad, decay, *sent = state_pass(
        step_input[0],
        step_proj,
        step_bias,
        decay_rate,
        output_coef[0],
        grad_output[0],
        place,
        expert,
        masks,
        part,
        capacity,
    )
    messages = [from_ahead(message, "seq", by) for by in range(1, spans)]
    if gathers:
        near = [sent[0]] + [across(v, "dp", m) for v, m in zip(sent[1:], masks[1:])]
    local = local_pass(step, decay, output_coef[0], input_coef[0], skip_weight, grad)

    if gathers:
        far, local, messages = lax.optimization_barrier((near[1:], local, messages))
        near = near[:1] + list(far)
        packs = near + [across(v, "dp", 1) for v in near]
        own = mine(place, packs, part, capacity)
        parts = [own] + [around(own, "seq", by) for by in range(1, spans)]
        grad_down = weight_grad(place, packs, parts, part, capacity)
    else:
        routed = routed_rows(expert_ids[0].T, gate_probs[0].T, cotangent[0], capacity)
        dense = lax.dot_general(
            lax.all_gather(routed, "seq", axis=0, tiled=True),
            hidden_acts,
            (((0,), (1,)), ((), ())),
            preferred_element_type=f32,
        )
        grad_down = lax.psum_scatter(dense, "dp", scatter_dimension=0, tiled=True)

    grad_x = carry_pass(local, step, later, decay, input_coef[0], messages)[None]
    return (grad_down, grad_x)


def solution(mesh):
    return jax.shard_map(
        on_device,
        mesh=mesh,
        in_specs=(
            P("dp", "seq", None),
            P("dp", "seq", None),
            P("dp", "seq", None),
            P("seq", "dp"),
            P("dp", "seq", None),
            P(),
            P(),
            P(),
            P("dp", None, "seq"),
            P("dp", None, "seq"),
            P("dp", "seq", None),
            P(),
        ),
        out_specs=(P("dp", "seq"), P("dp", "seq", None)),
        check_vma=False,
    )
```

time: 86.2 us -> 55.2 us (0.64)
  the two profiles are of different devices: /device:TPU:13 before, /device:TPU:0 now
where the time goes in v2:
time: 55.2 us; the launch traced here: 54.9 us
  Pallas kernels  31.5 us (57%)
  starting transfers between devices  14.7 us (27%)
  local copies, waits for them, and re-layouts  3.79 us (7%)
  waiting for transfers between devices  3.57 us (6%)
  between operations  0.78 us (1%)
  other arithmetic  0.61 us (1%)
    pallas_call x1, Pallas kernels, local_pass(): pl.pallas_call(local_kernel, in_specs=[WHOLE] * 6, out_specs=WHOLE, out_s...  11.7 us
    pallas_call x1, Pallas kernels, state_pass(): pl.pallas_call(functools.partial(state_kernel, masks, part), in_specs=[pl...  10.5 us
    pallas_call x1, Pallas kernels, carry_pass(): pl.pallas_call(carry_kernel, in_specs=[WHOLE] * (5 + len(msgs)), out_spec...  5.89 us
    ppermute x7, starting transfers between devices, across(): lax.ppermute(value, axis, [(i, i ^ mask) for i in range(lax.axis_size(axi...  5.67 us
    ppermute x3, starting transfers between devices, around(): lax.ppermute(value, axis, [(i, (i - by) % peers) for i in range(peers)])  5.14 us
    ppermute x3, starting transfers between devices, from_ahead(): return lax.ppermute(value, axis, [(i, i - by) for i in range(by, peers)])  3.85 us
    unnamed x22, local copies, waits for them, and re-layouts  3.79 us
    pallas_call x1, Pallas kernels, weight_grad(): pl.pallas_call(functools.partial(weight_kernel, capacity, peers), grid=(h...  2.87 us
  transfers between devices with their start and end apart: 13, of which 6 were waited for; matrix products, arithmetic and copies ran while one was open for 0% of the time, Pallas kernels for 32%

profile of v2, /device:TPU:0, one launch (start us, length us, event | category | flops | bytes accessed | tf_op | source)
XLA Modules:
  0.0 54.9 jit_solution(13944611193276842227)
XLA Ops:
  0.6 0.6 %pad_add_fusion.place_ref = s32[2]{0:T(128)} fusion(s32[1]{0:T(128)} %bitcast.1, s32[1]{0:T(128)} %bitcast), kind=kLoop, calls=%fused_computation | loop fusion | flops 2 | bytes 16 | tf_op jit(solution)/shard_map/stack | solution.py:447
  1.2 10.5 %state_pass.1 = (f32[128,4096]{1,0:T(8,128)}, bf16[128,4096]{1,0:T(8,128)(2,1)}, bf16[16,4608]{1,0:T(8,128)(2,1)}, bf16[128,4096]{1,0:T(8,128)(2,1)}, f32[16,409...) custom-call(s32[2]{0:T(128)} %pad_add_fusion.place_ref, ...), custom_call_target="tpu_custom_call" | custom-call | flops 80000000 | bytes 80000 | tf_op jit(solution)/shard_map/state_pass/pallas_call | solution.py:146
  11.8 1.3 %collective-permute-start.3 = (bf16[16,4608]{1,0:T(8,128)(2,1)}, bf16[16,4608]{1,0:T(8,128)(2,1)S(1)}, u32[]{:S(2)}, u32[]{:S(2)}) collective-permute-start(bf16[16,4608]{1,0:T(8,128)(2,1)} %get-tuple-element.25), channel_id=1, source_target_pairs={{1,0},{2,1},{3,2},{5,4},{6,5},{7,6},{9,8},{10,9},{11,10},{13,12},{... | collective-permute-start | bytes 442376 | tf_op jit(solution)/shard_map/ppermute | solution.py:415
  13.1 3.0 %collective-permute-start = (bf16[64,2048]{1,0:T(8,128)(2,1)}, bf16[64,2048]{1,0:T(8,128)(2,1)S(1)}, u32[]{:S(2)}, u32[]{:S(2)}) collective-permute-start(bf16[64,2048]{1,0:T(8,128)(2,1)} %get-tuple-element.19), channel_id=1, source_target_pairs={{0,8},{4,12},{8,0},{12,4},{16,24},{20,28},{24,16},{28,20},{1,9},{5... | collective-permute-start | bytes 786440 | tf_op jit(solution)/shard_map/ppermute | solution.py:424
  16.1 1.5 %collective-permute-start.1 = (bf16[64,2048]{1,0:T(8,128)(2,1)}, bf16[64,2048]{1,0:T(8,128)(2,1)S(1)}, u32[]{:S(2)}, u32[]{:S(2)}) collective-permute-start(bf16[64,2048]{1,0:T(8,128)(2,1)} %get-tuple-element.20), channel_id=1, source_target_pairs={{0,16},{4,20},{8,24},{12,28},{16,0},{20,4},{24,8},{28,12},{1,17},{... | collective-permute-start | bytes 786440 | tf_op jit(solution)/shard_map/ppermute | solution.py:424
  17.6 0.0 collective-permute-start.2
  17.6 1.3 %collective-permute-start.4 = (bf16[16,4608]{1,0:T(8,128)(2,1)}, bf16[16,4608]{1,0:T(8,128)(2,1)S(1)}, u32[]{:S(2)}, u32[]{:S(2)}) collective-permute-start(bf16[16,4608]{1,0:T(8,128)(2,1)} %get-tuple-element.25), channel_id=1, source_target_pairs={{2,0},{3,1},{6,4},{7,5},{10,8},{11,9},{14,12},{15,13},{18,16},{19,... | collective-permute-start | bytes 442376 | tf_op jit(solution)/shard_map/ppermute | solution.py:415
  18.9 1.8 %collective-permute-done.3.rest_0_ = bf16[16,4608]{1,0:T(8,128)(2,1)S(1)} collective-permute-done((bf16[16,4608]{1,0:T(8,128)(2,1)}, bf16[16,4608]{1,0:T(8,128)(2,1)S(1)}, u32[]{:S(2)}, u32[]{:S(2)}) %collective-permute-start.3) | collective-permute-done | bytes 147488 | tf_op jit(solution)/shard_map/ppermute | solution.py:415
  20.8 1.3 %collective-permute-start.5 = (bf16[16,4608]{1,0:T(8,128)(2,1)}, bf16[16,4608]{1,0:T(8,128)(2,1)S(1)}, u32[]{:S(2)}, u32[]{:S(2)}) collective-permute-start(bf16[16,4608]{1,0:T(8,128)(2,1)} %get-tuple-element.25), channel_id=1, source_target_pairs={{3,0},{7,4},{11,8},{15,12},{19,16},{23,20},{27,24},{31,28}} | collective-permute-start | bytes 442376 | tf_op jit(solution)/shard_map/ppermute | solution.py:415
  22.1 1.6 %copy-done = f32[128,4096]{1,0:T(8,128)S(1)} copy-done((f32[128,4096]{1,0:T(8,128)S(1)}, f32[128,4096]{1,0:T(8,128)}, u32[]{:S(2)}) %copy-start) | copy-done | bytes 2097176
  23.7 1.2 %copy-done.4 = bf16[128,4096]{1,0:T(8,128)(2,1)S(1)} copy-done((bf16[128,4096]{1,0:T(8,128)(2,1)S(1)}, bf16[128,4096]{1,0:T(8,128)(2,1)}, u32[]{:S(2)}) %copy-start.4) | copy-done | bytes 1048600
  24.9 0.9 %copy-done.5 = f32[16,4096]{1,0:T(8,128)S(1)} copy-done((f32[16,4096]{1,0:T(8,128)S(1)}, f32[16,4096]{1,0:T(8,128)}, u32[]{:S(2)}) %copy-start.5) | copy-done | bytes 262168
  25.8 11.7 %local_pass.1.local_ref = f32[128,4096]{1,0:T(8,128)S(1)} custom-call(f32[128,4096]{1,0:T(8,128)S(1)} %copy-done, f32[16,4096]{1,0:T(8,128)S(1)} %copy-done.5, f32[16,128]{1,0:T(8,128)S(1)} %bitcast.18, f32[16,128]{1,0:T(8,128)S(1)} %bitcast.19, f32[1,4096]{1,0:T(1,128)S(1)} %bitcast.21, bf16[128,4096]{1,0:T(8,128)(2,1)S(1)} %copy-done.4), custom_call_target="tpu_custom_call" | custom-call | flops 130000000 | bytes 130000 | tf_op jit(solution)/shard_map/local_pass/pallas_call | solution.py:218
  37.5 0.0 collective-permute-done.4.rest_1_
  37.5 0.1 collective-permute-start.6
  37.6 0.0 collective-permute-done.5.rest_2_
  37.6 0.0 collective-permute-done.rest_1_
  37.6 0.0 collective-permute-done.1.rest_2_
  37.7 0.5 collective-permute-start.7
  38.2 0.1 collective-permute-start.8
  38.3 0.4 collective-permute-start.9
  38.7 0.4 collective-permute-done.6.rest_4_
  39.1 0.4 collective-permute-done.7.rest_5_
  39.5 0.4 collective-permute-done.8.rest_6_
  39.9 0.4 collective-permute-done.9.rest_7_
  40.3 0.6 %own_columns.1.rest_8_ = bf16[128,256]{1,0:T(8,128)(2,1)S(1)} custom-call(s32[2]{0:T(128)S(1)} %copy-done.10, bf16[64,2048]{1,0:T(8,128)(2,1)S(1)} %copy-done.2, bf16[64,2048]{1,0:T(8,128)(2,1)S(1)} %collective-permute-done.rest_1_, bf16[64,2048]{1,0:T(8,128)(2,1)S(1)} %collective-permute-done.1.rest_2_, ...), custom_call_target="tpu_custom_call" | custom-call | flops 10000000 | bytes 10000 | tf_op jit(solution)/shard_map/own_columns/pallas_call | solution.py:348
  40.8 4.5 %collective-permute-start.10 = (bf16[128,256]{1,0:T(8,128)(2,1)S(1)}, bf16[128,256]{1,0:T(8,128)(2,1)S(1)}, u32[]{:S(2)}, u32[]{:S(2)}) collective-permute-start(bf16[128,256]{1,0:T(8,128)(2,1)S(1)} %own_columns.1.rest_8_), channel_id=1, source_target_pairs={{0,3},{1,0},{2,1},{3,2},{4,7},{5,4},{6,5},{7,6},{8,11},{9,8},{10,9... | collective-permute-start | bytes 196616 | tf_op jit(solution)/shard_map/ppermute | solution.py:420
  45.3 0.6 %collective-permute-start.12 = (bf16[128,256]{1,0:T(8,128)(2,1)S(1)}, bf16[128,256]{1,0:T(8,128)(2,1)S(1)}, u32[]{:S(2)}, u32[]{:S(2)}) collective-permute-start(bf16[128,256]{1,0:T(8,128)(2,1)S(1)} %own_columns.1.rest_8_), channel_id=1, source_target_pairs={{0,1},{1,2},{2,3},{3,0},{4,5},{5,6},{6,7},{7,4},{8,9},{9,10},{10,1... | collective-permute-start | bytes 196616 | tf_op jit(solution)/shard_map/ppermute | solution.py:420
  46.0 5.9 %carry_pass.1 = bf16[128,4096]{1,0:T(8,128)(2,1)} custom-call(f32[128,4096]{1,0:T(8,128)S(1)} %local_pass.1.local_ref, f32[128,4096]{1,0:T(8,128)S(1)} %copy-done.1, bf16[128,4096]{1,0:T(8,128)(2,1)S(1)} %copy-done.3, f32[16,4096]{1,0:T(8,128)S(1)} %copy-done.6, f32[16,128]{1,0:T(8,128)S(1)} %bitcast.20, ...), custom_call_target="tpu_custom_call" | custom-call | flops 60000000 | bytes 60000 | tf_op jit(solution)/shard_map/carry_pass/pallas_call | solution.py:291
  51.9 0.0 collective-permute-done.10.rest_9_
  51.9 0.1 collective-permute-done.11.rest_10_
  52.0 2.9 %weight_grad.1 = f32[256,1792]{1,0:T(8,128)} custom-call(s32[2]{0:T(128)S(1)} %copy-done.10, bf16[64,2048]{1,0:T(8,128)(2,1)S(1)} %copy-done.2, bf16[64,2048]{1,0:T(8,128)(2,1)S(1)} %collective-permute-done.rest_1_, bf16[64,2048]{1,0:T(8,128)(2,1)S(1)} %collective-permute-done.1.rest_2_, bf16[64,2048]{1,0:T(8,128)(2,1)S(1)} %collective-permute-done.2.rest_3_, ...), custom_call_target="tpu_custom_call" | custom-call | flops 30000000 | bytes 30000 | tf_op jit(solution)/shard_map/weight_grad/pallas_call | solution.py:384
  (22 shorter events, 0.0 us)
Async XLA Ops:
  1.2 20.8 %copy-start.7 = (f32[1,16,128]{2,1,0:T(8,128)S(1)}, f32[1,16,128]{2,1,0:T(8,128)}, u32[]{:S(2)}) copy-start(f32[1,16,128]{2,1,0:T(8,128)} %param.21) | copy-start | bytes 24580
  1.2 20.8 %copy-start.8 = (f32[1,16,128]{2,1,0:T(8,128)S(1)}, f32[1,16,128]{2,1,0:T(8,128)}, u32[]{:S(2)}) copy-start(f32[1,16,128]{2,1,0:T(8,128)} %param.20) | copy-start | bytes 24580
  1.2 20.8 %copy-start.9 = (f32[4096]{0:T(1024)S(1)}, f32[4096]{0:T(1024)}, u32[]{:S(2)}) copy-start(f32[4096]{0:T(1024)} %param.23) | copy-start | bytes 49156
  11.8 9.0 %collective-permute-start.3 = (bf16[16,4608]{1,0:T(8,128)(2,1)}, bf16[16,4608]{1,0:T(8,128)(2,1)S(1)}, u32[]{:S(2)}, u32[]{:S(2)}) collective-permute-start(bf16[16,4608]{1,0:T(8,128)(2,1)} %get-tuple-element.25), channel_id=1, source_target_pairs={{1,0},{2,1},{3,2},{5,4},{6,5},{7,6},{9,8},{10,9},{11,10},{13,12},{... | collective-permute-start | bytes 442376 | tf_op jit(solution)/shard_map/ppermute | solution.py:415
  13.1 24.6 %collective-permute-start = (bf16[64,2048]{1,0:T(8,128)(2,1)}, bf16[64,2048]{1,0:T(8,128)(2,1)S(1)}, u32[]{:S(2)}, u32[]{:S(2)}) collective-permute-start(bf16[64,2048]{1,0:T(8,128)(2,1)} %get-tuple-element.19), channel_id=1, source_target_pairs={{0,8},{4,12},{8,0},{12,4},{16,24},{20,28},{24,16},{28,20},{1,9},{5... | collective-permute-start | bytes 786440 | tf_op jit(solution)/shard_map/ppermute | solution.py:424
  16.1 21.6 %collective-permute-start.1 = (bf16[64,2048]{1,0:T(8,128)(2,1)}, bf16[64,2048]{1,0:T(8,128)(2,1)S(1)}, u32[]{:S(2)}, u32[]{:S(2)}) collective-permute-start(bf16[64,2048]{1,0:T(8,128)(2,1)} %get-tuple-element.20), channel_id=1, source_target_pairs={{0,16},{4,20},{8,24},{12,28},{16,0},{20,4},{24,8},{28,12},{1,17},{... | collective-permute-start | bytes 786440 | tf_op jit(solution)/shard_map/ppermute | solution.py:424
  17.6 20.1 %collective-permute-start.2 = (bf16[64,2048]{1,0:T(8,128)(2,1)}, bf16[64,2048]{1,0:T(8,128)(2,1)S(1)}, u32[]{:S(2)}, u32[]{:S(2)}) collective-permute-start(bf16[64,2048]{1,0:T(8,128)(2,1)} %get-tuple-element.21), channel_id=1, source_target_pairs={{0,24},{4,28},{8,16},{12,20},{16,8},{20,12},{24,0},{28,4},{1,25},{... | collective-permute-start | bytes 786440 | tf_op jit(solution)/shard_map/ppermute | solution.py:424
  17.6 19.9 %collective-permute-start.4 = (bf16[16,4608]{1,0:T(8,128)(2,1)}, bf16[16,4608]{1,0:T(8,128)(2,1)S(1)}, u32[]{:S(2)}, u32[]{:S(2)}) collective-permute-start(bf16[16,4608]{1,0:T(8,128)(2,1)} %get-tuple-element.25), channel_id=1, source_target_pairs={{2,0},{3,1},{6,4},{7,5},{10,8},{11,9},{14,12},{15,13},{18,16},{19,... | collective-permute-start | bytes 442376 | tf_op jit(solution)/shard_map/ppermute | solution.py:415
  20.8 16.9 %collective-permute-start.5 = (bf16[16,4608]{1,0:T(8,128)(2,1)}, bf16[16,4608]{1,0:T(8,128)(2,1)S(1)}, u32[]{:S(2)}, u32[]{:S(2)}) collective-permute-start(bf16[16,4608]{1,0:T(8,128)(2,1)} %get-tuple-element.25), channel_id=1, source_target_pairs={{3,0},{7,4},{11,8},{15,12},{19,16},{23,20},{27,24},{31,28}} | collective-permute-start | bytes 442376 | tf_op jit(solution)/shard_map/ppermute | solution.py:415
  22.1 1.6 %copy-start = (f32[128,4096]{1,0:T(8,128)S(1)}, f32[128,4096]{1,0:T(8,128)}, u32[]{:S(2)}) copy-start(f32[128,4096]{1,0:T(8,128)} %get-tuple-element.22.step_ref) | copy-start | bytes 6291460
  23.7 1.2 %copy-start.4 = (bf16[128,4096]{1,0:T(8,128)(2,1)S(1)}, bf16[128,4096]{1,0:T(8,128)(2,1)}, u32[]{:S(2)}) copy-start(bf16[128,4096]{1,0:T(8,128)(2,1)} %get-tuple-element.24.g_ref) | copy-start | bytes 3145732
  24.9 0.9 %copy-start.5 = (f32[16,4096]{1,0:T(8,128)S(1)}, f32[16,4096]{1,0:T(8,128)}, u32[]{:S(2)}) copy-start(f32[16,4096]{1,0:T(8,128)} %get-tuple-element.23.decay_ref) | copy-start | bytes 786436
  25.8 11.7 %copy-start.2 = (bf16[64,2048]{1,0:T(8,128)(2,1)S(1)}, bf16[64,2048]{1,0:T(8,128)(2,1)}, u32[]{:S(2)}) copy-start(bf16[64,2048]{1,0:T(8,128)(2,1)} %get-tuple-element.18.rest_0_) | copy-start | bytes 786436
  25.8 14.4 %copy-start.10 = (s32[2]{0:T(128)S(1)}, s32[2]{0:T(128)}, u32[]{:S(2)}) copy-start(s32[2]{0:T(128)} %pad_add_fusion.place_ref) | copy-start | bytes 28
  25.8 20.1 %copy-start.3 = (bf16[128,4096]{1,0:T(8,128)(2,1)S(1)}, bf16[128,4096]{1,0:T(8,128)(2,1)}, u32[]{:S(2)}) copy-start(bf16[128,4096]{1,0:T(8,128)(2,1)} %get-tuple-element.30.later_ref) | copy-start | bytes 3145732
  25.8 20.1 %copy-start.6 = (f32[16,4096]{1,0:T(8,128)S(1)}, f32[16,4096]{1,0:T(8,128)}, u32[]{:S(2)}) copy-start(f32[16,4096]{1,0:T(8,128)} %get-tuple-element.23.decay_ref) | copy-start | bytes 786436
  37.5 8.5 %copy-start.1 = (f32[128,4096]{1,0:T(8,128)S(1)}, f32[128,4096]{1,0:T(8,128)}, u32[]{:S(2)}) copy-start(f32[128,4096]{1,0:T(8,128)} %get-tuple-element.22.step_ref) | copy-start | bytes 6291460
  37.5 1.6 %collective-permute-start.6 = (bf16[64,2048]{1,0:T(8,128)(2,1)S(1)}, bf16[64,2048]{1,0:T(8,128)(2,1)S(1)}, u32[]{:S(2)}, u32[]{:S(2)}) collective-permute-start(bf16[64,2048]{1,0:T(8,128)(2,1)S(1)} %copy-done.2), channel_id=1, source_target_pairs={{0,4},{4,0},{8,12},{12,8},{16,20},{20,16},{24,28},{28,24},{1,5},{5... | collective-permute-start | bytes 786440 | tf_op jit(solution)/shard_map/ppermute | solution.py:424
  37.7 1.9 %collective-permute-start.7 = (bf16[64,2048]{1,0:T(8,128)(2,1)S(1)}, bf16[64,2048]{1,0:T(8,128)(2,1)S(1)}, u32[]{:S(2)}, u32[]{:S(2)}) collective-permute-start(bf16[64,2048]{1,0:T(8,128)(2,1)S(1)} %collective-permute-done.rest_1_), channel_id=1, source_target_pairs={{0,4},{4,0},{8,12},{12,8},{16,20},{20,16},{24,28},{28,24},{1,5},{5... | collective-permute-start | bytes 786440 | tf_op jit(solution)/shard_map/ppermute | solution.py:424
  38.2 1.7 %collective-permute-start.8 = (bf16[64,2048]{1,0:T(8,128)(2,1)S(1)}, bf16[64,2048]{1,0:T(8,128)(2,1)S(1)}, u32[]{:S(2)}, u32[]{:S(2)}) collective-permute-start(bf16[64,2048]{1,0:T(8,128)(2,1)S(1)} %collective-permute-done.1.rest_2_), channel_id=1, source_target_pairs={{0,4},{4,0},{8,12},{12,8},{16,20},{20,16},{24,28},{28,24},{1,5},{5... | collective-permute-start | bytes 786440 | tf_op jit(solution)/shard_map/ppermute | solution.py:424
  38.3 2.0 %collective-permute-start.9 = (bf16[64,2048]{1,0:T(8,128)(2,1)S(1)}, bf16[64,2048]{1,0:T(8,128)(2,1)S(1)}, u32[]{:S(2)}, u32[]{:S(2)}) collective-permute-start(bf16[64,2048]{1,0:T(8,128)(2,1)S(1)} %collective-permute-done.2.rest_3_), channel_id=1, source_target_pairs={{0,4},{4,0},{8,12},{12,8},{16,20},{20,16},{24,28},{28,24},{1,5},{5... | collective-permute-start | bytes 786440 | tf_op jit(solution)/shard_map/ppermute | solution.py:424
  40.8 11.0 %collective-permute-start.10 = (bf16[128,256]{1,0:T(8,128)(2,1)S(1)}, bf16[128,256]{1,0:T(8,128)(2,1)S(1)}, u32[]{:S(2)}, u32[]{:S(2)}) collective-permute-start(bf16[128,256]{1,0:T(8,128)(2,1)S(1)} %own_columns.1.rest_8_), channel_id=1, source_target_pairs={{0,3},{1,0},{2,1},{3,2},{4,7},{5,4},{6,5},{7,6},{8,11},{9,8},{10,9... | collective-permute-start | bytes 196616 | tf_op jit(solution)/shard_map/ppermute | solution.py:420
  45.3 6.7 %collective-permute-start.11 = (bf16[128,256]{1,0:T(8,128)(2,1)S(1)}, bf16[128,256]{1,0:T(8,128)(2,1)S(1)}, u32[]{:S(2)}, u32[]{:S(2)}) collective-permute-start(bf16[128,256]{1,0:T(8,128)(2,1)S(1)} %own_columns.1.rest_8_), channel_id=1, source_target_pairs={{0,2},{1,3},{2,0},{3,1},{4,6},{5,7},{6,4},{7,5},{8,10},{9,11},{10,... | collective-permute-start | bytes 196616 | tf_op jit(solution)/shard_map/ppermute | solution.py:420
  45.3 6.7 %collective-permute-start.12 = (bf16[128,256]{1,0:T(8,128)(2,1)S(1)}, bf16[128,256]{1,0:T(8,128)(2,1)S(1)}, u32[]{:S(2)}, u32[]{:S(2)}) collective-permute-start(bf16[128,256]{1,0:T(8,128)(2,1)S(1)} %own_columns.1.rest_8_), channel_id=1, source_target_pairs={{0,1},{1,2},{2,3},{3,0},{4,5},{5,6},{6,7},{7,4},{8,9},{9,10},{10,1... | collective-permute-start | bytes 196616 | tf_op jit(solution)/shard_map/ppermute | solution.py:420

commit v3 on v2

--- a/solution.py
+++ b/solution.py
@@ -53,13 +53,12 @@
             picks[b, part * BLOCK : (part + 1) * BLOCK, :] = wide[b * BLOCK : (b + 1) * BLOCK]
 
 
-def state_kernel(masks, part, place_ref, *rest):
+def state_kernel(masks, part, *rest):
     count = 10 if masks else 6
     sources, rest = rest[:count], rest[count:]
-    (step_ref, later_ref, msg_ref, g_out, decay_out), rest = rest[:5], rest[5:]
+    (step_ref, later_ref, msg_ref), rest = rest[:3], rest[3:]
     packs, rest = rest[: len(masks)], rest[len(masks) :]
-    fetched, rest = rest[: count - 2], rest[count - 2 :]
-    fetched = (*fetched[:-2], decay_out, *fetched[-2:], g_out)
+    fetched, rest = rest[:count], rest[count:]
     coef, sums, upto, terms0, terms1, tots, routed, small, wide = rest
     x_ref, bias_ref, decay_ref, outc_ref, proj_ref, g_ref = fetched[-6:]
     toks, chans = g_ref.shape
@@ -92,7 +91,7 @@
     for copy in copies:
         copy.wait()
     if masks:
-        fill_packs(masks, part, place_ref, *fetched[:4], packs, routed)
+        fill_packs(masks, part, *fetched[:4], packs, routed)
     rows = lax.broadcasted_iota(jnp.int32, (n, toks), 0)
     for half, vals in enumerate(halves(outc_ref[...])):
         for m in range(n):
@@ -100,18 +99,18 @@
                 rows == m, vals, jnp.zeros_like(vals)
             )
 
-    for c in range(preps):
-        at = slice(c * PREP_CT, (c + 1) * PREP_CT)
-        for copy in columns[c]:
-            copy.wait()
-        step = softplus(jnp.dot(x_ref[...], proj_ref[:, at], preferred_element_type=f32) + bias_ref[:, at])
-        step_ref[:, at] = step
-        both = jnp.dot(sums[...], jnp.concatenate(halves(step), axis=0), preferred_element_type=f32)
-        upto[:, at] = both[:toks].astype(bf16)
-        later_ref[:, at] = both[toks:].astype(bf16)
-        tots[:, at] = both[toks - 1 : toks]
-
     for c in range(chunks + 1):
+        if c < chunks and c * chunk % PREP_CT == 0:
+            p = c * chunk // PREP_CT
+            at = slice(p * PREP_CT, (p + 1) * PREP_CT)
+            for copy in columns[p]:
+                copy.wait()
+            step = softplus(jnp.dot(x_ref[...], proj_ref[:, at], preferred_element_type=f32) + bias_ref[:, at])
+            step_ref[:, at] = step
+            both = jnp.dot(sums[...], jnp.concatenate(halves(step), axis=0), preferred_element_type=f32)
+            upto[:, at] = both[:toks].astype(bf16)
+            later_ref[:, at] = both[toks:].astype(bf16)
+            tots[:, at] = both[toks - 1 : toks]
         for m in range(n):
             if c < chunks:
                 at = slice(c * chunk, (c + 1) * chunk)
@@ -131,12 +130,11 @@
     msg_ref[:, chans + width : chans + 2 * width] = low
 
 
-def state_pass(x, proj, bias, decay, outc, g, place, expert, masks, part, capacity):
+def state_pass(x, proj, bias, decay, outc, g, expert, masks, part, capacity):
     toks, chans = g.shape
     n = decay.shape[0]
     width = chans // n
     sources = [*expert, x, bias.reshape(1, -1), decay, outc, proj, g]
-    kept = [v for v in sources if v is not decay and v is not g]
     if masks:
         rows, hid = expert[3].shape
         packed = [jax.ShapeDtypeStruct((rows, hid + part), bf16)] * len(masks)
@@ -145,17 +143,15 @@
         packed, routed = [], (BLOCK, LANES)
     return pl.pallas_call(
         functools.partial(state_kernel, masks, part),
-        in_specs=[pl.BlockSpec(memory_space=pltpu.SMEM)] + [pl.BlockSpec(memory_space=pl.ANY)] * len(sources),
-        out_specs=[WHOLE] * (5 + len(packed)),
+        in_specs=[pl.BlockSpec(memory_space=pl.ANY)] * len(sources),
+        out_specs=[WHOLE] * (3 + len(packed)),
         out_shape=[
             jax.ShapeDtypeStruct((toks, chans), f32),
             jax.ShapeDtypeStruct((toks, chans), bf16),
             jax.ShapeDtypeStruct((n, chans + 2 * width), bf16),
-            jax.ShapeDtypeStruct(g.shape, g.dtype),
-            jax.ShapeDtypeStruct(decay.shape, decay.dtype),
         ]
         + packed,
-        scratch_shapes=[pltpu.VMEM(v.shape, v.dtype) for v in kept]
+        scratch_shapes=[pltpu.VMEM(v.shape, v.dtype) for v in sources]
         + [
             pltpu.VMEM((2 * n, n * toks), bf16),
             pltpu.VMEM((2 * toks, 2 * toks), bf16),
@@ -167,10 +163,10 @@
             pltpu.SemaphoreType.DMA((len(sources) - 2,)),
             pltpu.SemaphoreType.DMA((2, chans // PREP_CT)),
         ],
-        compiler_params=pltpu.CompilerParams(vmem_limit_bytes=56 * 2**20),
+        compiler_params=pltpu.CompilerParams(vmem_limit_bytes=58 * 2**20),
         cost_estimate=work(8),
         name="state_pass",
-    )(place, *sources)
+    )(*sources)
 
 
 def local_kernel(step_ref, decay_ref, outc_ref, inc_ref, skip_ref, g_ref, out_ref, outb, picks, step3, g3, adjs):
@@ -320,11 +316,11 @@
     return (weight * rows).astype(bf16)
 
 
-def fill_packs(masks, part, place_ref, ids_ref, gate_ref, cot_ref, hidden_ref, outs, routed):
+def fill_packs(masks, part, ids_ref, gate_ref, cot_ref, hidden_ref, outs, routed):
     rows, hid = hidden_ref.shape
     capacity = routed.shape[0]
     routed[...] = slot_rows(ids_ref, gate_ref, cot_ref, capacity)
-    pair = place_ref[0] // 2
+    pair = lax.axis_index("dp") // 2
     for mask, out in zip(masks, outs):
         out[:, :hid] = hidden_ref[...]
         target = (pair ^ (mask // 2)) * 2
@@ -335,28 +331,28 @@
             out[2 * capacity :, hid:] = jnp.zeros((rows - 2 * capacity, part), bf16)
 
 
-def mine_kernel(capacity, place_ref, *rest):
+def mine_kernel(capacity, *rest):
     *packs, out_ref = rest
-    start = pl.multiple_of((place_ref[0] % 2) * capacity, capacity)
+    start = pl.multiple_of((lax.axis_index("dp") % 2) * capacity, capacity)
     part = out_ref.shape[1]
     for slot, block in enumerate(packs):
         hid = block.shape[1] - part
         out_ref[slot * capacity : (slot + 1) * capacity] = block[pl.ds(start, capacity), hid:]
 
 
-def mine(place, packs, part, capacity):
+def mine(packs, part, capacity):
     return pl.pallas_call(
         functools.partial(mine_kernel, capacity),
-        in_specs=[pl.BlockSpec(memory_space=pltpu.SMEM)] + [WHOLE] * len(packs),
+        in_specs=[WHOLE] * len(packs),
         out_specs=WHOLE,
         out_shape=jax.ShapeDtypeStruct((len(packs) * capacity, part), bf16),
         compiler_params=pltpu.CompilerParams(vmem_limit_bytes=2 * 2**20),
         cost_estimate=work(1),
         name="own_columns",
-    )(place, *packs)
-
-
-def weight_kernel(capacity, peers, place_ref, *rest):
+    )(*packs)
+
+
+def weight_kernel(capacity, peers, step, *rest):
     packs = rest[:peers]
     *parts, out_ref, rows_ref = rest[peers:]
     count = len(parts)
@@ -365,35 +361,34 @@
     @pl.when(pl.program_id(0) == 0)
     def _():
         for ahead, piece in enumerate(parts):
-            block = lax.rem(place_ref[1] + ahead, count)
+            block = lax.axis_index("seq") ^ ahead
             for slot in range(peers):
                 start = pl.multiple_of(slot * rows + block * capacity, capacity)
                 rows_ref[pl.ds(start, capacity), :] = piece[slot * capacity : (slot + 1) * capacity]
 
-    hidden = jnp.concatenate([block[...] for block in packs], axis=0)
+    lanes = pl.ds(pl.multiple_of(pl.program_id(0) * step, LANES), step)
+    hidden = jnp.concatenate([block[:, lanes] for block in packs], axis=0)
     out_ref[...] = lax.dot_general(
         rows_ref[...], hidden, (((0,), (0,)), ((), ())), preferred_element_type=f32
     )
 
 
-def weight_grad(place, packs, parts, part, capacity):
+def weight_grad(packs, parts, part, capacity):
     peers = len(packs)
     rows = packs[0].shape[0]
     hid = packs[0].shape[1] - part
     step = hid // 2 if hid % (2 * LANES) == 0 else hid
     return pl.pallas_call(
-        functools.partial(weight_kernel, capacity, peers),
+        functools.partial(weight_kernel, capacity, peers, step),
         grid=(hid // step,),
-        in_specs=[pl.BlockSpec(memory_space=pltpu.SMEM)]
-        + [pl.BlockSpec((rows, step), lambda c: (0, c))] * peers
-        + [pl.BlockSpec(p.shape, lambda c: (0, 0)) for p in parts],
+        in_specs=[WHOLE] * (peers + len(parts)),
         out_specs=pl.BlockSpec((part, step), lambda c: (0, c)),
         out_shape=jax.ShapeDtypeStruct((part, hid), f32),
         scratch_shapes=[pltpu.VMEM((peers * rows, part), bf16)],
         compiler_params=pltpu.CompilerParams(vmem_limit_bytes=16 * 2**20),
         cost_estimate=work(3),
         name="weight_grad",
-    )(place, *packs, *parts)
+    )(*packs, *parts)
 
 
 def routed_kernel(ids_ref, gate_ref, cot_ref, out_ref):
@@ -413,11 +408,6 @@
 def from_ahead(value, axis, by):
     peers = lax.axis_size(axis)
     return lax.ppermute(value, axis, [(i, i - by) for i in range(by, peers)])
-
-
-def around(value, axis, by):
-    peers = lax.axis_size(axis)
-    return lax.ppermute(value, axis, [(i, (i - by) % peers) for i in range(peers)])
 
 
 def across(value, axis, mask):
@@ -444,10 +434,10 @@
     features = cotangent.shape[2]
     capacity = rows // spans
     part = features // peers
-    place = jnp.stack([lax.axis_index("dp"), lax.axis_index("seq")]).astype(jnp.int32)
     gathers = (
         peers * rows * 2 < features * 4
         and peers & (peers - 1) == 0
+        and spans & (spans - 1) == 0
         and peers > 1
         and part % LANES == 0
         and hid % part == 0
@@ -455,14 +445,13 @@
     )
     masks = list(range(0, peers, 2)) if gathers else []
     expert = [expert_ids[0].T, gate_probs[0].T, cotangent[0], hidden_acts.T] if gathers else []
-    step, later, message, grad, decay, *sent = state_pass(
+    step, later, message, *sent = state_pass(
         step_input[0],
         step_proj,
         step_bias,
         decay_rate,
         output_coef[0],
         grad_output[0],
-        place,
         expert,
         masks,
         part,
@@ -471,15 +460,15 @@
     messages = [from_ahead(message, "seq", by) for by in range(1, spans)]
     if gathers:
         near = [sent[0]] + [across(v, "dp", m) for v, m in zip(sent[1:], masks[1:])]
-    local = local_pass(step, decay, output_coef[0], input_coef[0], skip_weight, grad)
+    local = local_pass(step, decay_rate, output_coef[0], input_coef[0], skip_weight, grad_output[0])
 
     if gathers:
         far, local, messages = lax.optimization_barrier((near[1:], local, messages))
         near = near[:1] + list(far)
         packs = near + [across(v, "dp", 1) for v in near]
-        own = mine(place, packs, part, capacity)
-        parts = [own] + [around(own, "seq", by) for by in range(1, spans)]
-        grad_down = weight_grad(place, packs, parts, part, capacity)
+        own = mine(packs, part, capacity)
+        parts = [own] + [across(own, "seq", by) for by in range(1, spans)]
+        grad_down = weight_grad(packs, parts, part, capacity)
     else:
         routed = routed_rows(expert_ids[0].T, gate_probs[0].T, cotangent[0], capacity)
         dense = lax.dot_general(
@@ -490,7 +479,7 @@
         )
         grad_down = lax.psum_scatter(dense, "dp", scatter_dimension=0, tiled=True)
 
-    grad_x = carry_pass(local, step, later, decay, input_coef[0], messages)[None]
+    grad_x = carry_pass(local, step, later, decay_rate, input_coef[0], messages)[None]
     return (grad_down, grad_x)
 
 

time: 55.2 us -> 50.6 us (0.917)
  local copies, waits for them, and re-layouts: 3.79 us -> 1.62 us
  Pallas kernels: 31.5 us -> 29.5 us
  other arithmetic: 0.61 us -> 0 us
    ppermute x3 -> x0, starting transfers between devices: 5.14 us -> none  [around(): lax.ppermute(value, axis, [(i, (i - by) % peers) for i in range(peers)])]
    ppermute x7 -> x10, starting transfers between devices: 5.67 us -> 10.7 us  [across(): lax.ppermute(value, axis, [(i, i ^ mask) for i in range(lax.axis_size(axi...]
    unnamed x22 -> x18, local copies, waits for them, and re-layouts: 3.79 us -> 1.62 us
    pallas_call x2, Pallas kernels: 3.43 us -> 1.93 us  [the longest x1 1.92 us: weight_grad(): pl.pallas_call(functools.partial(weight_kernel, capacity, peers, step), g...]
    another operation x1 -> x0, other arithmetic: 0.61 us -> none  [on_device(): jnp.stack([lax.axis_index('dp'), lax.axis_index('seq')]).astype(jnp.int32)]
    ppermute x7 -> x10, waiting for transfers between devices: 1.56 us -> 1.82 us  [across(): lax.ppermute(value, axis, [(i, i ^ mask) for i in range(lax.axis_size(axi...]
  transfers between devices with their start and end apart: 13 -> 13, of which waited for: 6 -> 6; matrix products, arithmetic and copies ran while one was open for 0% -> 0% of each run, Pallas kernels for 32% -> 35%
where the time goes in v3:
time: 50.6 us; the launch traced here: 50.4 us
  Pallas kernels  29.5 us (58%)
  starting transfers between devices  14.8 us (29%)
  waiting for transfers between devices  3.69 us (7%)
  local copies, waits for them, and re-layouts  1.62 us (3%)
  between operations  0.83 us (2%)
    pallas_call x1, Pallas kernels, local_pass(): pl.pallas_call(local_kernel, in_specs=[WHOLE] * 6, out_specs=WHOLE, out_s...  11.7 us
    ppermute x10, starting transfers between devices, across(): lax.ppermute(value, axis, [(i, i ^ mask) for i in range(lax.axis_size(axi...  10.7 us
    pallas_call x1, Pallas kernels, state_pass(): pl.pallas_call(functools.partial(state_kernel, masks, part), in_specs=[pl...  10 us
    pallas_call x1, Pallas kernels, carry_pass(): pl.pallas_call(carry_kernel, in_specs=[WHOLE] * (5 + len(msgs)), out_spec...  5.89 us
    ppermute x3, starting transfers between devices, from_ahead(): return lax.ppermute(value, axis, [(i, i - by) for i in range(by, peers)])  4.03 us
    pallas_call x1, Pallas kernels, weight_grad(): pl.pallas_call(functools.partial(weight_kernel, capacity, peers, step), g...  1.92 us
    ppermute x3, waiting for transfers between devices, from_ahead(): return lax.ppermute(value, axis, [(i, i - by) for i in range(by, peers)])  1.86 us
    ppermute x10, waiting for transfers between devices, across(): lax.ppermute(value, axis, [(i, i ^ mask) for i in range(lax.axis_size(axi...  1.82 us
  transfers between devices with their start and end apart: 13, of which 6 were waited for; matrix products, arithmetic and copies ran while one was open for 0% of the time, Pallas kernels for 35%

profile of v3, /device:TPU:0, one launch (start us, length us, event | category | flops | bytes accessed | tf_op | source)
XLA Modules:
  0.0 50.4 jit_solution(15971935674189673469)
XLA Ops:
  0.7 10.0 %state_pass.1 = (f32[128,4096]{1,0:T(8,128)}, bf16[128,4096]{1,0:T(8,128)(2,1)}, bf16[16,4608]{1,0:T(8,128)(2,1)}, bf16[64,2048]{1,0:T(8,128)(2,1)}, bf16[64,204...) custom-call(s32[2,128]{1,0:T(2,128)} %bitcast.27, f32[2,128]{1,0:T(2,128)} %bitcast.28, ...), custom_call_target="tpu_custom_call" | custom-call | flops 80000000 | bytes 80000 | tf_op jit(solution)/shard_map/state_pass/pallas_call | solution.py:144
  10.7 1.3 %collective-permute-start.3 = (bf16[16,4608]{1,0:T(8,128)(2,1)}, bf16[16,4608]{1,0:T(8,128)(2,1)S(1)}, u32[]{:S(2)}, u32[]{:S(2)}) collective-permute-start(bf16[16,4608]{1,0:T(8,128)(2,1)} %get-tuple-element.21), channel_id=1, source_target_pairs={{1,0},{2,1},{3,2},{5,4},{6,5},{7,6},{9,8},{10,9},{11,10},{13,12},{... | collective-permute-start | bytes 442376 | tf_op jit(solution)/shard_map/ppermute | solution.py:410
  12.0 3.0 %collective-permute-start = (bf16[64,2048]{1,0:T(8,128)(2,1)}, bf16[64,2048]{1,0:T(8,128)(2,1)S(1)}, u32[]{:S(2)}, u32[]{:S(2)}) collective-permute-start(bf16[64,2048]{1,0:T(8,128)(2,1)} %get-tuple-element.17), channel_id=1, source_target_pairs={{0,8},{4,12},{8,0},{12,4},{16,24},{20,28},{24,16},{28,20},{1,9},{5... | collective-permute-start | bytes 786440 | tf_op jit(solution)/shard_map/ppermute | solution.py:414
  15.0 1.5 %collective-permute-start.1 = (bf16[64,2048]{1,0:T(8,128)(2,1)}, bf16[64,2048]{1,0:T(8,128)(2,1)S(1)}, u32[]{:S(2)}, u32[]{:S(2)}) collective-permute-start(bf16[64,2048]{1,0:T(8,128)(2,1)} %get-tuple-element.18), channel_id=1, source_target_pairs={{0,16},{4,20},{8,24},{12,28},{16,0},{20,4},{24,8},{28,12},{1,17},{... | collective-permute-start | bytes 786440 | tf_op jit(solution)/shard_map/ppermute | solution.py:414
  16.6 0.0 collective-permute-start.2
  16.6 1.3 %collective-permute-start.4 = (bf16[16,4608]{1,0:T(8,128)(2,1)}, bf16[16,4608]{1,0:T(8,128)(2,1)S(1)}, u32[]{:S(2)}, u32[]{:S(2)}) collective-permute-start(bf16[16,4608]{1,0:T(8,128)(2,1)} %get-tuple-element.21), channel_id=1, source_target_pairs={{2,0},{3,1},{6,4},{7,5},{10,8},{11,9},{14,12},{15,13},{18,16},{19,... | collective-permute-start | bytes 442376 | tf_op jit(solution)/shard_map/ppermute | solution.py:410
  17.9 1.8 %collective-permute-done.3.rest_0_ = bf16[16,4608]{1,0:T(8,128)(2,1)S(1)} collective-permute-done((bf16[16,4608]{1,0:T(8,128)(2,1)}, bf16[16,4608]{1,0:T(8,128)(2,1)S(1)}, u32[]{:S(2)}, u32[]{:S(2)}) %collective-permute-start.3) | collective-permute-done | bytes 147488 | tf_op jit(solution)/shard_map/ppermute | solution.py:410
  19.7 1.5 %collective-permute-start.5 = (bf16[16,4608]{1,0:T(8,128)(2,1)}, bf16[16,4608]{1,0:T(8,128)(2,1)S(1)}, u32[]{:S(2)}, u32[]{:S(2)}) collective-permute-start(bf16[16,4608]{1,0:T(8,128)(2,1)} %get-tuple-element.21), channel_id=1, source_target_pairs={{3,0},{7,4},{11,8},{15,12},{19,16},{23,20},{27,24},{31,28}} | collective-permute-start | bytes 442376 | tf_op jit(solution)/shard_map/ppermute | solution.py:410
  21.2 1.6 %copy-done = f32[128,4096]{1,0:T(8,128)S(1)} copy-done((f32[128,4096]{1,0:T(8,128)S(1)}, f32[128,4096]{1,0:T(8,128)}, u32[]{:S(2)}) %copy-start) | copy-done | bytes 2097176
  22.8 11.7 %local_pass.1.local_ref = f32[128,4096]{1,0:T(8,128)S(1)} custom-call(f32[128,4096]{1,0:T(8,128)S(1)} %copy-done, f32[16,4096]{1,0:T(8,128)S(1)} %copy-done.3, f32[16,128]{1,0:T(8,128)S(1)} %bitcast.18, f32[16,128]{1,0:T(8,128)S(1)} %bitcast.19, f32[1,4096]{1,0:T(1,128)S(1)} %bitcast.21, bf16[128,4096]{1,0:T(8,128)(2,1)S(1)} %bitcast.16), custom_call_target="tpu_custom_call" | custom-call | flops 130000000 | bytes 130000 | tf_op jit(solution)/shard_map/local_pass/pallas_call | solution.py:214
  34.5 0.0 collective-permute-done.4.rest_1_
  34.5 0.0 copy-done.4
  34.5 0.1 collective-permute-start.6
  34.6 0.0 collective-permute-done.5.rest_2_
  34.6 0.0 collective-permute-done.rest_1_
  34.6 0.0 collective-permute-done.1.rest_2_
  34.6 0.0 collective-permute-done.2.rest_3_
  34.6 0.5 %collective-permute-start.7 = (bf16[64,2048]{1,0:T(8,128)(2,1)S(1)}, bf16[64,2048]{1,0:T(8,128)(2,1)S(1)}, u32[]{:S(2)}, u32[]{:S(2)}) collective-permute-start(bf16[64,2048]{1,0:T(8,128)(2,1)S(1)} %collective-permute-done.rest_1_), channel_id=1, source_target_pairs={{0,4},{4,0},{8,12},{12,8},{16,20},{20,16},{24,28},{28,24},{1,5},{5... | collective-permute-start | bytes 786440 | tf_op jit(solution)/shard_map/ppermute | solution.py:414
  35.2 0.1 collective-permute-start.8
  35.3 0.4 collective-permute-start.9
  35.7 0.4 collective-permute-done.6.rest_4_
  36.1 0.4 collective-permute-done.7.rest_5_
  36.5 0.4 collective-permute-done.8.rest_6_
  36.9 0.4 collective-permute-done.9.rest_7_
  37.3 1.2 %collective-permute-start.10 = (bf16[128,256]{1,0:T(8,128)(2,1)S(1)}, bf16[128,256]{1,0:T(8,128)(2,1)S(1)}, u32[]{:S(2)}, u32[]{:S(2)}) collective-permute-start(bf16[128,256]{1,0:T(8,128)(2,1)S(1)} %own_columns.1.rest_8_), channel_id=1, source_target_pairs={{0,1},{1,0},{2,3},{3,2},{4,5},{5,4},{6,7},{7,6},{8,9},{9,8},{10,11... | collective-permute-start | bytes 196616 | tf_op jit(solution)/shard_map/ppermute | solution.py:414
  38.4 3.9 %collective-permute-start.11 = (bf16[128,256]{1,0:T(8,128)(2,1)S(1)}, bf16[128,256]{1,0:T(8,128)(2,1)S(1)}, u32[]{:S(2)}, u32[]{:S(2)}) collective-permute-start(bf16[128,256]{1,0:T(8,128)(2,1)S(1)} %own_columns.1.rest_8_), channel_id=1, source_target_pairs={{0,2},{1,3},{2,0},{3,1},{4,6},{5,7},{6,4},{7,5},{8,10},{9,11},{10,... | collective-permute-start | bytes 196616 | tf_op jit(solution)/shard_map/ppermute | solution.py:414
  42.3 0.0 collective-permute-start.12
  42.3 5.9 %carry_pass.1 = bf16[128,4096]{1,0:T(8,128)(2,1)} custom-call(f32[128,4096]{1,0:T(8,128)S(1)} %local_pass.1.local_ref, f32[128,4096]{1,0:T(8,128)S(1)} %copy-done.1, bf16[128,4096]{1,0:T(8,128)(2,1)S(1)} %copy-done.5, f32[16,4096]{1,0:T(8,128)S(1)} %copy-done.3, f32[16,128]{1,0:T(8,128)S(1)} %bitcast.20, ...), custom_call_target="tpu_custom_call" | custom-call | flops 60000000 | bytes 60000 | tf_op jit(solution)/shard_map/carry_pass/pallas_call | solution.py:287
  48.2 0.0 collective-permute-done.10.rest_9_
  48.2 0.0 collective-permute-done.11.rest_10_
  48.2 0.3 collective-permute-done.12.rest_11_
  48.5 1.9 %weight_grad.1 = f32[256,1792]{1,0:T(8,128)} custom-call(bf16[64,2048]{1,0:T(8,128)(2,1)S(1)} %copy-done.4, bf16[64,2048]{1,0:T(8,128)(2,1)S(1)} %collective-permute-done.rest_1_, bf16[64,2048]{1,0:T(8,128)(2,1)S(1)} %collective-permute-done.1.rest_2_, bf16[64,2048]{1,0:T(8,128)(2,1)S(1)} %collective-permute-done.2.rest_3_, ...), custom_call_target="tpu_custom_call" | custom-call | flops 30000000 | bytes 30000 | tf_op jit(solution)/shard_map/weight_grad/pallas_call | solution.py:381
  (17 shorter events, 0.0 us)
Async XLA Ops:
  0.6 20.5 %copy-start.2 = (bf16[1,128,4096]{2,1,0:T(8,128)(2,1)S(1)}, bf16[1,128,4096]{2,1,0:T(8,128)(2,1)}, u32[]{:S(2)}) copy-start(bf16[1,128,4096]{2,1,0:T(8,128)(2,1)} %param.22) | copy-start | bytes 3145732
  0.6 20.5 %copy-start.3 = (f32[16,4096]{1,0:T(8,128)S(1)}, f32[16,4096]{1,0:T(8,128)}, u32[]{:S(2)}) copy-start(f32[16,4096]{1,0:T(8,128)} %decay_ref.3) | copy-start | bytes 786436
  0.7 20.5 %copy-start.6 = (f32[1,16,128]{2,1,0:T(8,128)S(1)}, f32[1,16,128]{2,1,0:T(8,128)}, u32[]{:S(2)}) copy-start(f32[1,16,128]{2,1,0:T(8,128)} %param.21) | copy-start | bytes 24580
  0.7 20.5 %copy-start.7 = (f32[1,16,128]{2,1,0:T(8,128)S(1)}, f32[1,16,128]{2,1,0:T(8,128)}, u32[]{:S(2)}) copy-start(f32[1,16,128]{2,1,0:T(8,128)} %param.20) | copy-start | bytes 24580
  0.7 20.5 %copy-start.8 = (f32[4096]{0:T(1024)S(1)}, f32[4096]{0:T(1024)}, u32[]{:S(2)}) copy-start(f32[4096]{0:T(1024)} %param.23) | copy-start | bytes 49156
  10.7 9.0 %collective-permute-start.3 = (bf16[16,4608]{1,0:T(8,128)(2,1)}, bf16[16,4608]{1,0:T(8,128)(2,1)S(1)}, u32[]{:S(2)}, u32[]{:S(2)}) collective-permute-start(bf16[16,4608]{1,0:T(8,128)(2,1)} %get-tuple-element.21), channel_id=1, source_target_pairs={{1,0},{2,1},{3,2},{5,4},{6,5},{7,6},{9,8},{10,9},{11,10},{13,12},{... | collective-permute-start | bytes 442376 | tf_op jit(solution)/shard_map/ppermute | solution.py:410
  12.0 22.6 %collective-permute-start = (bf16[64,2048]{1,0:T(8,128)(2,1)}, bf16[64,2048]{1,0:T(8,128)(2,1)S(1)}, u32[]{:S(2)}, u32[]{:S(2)}) collective-permute-start(bf16[64,2048]{1,0:T(8,128)(2,1)} %get-tuple-element.17), channel_id=1, source_target_pairs={{0,8},{4,12},{8,0},{12,4},{16,24},{20,28},{24,16},{28,20},{1,9},{5... | collective-permute-start | bytes 786440 | tf_op jit(solution)/shard_map/ppermute | solution.py:414
  15.0 19.6 %collective-permute-start.1 = (bf16[64,2048]{1,0:T(8,128)(2,1)}, bf16[64,2048]{1,0:T(8,128)(2,1)S(1)}, u32[]{:S(2)}, u32[]{:S(2)}) collective-permute-start(bf16[64,2048]{1,0:T(8,128)(2,1)} %get-tuple-element.18), channel_id=1, source_target_pairs={{0,16},{4,20},{8,24},{12,28},{16,0},{20,4},{24,8},{28,12},{1,17},{... | collective-permute-start | bytes 786440 | tf_op jit(solution)/shard_map/ppermute | solution.py:414
  16.6 18.1 %collective-permute-start.2 = (bf16[64,2048]{1,0:T(8,128)(2,1)}, bf16[64,2048]{1,0:T(8,128)(2,1)S(1)}, u32[]{:S(2)}, u32[]{:S(2)}) collective-permute-start(bf16[64,2048]{1,0:T(8,128)(2,1)} %get-tuple-element.19), channel_id=1, source_target_pairs={{0,24},{4,28},{8,16},{12,20},{16,8},{20,12},{24,0},{28,4},{1,25},{... | collective-permute-start | bytes 786440 | tf_op jit(solution)/shard_map/ppermute | solution.py:414
  16.6 17.9 %collective-permute-start.4 = (bf16[16,4608]{1,0:T(8,128)(2,1)}, bf16[16,4608]{1,0:T(8,128)(2,1)S(1)}, u32[]{:S(2)}, u32[]{:S(2)}) collective-permute-start(bf16[16,4608]{1,0:T(8,128)(2,1)} %get-tuple-element.21), channel_id=1, source_target_pairs={{2,0},{3,1},{6,4},{7,5},{10,8},{11,9},{14,12},{15,13},{18,16},{19,... | collective-permute-start | bytes 442376 | tf_op jit(solution)/shard_map/ppermute | solution.py:410
  19.7 14.9 %collective-permute-start.5 = (bf16[16,4608]{1,0:T(8,128)(2,1)}, bf16[16,4608]{1,0:T(8,128)(2,1)S(1)}, u32[]{:S(2)}, u32[]{:S(2)}) collective-permute-start(bf16[16,4608]{1,0:T(8,128)(2,1)} %get-tuple-element.21), channel_id=1, source_target_pairs={{3,0},{7,4},{11,8},{15,12},{19,16},{23,20},{27,24},{31,28}} | collective-permute-start | bytes 442376 | tf_op jit(solution)/shard_map/ppermute | solution.py:410
  21.2 1.6 %copy-start = (f32[128,4096]{1,0:T(8,128)S(1)}, f32[128,4096]{1,0:T(8,128)}, u32[]{:S(2)}) copy-start(f32[128,4096]{1,0:T(8,128)} %get-tuple-element.20.step_ref) | copy-start | bytes 6291460
  22.8 11.7 %copy-start.4 = (bf16[64,2048]{1,0:T(8,128)(2,1)S(1)}, bf16[64,2048]{1,0:T(8,128)(2,1)}, u32[]{:S(2)}) copy-start(bf16[64,2048]{1,0:T(8,128)(2,1)} %get-tuple-element.16.rest_0_) | copy-start | bytes 786436
  22.8 19.5 %copy-start.5 = (bf16[128,4096]{1,0:T(8,128)(2,1)S(1)}, bf16[128,4096]{1,0:T(8,128)(2,1)}, u32[]{:S(2)}) copy-start(bf16[128,4096]{1,0:T(8,128)(2,1)} %get-tuple-element.26.later_ref) | copy-start | bytes 3145732
  34.5 7.9 %copy-start.1 = (f32[128,4096]{1,0:T(8,128)S(1)}, f32[128,4096]{1,0:T(8,128)}, u32[]{:S(2)}) copy-start(f32[128,4096]{1,0:T(8,128)} %get-tuple-element.20.step_ref) | copy-start | bytes 6291460
  34.5 1.6 %collective-permute-start.6 = (bf16[64,2048]{1,0:T(8,128)(2,1)S(1)}, bf16[64,2048]{1,0:T(8,128)(2,1)S(1)}, u32[]{:S(2)}, u32[]{:S(2)}) collective-permute-start(bf16[64,2048]{1,0:T(8,128)(2,1)S(1)} %copy-done.4), channel_id=1, source_target_pairs={{0,4},{4,0},{8,12},{12,8},{16,20},{20,16},{24,28},{28,24},{1,5},{5... | collective-permute-start | bytes 786440 | tf_op jit(solution)/shard_map/ppermute | solution.py:414
  34.6 1.9 %collective-permute-start.7 = (bf16[64,2048]{1,0:T(8,128)(2,1)S(1)}, bf16[64,2048]{1,0:T(8,128)(2,1)S(1)}, u32[]{:S(2)}, u32[]{:S(2)}) collective-permute-start(bf16[64,2048]{1,0:T(8,128)(2,1)S(1)} %collective-permute-done.rest_1_), channel_id=1, source_target_pairs={{0,4},{4,0},{8,12},{12,8},{16,20},{20,16},{24,28},{28,24},{1,5},{5... | collective-permute-start | bytes 786440 | tf_op jit(solution)/shard_map/ppermute | solution.py:414
  35.2 1.7 %collective-permute-start.8 = (bf16[64,2048]{1,0:T(8,128)(2,1)S(1)}, bf16[64,2048]{1,0:T(8,128)(2,1)S(1)}, u32[]{:S(2)}, u32[]{:S(2)}) collective-permute-start(bf16[64,2048]{1,0:T(8,128)(2,1)S(1)} %collective-permute-done.1.rest_2_), channel_id=1, source_target_pairs={{0,4},{4,0},{8,12},{12,8},{16,20},{20,16},{24,28},{28,24},{1,5},{5... | collective-permute-start | bytes 786440 | tf_op jit(solution)/shard_map/ppermute | solution.py:414
  35.3 2.0 %collective-permute-start.9 = (bf16[64,2048]{1,0:T(8,128)(2,1)S(1)}, bf16[64,2048]{1,0:T(8,128)(2,1)S(1)}, u32[]{:S(2)}, u32[]{:S(2)}) collective-permute-start(bf16[64,2048]{1,0:T(8,128)(2,1)S(1)} %collective-permute-done.2.rest_3_), channel_id=1, source_target_pairs={{0,4},{4,0},{8,12},{12,8},{16,20},{20,16},{24,28},{28,24},{1,5},{5... | collective-permute-start | bytes 786440 | tf_op jit(solution)/shard_map/ppermute | solution.py:414
  37.3 11.0 %collective-permute-start.10 = (bf16[128,256]{1,0:T(8,128)(2,1)S(1)}, bf16[128,256]{1,0:T(8,128)(2,1)S(1)}, u32[]{:S(2)}, u32[]{:S(2)}) collective-permute-start(bf16[128,256]{1,0:T(8,128)(2,1)S(1)} %own_columns.1.rest_8_), channel_id=1, source_target_pairs={{0,1},{1,0},{2,3},{3,2},{4,5},{5,4},{6,7},{7,6},{8,9},{9,8},{10,11... | collective-permute-start | bytes 196616 | tf_op jit(solution)/shard_map/ppermute | solution.py:414
  38.4 9.8 %collective-permute-start.11 = (bf16[128,256]{1,0:T(8,128)(2,1)S(1)}, bf16[128,256]{1,0:T(8,128)(2,1)S(1)}, u32[]{:S(2)}, u32[]{:S(2)}) collective-permute-start(bf16[128,256]{1,0:T(8,128)(2,1)S(1)} %own_columns.1.rest_8_), channel_id=1, source_target_pairs={{0,2},{1,3},{2,0},{3,1},{4,6},{5,7},{6,4},{7,5},{8,10},{9,11},{10,... | collective-permute-start | bytes 196616 | tf_op jit(solution)/shard_map/ppermute | solution.py:414
  42.3 6.2 %collective-permute-start.12 = (bf16[128,256]{1,0:T(8,128)(2,1)S(1)}, bf16[128,256]{1,0:T(8,128)(2,1)S(1)}, u32[]{:S(2)}, u32[]{:S(2)}) collective-permute-start(bf16[128,256]{1,0:T(8,128)(2,1)S(1)} %own_columns.1.rest_8_), channel_id=1, source_target_pairs={{0,3},{1,2},{2,1},{3,0},{4,7},{5,6},{6,5},{7,4},{8,11},{9,10},{10,... | collective-permute-start | bytes 196616 | tf_op jit(solution)/shard_map/ppermute | solution.py:414

commit v4 on v3

--- a/solution.py
+++ b/solution.py
@@ -11,7 +11,7 @@
 LANES = 128
 BLOCK = 16
 CT = 1024
-CARRY_CT = 512
+CARRY_CT = 256
 STATE_CT = 512
 PREP_CT = 2048
 HALF = 8
@@ -85,9 +85,7 @@
     row = lax.broadcasted_iota(jnp.int32, (toks, toks), 0)
     col = lax.broadcasted_iota(jnp.int32, (toks, toks), 1)
     for half in range(2):
-        lanes = slice(half * toks, (half + 1) * toks)
-        sums[:toks, lanes] = (col <= row).astype(bf16)
-        sums[toks:, lanes] = (col > row).astype(bf16)
+        sums[:, half * toks : (half + 1) * toks] = (col <= row).astype(bf16)
     for copy in copies:
         copy.wait()
     if masks:
@@ -107,10 +105,11 @@
                 copy.wait()
             step = softplus(jnp.dot(x_ref[...], proj_ref[:, at], preferred_element_type=f32) + bias_ref[:, at])
             step_ref[:, at] = step
-            both = jnp.dot(sums[...], jnp.concatenate(halves(step), axis=0), preferred_element_type=f32)
-            upto[:, at] = both[:toks].astype(bf16)
-            later_ref[:, at] = both[toks:].astype(bf16)
-            tots[:, at] = both[toks - 1 : toks]
+            summed = jnp.dot(sums[...], jnp.concatenate(halves(step), axis=0), preferred_element_type=f32)
+            total = summed[toks - 1 : toks]
+            upto[:, at] = summed.astype(bf16)
+            later_ref[:, at] = (total - summed).astype(bf16)
+            tots[:, at] = total
         for m in range(n):
             if c < chunks:
                 at = slice(c * chunk, (c + 1) * chunk)
@@ -154,7 +153,7 @@
         scratch_shapes=[pltpu.VMEM(v.shape, v.dtype) for v in sources]
         + [
             pltpu.VMEM((2 * n, n * toks), bf16),
-            pltpu.VMEM((2 * toks, 2 * toks), bf16),
+            pltpu.VMEM((toks, 2 * toks), bf16),
             pltpu.VMEM((toks, chans), bf16),
             pltpu.VMEM((n * toks, STATE_CT), bf16),
             pltpu.VMEM((n * toks, STATE_CT), bf16),
@@ -169,7 +168,7 @@
     )(*sources)
 
 
-def local_kernel(step_ref, decay_ref, outc_ref, inc_ref, skip_ref, g_ref, out_ref, outb, picks, step3, g3, adjs):
+def local_kernel(step_ref, decay_ref, outc_ref, inc_ref, skip_ref, g_ref, out_ref, outb, picks, g3, adjs):
     toks, chans = g_ref.shape
     n = decay_ref.shape[0]
     tiles = CT // LANES
@@ -181,7 +180,6 @@
 
     for c in range(chans // CT):
         lanes = slice(c * CT, (c + 1) * CT)
-        step3[...] = step_ref[:, lanes].reshape(blocks, BLOCK, CT)
         g3[...] = g_ref[:, lanes].astype(f32).reshape(blocks, BLOCK, CT)
         rate = [decay_ref[:, c * CT + q * LANES : c * CT + (q + 1) * LANES] * (-LOG2E) for q in range(tiles)]
 
@@ -192,7 +190,9 @@
                 ob = outb[b * BLOCK + k]
                 for q in range(tiles):
                     sl = slice(q * LANES, (q + 1) * LANES)
-                    s = jnp.broadcast_to(step3[b, k : k + 1, sl], (n, LANES))
+                    s = jnp.broadcast_to(
+                        step_ref[b, k : k + 1, c * CT + q * LANES : c * CT + (q + 1) * LANES], (n, LANES)
+                    )
                     g = jnp.broadcast_to(g3[b, k : k + 1, sl], (n, LANES))
                     adj = states[q] + ob * g
                     adjs[b, k * n : (k + 1) * n, sl] = adj.astype(bf16)
@@ -204,7 +204,7 @@
             both = jnp.dot(picks[b], adjs[b], preferred_element_type=f32)
             y = both[:BLOCK] + both[BLOCK:]
             rows = slice(b * BLOCK, (b + 1) * BLOCK)
-            out_ref[rows, lanes] = step_ref[rows, lanes] * y + skip_ref[:, lanes] * g_ref[rows, lanes].astype(f32)
+            out_ref[rows, lanes] = step_ref[b, :, lanes] * y + skip_ref[:, lanes] * g_ref[rows, lanes].astype(f32)
 
 
 def local_pass(step, decay, outc, inc, skip, g):
@@ -220,13 +220,12 @@
             pltpu.VMEM((toks, n, LANES), f32),
             pltpu.VMEM((blocks, 2 * BLOCK, BLOCK * n), bf16),
             pltpu.VMEM((blocks, BLOCK, CT), f32),
-            pltpu.VMEM((blocks, BLOCK, CT), f32),
             pltpu.VMEM((blocks, BLOCK * n, CT), bf16),
         ],
         compiler_params=pltpu.CompilerParams(vmem_limit_bytes=VMEM_BYTES),
         cost_estimate=work(13),
         name="local_pass",
-    )(step, decay, outc, inc, skip.reshape(1, -1), g)
+    )(step.reshape(blocks, BLOCK, chans), decay, outc, inc, skip.reshape(1, -1), g)
 
 
 def carry_kernel(local_ref, step_ref, later_ref, decay_ref, inc_ref, *rest):
@@ -457,13 +456,13 @@
         part,
         capacity,
     )
-    messages = [from_ahead(message, "seq", by) for by in range(1, spans)]
+    messages = [from_ahead(message, "seq", by) for by in range(2, spans)]
     if gathers:
         near = [sent[0]] + [across(v, "dp", m) for v, m in zip(sent[1:], masks[1:])]
     local = local_pass(step, decay_rate, output_coef[0], input_coef[0], skip_weight, grad_output[0])
 
     if gathers:
-        far, local, messages = lax.optimization_barrier((near[1:], local, messages))
+        far, local, messages, message = lax.optimization_barrier((near[1:], local, messages, message))
         near = near[:1] + list(far)
         packs = near + [across(v, "dp", 1) for v in near]
         own = mine(packs, part, capacity)
@@ -479,6 +478,7 @@
         )
         grad_down = lax.psum_scatter(dense, "dp", scatter_dimension=0, tiled=True)
 
+    messages = [from_ahead(message, "seq", 1)] + list(messages)
     grad_x = carry_pass(local, step, later, decay_rate, input_coef[0], messages)[None]
     return (grad_down, grad_x)
 

time: 50.6 us -> 48.3 us (0.955)
  waiting for transfers between devices: 3.69 us -> 1.02 us
    ppermute x3, waiting for transfers between devices: 1.86 us -> 0.53 us  [from_ahead(): return lax.ppermute(value, axis, [(i, i - by) for i in range(by, peers)])]
    ppermute x10, waiting for transfers between devices: 1.82 us -> 0.5 us  [across(): lax.ppermute(value, axis, [(i, i ^ mask) for i in range(lax.axis_size(axi...]
    ppermute x10, starting transfers between devices: 10.7 us -> 11.3 us  [across(): lax.ppermute(value, axis, [(i, i ^ mask) for i in range(lax.axis_size(axi...]
    unnamed x18 -> x20, local copies, waits for them, and re-layouts: 1.62 us -> 1.62 us
  transfers between devices with their start and end apart: 13 -> 13, of which waited for: 6 -> 3; matrix products, arithmetic and copies ran while one was open for 0% -> 0% of each run, Pallas kernels for 35% -> 36%
where the time goes in v4:
time: 48.3 us; the launch traced here: 48.1 us
  Pallas kernels  29.3 us (61%)
  starting transfers between devices  15.3 us (32%)
  local copies, waits for them, and re-layouts  1.62 us (3%)
  waiting for transfers between devices  1.02 us (2%)
  between operations  0.85 us (2%)
    pallas_call x1, Pallas kernels, local_pass(): pl.pallas_call(local_kernel, in_specs=[WHOLE] * 6, out_specs=WHOLE, out_s...  11.7 us
    ppermute x10, starting transfers between devices, across(): lax.ppermute(value, axis, [(i, i ^ mask) for i in range(lax.axis_size(axi...  11.3 us
    pallas_call x1, Pallas kernels, state_pass(): pl.pallas_call(functools.partial(state_kernel, masks, part), in_specs=[pl...  10 us
    pallas_call x1, Pallas kernels, carry_pass(): pl.pallas_call(carry_kernel, in_specs=[WHOLE] * (5 + len(msgs)), out_spec...  5.62 us
    ppermute x3, starting transfers between devices, from_ahead(): return lax.ppermute(value, axis, [(i, i - by) for i in range(by, peers)])  4.03 us
    pallas_call x1, Pallas kernels, weight_grad(): pl.pallas_call(functools.partial(weight_kernel, capacity, peers, step), g...  1.92 us
    unnamed x20, local copies, waits for them, and re-layouts  1.62 us
  transfers between devices with their start and end apart: 13, of which 3 were waited for; matrix products, arithmetic and copies ran while one was open for 0% of the time, Pallas kernels for 36%

profile of v4, /device:TPU:0, one launch (start us, length us, event | category | flops | bytes accessed | tf_op | source)
XLA Modules:
  0.0 48.1 jit_solution(15977318000321101848)
XLA Ops:
  0.6 0.0 copy-start.2
  0.7 10.0 %state_pass.1 = (f32[128,4096]{1,0:T(8,128)}, bf16[128,4096]{1,0:T(8,128)(2,1)}, bf16[16,4608]{1,0:T(8,128)(2,1)}, bf16[64,2048]{1,0:T(8,128)(2,1)}, bf16[64,204...) custom-call(s32[2,128]{1,0:T(2,128)} %bitcast.29, f32[2,128]{1,0:T(2,128)} %bitcast.30, ...), custom_call_target="tpu_custom_call" | custom-call | flops 80000000 | bytes 80000 | tf_op jit(solution)/shard_map/state_pass/pallas_call | solution.py:143
  10.7 3.0 %collective-permute-start = (bf16[64,2048]{1,0:T(8,128)(2,1)}, bf16[64,2048]{1,0:T(8,128)(2,1)S(1)}, u32[]{:S(2)}, u32[]{:S(2)}) collective-permute-start(bf16[64,2048]{1,0:T(8,128)(2,1)} %get-tuple-element.17), channel_id=1, source_target_pairs={{0,8},{4,12},{8,0},{12,4},{16,24},{20,28},{24,16},{28,20},{1,9},{5... | collective-permute-start | bytes 786440 | tf_op jit(solution)/shard_map/ppermute | solution.py:413
  13.7 1.5 %collective-permute-start.1 = (bf16[64,2048]{1,0:T(8,128)(2,1)}, bf16[64,2048]{1,0:T(8,128)(2,1)S(1)}, u32[]{:S(2)}, u32[]{:S(2)}) collective-permute-start(bf16[64,2048]{1,0:T(8,128)(2,1)} %get-tuple-element.18), channel_id=1, source_target_pairs={{0,16},{4,20},{8,24},{12,28},{16,0},{20,4},{24,8},{28,12},{1,17},{... | collective-permute-start | bytes 786440 | tf_op jit(solution)/shard_map/ppermute | solution.py:413
  15.3 0.0 collective-permute-start.2
  15.3 1.3 %collective-permute-start.3 = (bf16[16,4608]{1,0:T(8,128)(2,1)}, bf16[16,4608]{1,0:T(8,128)(2,1)S(1)}, u32[]{:S(2)}, u32[]{:S(2)}) collective-permute-start(bf16[16,4608]{1,0:T(8,128)(2,1)} %get-tuple-element.27), channel_id=1, source_target_pairs={{2,0},{3,1},{6,4},{7,5},{10,8},{11,9},{14,12},{15,13},{18,16},{19,... | collective-permute-start | bytes 442376 | tf_op jit(solution)/shard_map/ppermute | solution.py:409
  16.6 1.3 %collective-permute-start.4 = (bf16[16,4608]{1,0:T(8,128)(2,1)}, bf16[16,4608]{1,0:T(8,128)(2,1)S(1)}, u32[]{:S(2)}, u32[]{:S(2)}) collective-permute-start(bf16[16,4608]{1,0:T(8,128)(2,1)} %get-tuple-element.27), channel_id=1, source_target_pairs={{3,0},{7,4},{11,8},{15,12},{19,16},{23,20},{27,24},{31,28}} | collective-permute-start | bytes 442376 | tf_op jit(solution)/shard_map/ppermute | solution.py:409
  17.9 1.6 %copy-done = f32[128,4096]{1,0:T(8,128)S(1)} copy-done((f32[128,4096]{1,0:T(8,128)S(1)}, f32[128,4096]{1,0:T(8,128)}, u32[]{:S(2)}) %copy-start) | copy-done | bytes 2097176
  19.5 11.7 %local_pass.1.local_ref = f32[128,4096]{1,0:T(8,128)S(1)} custom-call(f32[8,16,4096]{2,1,0:T(8,128)S(1)} %bitcast.16, f32[16,4096]{1,0:T(8,128)S(1)} %copy-done.3, f32[16,128]{1,0:T(8,128)S(1)} %bitcast.20, f32[16,128]{1,0:T(8,128)S(1)} %bitcast.21, f32[1,4096]{1,0:T(1,128)S(1)} %bitcast.23, bf16[128,4096]{1,0:T(8,128)(2,1)S(1)} %bitcast.18), custom_call_target="tpu_custom_call" | custom-call | flops 130000000 | bytes 130000 | tf_op jit(solution)/shard_map/local_pass/pallas_call | solution.py:214
  31.2 0.0 collective-permute-done.3.rest_1_
  31.3 0.1 collective-permute-start.5
  31.3 0.0 collective-permute-done.4.rest_2_
  31.4 0.0 collective-permute-done.rest_1_
  31.4 0.0 collective-permute-done.1.rest_2_
  31.4 0.0 collective-permute-done.2.rest_3_
  31.4 0.5 %collective-permute-start.6 = (bf16[64,2048]{1,0:T(8,128)(2,1)S(1)}, bf16[64,2048]{1,0:T(8,128)(2,1)S(1)}, u32[]{:S(2)}, u32[]{:S(2)}) collective-permute-start(bf16[64,2048]{1,0:T(8,128)(2,1)S(1)} %collective-permute-done.rest_1_), channel_id=1, source_target_pairs={{0,4},{4,0},{8,12},{12,8},{16,20},{20,16},{24,28},{28,24},{1,5},{5... | collective-permute-start | bytes 786440 | tf_op jit(solution)/shard_map/ppermute | solution.py:413
  31.9 0.1 collective-permute-start.7
  32.0 0.4 collective-permute-start.8
  32.4 1.5 %collective-permute-start.12 = (bf16[16,4608]{1,0:T(8,128)(2,1)S(1)}, bf16[16,4608]{1,0:T(8,128)(2,1)S(1)}, u32[]{:S(2)}, u32[]{:S(2)}) collective-permute-start(bf16[16,4608]{1,0:T(8,128)(2,1)S(1)} %copy-done.9), channel_id=1, source_target_pairs={{1,0},{2,1},{3,2},{5,4},{6,5},{7,6},{9,8},{10,9},{11,10},{13,12},{... | collective-permute-start | bytes 442376 | tf_op jit(solution)/shard_map/ppermute | solution.py:409
  33.9 0.0 collective-permute-done.5.rest_4_
  33.9 0.0 collective-permute-done.6.rest_5_
  33.9 0.0 collective-permute-done.7.rest_6_
  33.9 0.0 collective-permute-done.8.rest_7_
  34.0 3.6 %collective-permute-start.10 = (bf16[128,256]{1,0:T(8,128)(2,1)S(1)}, bf16[128,256]{1,0:T(8,128)(2,1)S(1)}, u32[]{:S(2)}, u32[]{:S(2)}) collective-permute-start(bf16[128,256]{1,0:T(8,128)(2,1)S(1)} %own_columns.1.rest_8_), channel_id=1, source_target_pairs={{0,2},{1,3},{2,0},{3,1},{4,6},{5,7},{6,4},{7,5},{8,10},{9,11},{10,... | collective-permute-start | bytes 196616 | tf_op jit(solution)/shard_map/ppermute | solution.py:413
  37.6 1.5 %collective-permute-start.11 = (bf16[128,256]{1,0:T(8,128)(2,1)S(1)}, bf16[128,256]{1,0:T(8,128)(2,1)S(1)}, u32[]{:S(2)}, u32[]{:S(2)}) collective-permute-start(bf16[128,256]{1,0:T(8,128)(2,1)S(1)} %own_columns.1.rest_8_), channel_id=1, source_target_pairs={{0,3},{1,2},{2,1},{3,0},{4,7},{5,6},{6,5},{7,4},{8,11},{9,10},{10,... | collective-permute-start | bytes 196616 | tf_op jit(solution)/shard_map/ppermute | solution.py:413
  39.2 0.5 %collective-permute-start.9 = (bf16[128,256]{1,0:T(8,128)(2,1)S(1)}, bf16[128,256]{1,0:T(8,128)(2,1)S(1)}, u32[]{:S(2)}, u32[]{:S(2)}) collective-permute-start(bf16[128,256]{1,0:T(8,128)(2,1)S(1)} %own_columns.1.rest_8_), channel_id=1, source_target_pairs={{0,1},{1,0},{2,3},{3,2},{4,5},{5,4},{6,7},{7,6},{8,9},{9,8},{10,11... | collective-permute-start | bytes 196616 | tf_op jit(solution)/shard_map/ppermute | solution.py:413
  39.6 0.5 %collective-permute-done.12.rest_0_ = bf16[16,4608]{1,0:T(8,128)(2,1)S(1)} collective-permute-done((bf16[16,4608]{1,0:T(8,128)(2,1)S(1)}, bf16[16,4608]{1,0:T(8,128)(2,1)S(1)}, u32[]{:S(2)}, u32[]{:S(2)}) %collective-permute-start.12) | collective-permute-done | bytes 147488 | tf_op jit(solution)/shard_map/ppermute | solution.py:409
  40.2 5.6 %carry_pass.1 = bf16[128,4096]{1,0:T(8,128)(2,1)} custom-call(f32[128,4096]{1,0:T(8,128)S(1)} %local_pass.1.local_ref, f32[128,4096]{1,0:T(8,128)S(1)} %copy-done.1, bf16[128,4096]{1,0:T(8,128)(2,1)S(1)} %copy-done.5, f32[16,4096]{1,0:T(8,128)S(1)} %copy-done.3, f32[16,128]{1,0:T(8,128)S(1)} %bitcast.22, ...), custom_call_target="tpu_custom_call" | custom-call | flops 60000000 | bytes 60000 | tf_op jit(solution)/shard_map/carry_pass/pallas_call | solution.py:286
  45.8 0.2 collective-permute-done.10.rest_10_
  46.0 0.2 collective-permute-done.11.rest_11_
  46.2 0.0 collective-permute-done.9.rest_9_
  46.2 1.9 %weight_grad.1 = f32[256,1792]{1,0:T(8,128)} custom-call(bf16[64,2048]{1,0:T(8,128)(2,1)S(1)} %copy-done.4, bf16[64,2048]{1,0:T(8,128)(2,1)S(1)} %collective-permute-done.rest_1_, bf16[64,2048]{1,0:T(8,128)(2,1)S(1)} %collective-permute-done.1.rest_2_, bf16[64,2048]{1,0:T(8,128)(2,1)S(1)} %collective-permute-done.2.rest_3_, ...), custom_call_target="tpu_custom_call" | custom-call | flops 30000000 | bytes 30000 | tf_op jit(solution)/shard_map/weight_grad/pallas_call | solution.py:380
  (19 shorter events, 0.0 us)
Async XLA Ops:
  0.6 17.2 %copy-start.2 = (bf16[1,128,4096]{2,1,0:T(8,128)(2,1)S(1)}, bf16[1,128,4096]{2,1,0:T(8,128)(2,1)}, u32[]{:S(2)}) copy-start(bf16[1,128,4096]{2,1,0:T(8,128)(2,1)} %param.22) | copy-start | bytes 3145732
  0.6 17.2 %copy-start.3 = (f32[16,4096]{1,0:T(8,128)S(1)}, f32[16,4096]{1,0:T(8,128)}, u32[]{:S(2)}) copy-start(f32[16,4096]{1,0:T(8,128)} %decay_ref.3) | copy-start | bytes 786436
  0.7 17.2 %copy-start.6 = (f32[1,16,128]{2,1,0:T(8,128)S(1)}, f32[1,16,128]{2,1,0:T(8,128)}, u32[]{:S(2)}) copy-start(f32[1,16,128]{2,1,0:T(8,128)} %param.21) | copy-start | bytes 24580
  0.7 17.2 %copy-start.7 = (f32[1,16,128]{2,1,0:T(8,128)S(1)}, f32[1,16,128]{2,1,0:T(8,128)}, u32[]{:S(2)}) copy-start(f32[1,16,128]{2,1,0:T(8,128)} %param.20) | copy-start | bytes 24580
  0.7 17.2 %copy-start.8 = (f32[4096]{0:T(1024)S(1)}, f32[4096]{0:T(1024)}, u32[]{:S(2)}) copy-start(f32[4096]{0:T(1024)} %param.23) | copy-start | bytes 49156
  10.7 20.6 %collective-permute-start = (bf16[64,2048]{1,0:T(8,128)(2,1)}, bf16[64,2048]{1,0:T(8,128)(2,1)S(1)}, u32[]{:S(2)}, u32[]{:S(2)}) collective-permute-start(bf16[64,2048]{1,0:T(8,128)(2,1)} %get-tuple-element.17), channel_id=1, source_target_pairs={{0,8},{4,12},{8,0},{12,4},{16,24},{20,28},{24,16},{28,20},{1,9},{5... | collective-permute-start | bytes 786440 | tf_op jit(solution)/shard_map/ppermute | solution.py:413
  13.7 17.6 %collective-permute-start.1 = (bf16[64,2048]{1,0:T(8,128)(2,1)}, bf16[64,2048]{1,0:T(8,128)(2,1)S(1)}, u32[]{:S(2)}, u32[]{:S(2)}) collective-permute-start(bf16[64,2048]{1,0:T(8,128)(2,1)} %get-tuple-element.18), channel_id=1, source_target_pairs={{0,16},{4,20},{8,24},{12,28},{16,0},{20,4},{24,8},{28,12},{1,17},{... | collective-permute-start | bytes 786440 | tf_op jit(solution)/shard_map/ppermute | solution.py:413
  15.3 16.1 %collective-permute-start.2 = (bf16[64,2048]{1,0:T(8,128)(2,1)}, bf16[64,2048]{1,0:T(8,128)(2,1)S(1)}, u32[]{:S(2)}, u32[]{:S(2)}) collective-permute-start(bf16[64,2048]{1,0:T(8,128)(2,1)} %get-tuple-element.19), channel_id=1, source_target_pairs={{0,24},{4,28},{8,16},{12,20},{16,8},{20,12},{24,0},{28,4},{1,25},{... | collective-permute-start | bytes 786440 | tf_op jit(solution)/shard_map/ppermute | solution.py:413
  15.3 16.0 %collective-permute-start.3 = (bf16[16,4608]{1,0:T(8,128)(2,1)}, bf16[16,4608]{1,0:T(8,128)(2,1)S(1)}, u32[]{:S(2)}, u32[]{:S(2)}) collective-permute-start(bf16[16,4608]{1,0:T(8,128)(2,1)} %get-tuple-element.27), channel_id=1, source_target_pairs={{2,0},{3,1},{6,4},{7,5},{10,8},{11,9},{14,12},{15,13},{18,16},{19,... | collective-permute-start | bytes 442376 | tf_op jit(solution)/shard_map/ppermute | solution.py:409
  16.6 14.8 %collective-permute-start.4 = (bf16[16,4608]{1,0:T(8,128)(2,1)}, bf16[16,4608]{1,0:T(8,128)(2,1)S(1)}, u32[]{:S(2)}, u32[]{:S(2)}) collective-permute-start(bf16[16,4608]{1,0:T(8,128)(2,1)} %get-tuple-element.27), channel_id=1, source_target_pairs={{3,0},{7,4},{11,8},{15,12},{19,16},{23,20},{27,24},{31,28}} | collective-permute-start | bytes 442376 | tf_op jit(solution)/shard_map/ppermute | solution.py:409
  17.9 1.6 %copy-start = (f32[128,4096]{1,0:T(8,128)S(1)}, f32[128,4096]{1,0:T(8,128)}, u32[]{:S(2)}) copy-start(f32[128,4096]{1,0:T(8,128)} %get-tuple-element.20.step_ref) | copy-start | bytes 6291460
  19.5 11.7 %copy-start.4 = (bf16[64,2048]{1,0:T(8,128)(2,1)S(1)}, bf16[64,2048]{1,0:T(8,128)(2,1)}, u32[]{:S(2)}) copy-start(bf16[64,2048]{1,0:T(8,128)(2,1)} %get-tuple-element.16.rest_0_) | copy-start | bytes 786436
  19.5 12.9 %copy-start.9 = (bf16[16,4608]{1,0:T(8,128)(2,1)S(1)}, bf16[16,4608]{1,0:T(8,128)(2,1)}, u32[]{:S(2)}) copy-start(bf16[16,4608]{1,0:T(8,128)(2,1)} %get-tuple-element.27) | copy-start | bytes 442372
  19.5 20.6 %copy-start.5 = (bf16[128,4096]{1,0:T(8,128)(2,1)S(1)}, bf16[128,4096]{1,0:T(8,128)(2,1)}, u32[]{:S(2)}) copy-start(bf16[128,4096]{1,0:T(8,128)(2,1)} %get-tuple-element.26.later_ref) | copy-start | bytes 3145732
  31.2 8.9 %copy-start.1 = (f32[128,4096]{1,0:T(8,128)S(1)}, f32[128,4096]{1,0:T(8,128)}, u32[]{:S(2)}) copy-start(f32[128,4096]{1,0:T(8,128)} %get-tuple-element.20.step_ref) | copy-start | bytes 6291460
  31.3 2.6 %collective-permute-start.5 = (bf16[64,2048]{1,0:T(8,128)(2,1)S(1)}, bf16[64,2048]{1,0:T(8,128)(2,1)S(1)}, u32[]{:S(2)}, u32[]{:S(2)}) collective-permute-start(bf16[64,2048]{1,0:T(8,128)(2,1)S(1)} %copy-done.4), channel_id=1, source_target_pairs={{0,4},{4,0},{8,12},{12,8},{16,20},{20,16},{24,28},{28,24},{1,5},{5... | collective-permute-start | bytes 786440 | tf_op jit(solution)/shard_map/ppermute | solution.py:413
  31.4 2.5 %collective-permute-start.6 = (bf16[64,2048]{1,0:T(8,128)(2,1)S(1)}, bf16[64,2048]{1,0:T(8,128)(2,1)S(1)}, u32[]{:S(2)}, u32[]{:S(2)}) collective-permute-start(bf16[64,2048]{1,0:T(8,128)(2,1)S(1)} %collective-permute-done.rest_1_), channel_id=1, source_target_pairs={{0,4},{4,0},{8,12},{12,8},{16,20},{20,16},{24,28},{28,24},{1,5},{5... | collective-permute-start | bytes 786440 | tf_op jit(solution)/shard_map/ppermute | solution.py:413
  31.9 2.0 %collective-permute-start.7 = (bf16[64,2048]{1,0:T(8,128)(2,1)S(1)}, bf16[64,2048]{1,0:T(8,128)(2,1)S(1)}, u32[]{:S(2)}, u32[]{:S(2)}) collective-permute-start(bf16[64,2048]{1,0:T(8,128)(2,1)S(1)} %collective-permute-done.1.rest_2_), channel_id=1, source_target_pairs={{0,4},{4,0},{8,12},{12,8},{16,20},{20,16},{24,28},{28,24},{1,5},{5... | collective-permute-start | bytes 786440 | tf_op jit(solution)/shard_map/ppermute | solution.py:413
  32.0 2.0 %collective-permute-start.8 = (bf16[64,2048]{1,0:T(8,128)(2,1)S(1)}, bf16[64,2048]{1,0:T(8,128)(2,1)S(1)}, u32[]{:S(2)}, u32[]{:S(2)}) collective-permute-start(bf16[64,2048]{1,0:T(8,128)(2,1)S(1)} %collective-permute-done.2.rest_3_), channel_id=1, source_target_pairs={{0,4},{4,0},{8,12},{12,8},{16,20},{20,16},{24,28},{28,24},{1,5},{5... | collective-permute-start | bytes 786440 | tf_op jit(solution)/shard_map/ppermute | solution.py:413
  32.4 7.7 %collective-permute-start.12 = (bf16[16,4608]{1,0:T(8,128)(2,1)S(1)}, bf16[16,4608]{1,0:T(8,128)(2,1)S(1)}, u32[]{:S(2)}, u32[]{:S(2)}) collective-permute-start(bf16[16,4608]{1,0:T(8,128)(2,1)S(1)} %copy-done.9), channel_id=1, source_target_pairs={{1,0},{2,1},{3,2},{5,4},{6,5},{7,6},{9,8},{10,9},{11,10},{13,12},{... | collective-permute-start | bytes 442376 | tf_op jit(solution)/shard_map/ppermute | solution.py:409
  34.0 12.0 %collective-permute-start.10 = (bf16[128,256]{1,0:T(8,128)(2,1)S(1)}, bf16[128,256]{1,0:T(8,128)(2,1)S(1)}, u32[]{:S(2)}, u32[]{:S(2)}) collective-permute-start(bf16[128,256]{1,0:T(8,128)(2,1)S(1)} %own_columns.1.rest_8_), channel_id=1, source_target_pairs={{0,2},{1,3},{2,0},{3,1},{4,6},{5,7},{6,4},{7,5},{8,10},{9,11},{10,... | collective-permute-start | bytes 196616 | tf_op jit(solution)/shard_map/ppermute | solution.py:413
  37.6 8.6 %collective-permute-start.11 = (bf16[128,256]{1,0:T(8,128)(2,1)S(1)}, bf16[128,256]{1,0:T(8,128)(2,1)S(1)}, u32[]{:S(2)}, u32[]{:S(2)}) collective-permute-start(bf16[128,256]{1,0:T(8,128)(2,1)S(1)} %own_columns.1.rest_8_), channel_id=1, source_target_pairs={{0,3},{1,2},{2,1},{3,0},{4,7},{5,6},{6,5},{7,4},{8,11},{9,10},{10,... | collective-permute-start | bytes 196616 | tf_op jit(solution)/shard_map/ppermute | solution.py:413
  39.2 7.1 %collective-permute-start.9 = (bf16[128,256]{1,0:T(8,128)(2,1)S(1)}, bf16[128,256]{1,0:T(8,128)(2,1)S(1)}, u32[]{:S(2)}, u32[]{:S(2)}) collective-permute-start(bf16[128,256]{1,0:T(8,128)(2,1)S(1)} %own_columns.1.rest_8_), channel_id=1, source_target_pairs={{0,1},{1,0},{2,3},{3,2},{4,5},{5,4},{6,7},{7,6},{8,9},{9,8},{10,11... | collective-permute-start | bytes 196616 | tf_op jit(solution)/shard_map/ppermute | solution.py:413

commit v5 on v4

--- a/solution.py
+++ b/solution.py
@@ -12,7 +12,7 @@
 BLOCK = 16
 CT = 1024
 CARRY_CT = 256
-STATE_CT = 512
+STATE_CT = 256
 PREP_CT = 2048
 HALF = 8
 VMEM_BYTES = 32 * 2**20
@@ -442,7 +442,7 @@
         and hid % part == 0
         and 2 * capacity <= rows
     )
-    masks = list(range(0, peers, 2)) if gathers else []
+    masks = [0, *range(peers - 2, 0, -2)] if gathers else []
     expert = [expert_ids[0].T, gate_probs[0].T, cotangent[0], hidden_acts.T] if gathers else []
     step, later, message, *sent = state_pass(
         step_input[0],

time: 48.3 us -> 48 us (level)
  no operation moved by 1% of the time
where the time goes in v5:
time: 48 us; the launch traced here: 47.8 us
  Pallas kernels  28.9 us (60%)
  starting transfers between devices  15.4 us (32%)
  local copies, waits for them, and re-layouts  1.62 us (3%)
  waiting for transfers between devices  1.03 us (2%)
  between operations  0.85 us (2%)
    pallas_call x1, Pallas kernels, local_pass(): pl.pallas_call(local_kernel, in_specs=[WHOLE] * 6, out_specs=WHOLE, out_s...  11.7 us
    ppermute x10, starting transfers between devices, across(): lax.ppermute(value, axis, [(i, i ^ mask) for i in range(lax.axis_size(axi...  11.4 us
    pallas_call x1, Pallas kernels, state_pass(): pl.pallas_call(functools.partial(state_kernel, masks, part), in_specs=[pl...  9.68 us
    pallas_call x1, Pallas kernels, carry_pass(): pl.pallas_call(carry_kernel, in_specs=[WHOLE] * (5 + len(msgs)), out_spec...  5.62 us
    ppermute x3, starting transfers between devices, from_ahead(): return lax.ppermute(value, axis, [(i, i - by) for i in range(by, peers)])  4.03 us
    pallas_call x1, Pallas kernels, weight_grad(): pl.pallas_call(functools.partial(weight_kernel, capacity, peers, step), g...  1.92 us
    unnamed x20, local copies, waits for them, and re-layouts  1.62 us
  transfers between devices with their start and end apart: 13, of which 3 were waited for; matrix products, arithmetic and copies ran while one was open for 0% of the time, Pallas kernels for 36%

profile of v5, /device:TPU:0, one launch (start us, length us, event | category | flops | bytes accessed | tf_op | source)
XLA Modules:
  0.0 47.8 jit_solution(399117288191066947)
XLA Ops:
  0.7 9.7 %state_pass.1 = (f32[128,4096]{1,0:T(8,128)}, bf16[128,4096]{1,0:T(8,128)(2,1)}, bf16[16,4608]{1,0:T(8,128)(2,1)}, bf16[64,2048]{1,0:T(8,128)(2,1)}, bf16[64,204...) custom-call(s32[2,128]{1,0:T(2,128)} %bitcast.29, f32[2,128]{1,0:T(2,128)} %bitcast.30, ...), custom_call_target="tpu_custom_call" | custom-call | flops 80000000 | bytes 80000 | tf_op jit(solution)/shard_map/state_pass/pallas_call | solution.py:143
  10.4 4.0 %collective-permute-start = (bf16[64,2048]{1,0:T(8,128)(2,1)}, bf16[64,2048]{1,0:T(8,128)(2,1)S(1)}, u32[]{:S(2)}, u32[]{:S(2)}) collective-permute-start(bf16[64,2048]{1,0:T(8,128)(2,1)} %get-tuple-element.17), channel_id=1, source_target_pairs={{0,24},{4,28},{8,16},{12,20},{16,8},{20,12},{24,0},{28,4},{1,25},{... | collective-permute-start | bytes 786440 | tf_op jit(solution)/shard_map/ppermute | solution.py:413
  14.3 0.5 %collective-permute-start.1 = (bf16[64,2048]{1,0:T(8,128)(2,1)}, bf16[64,2048]{1,0:T(8,128)(2,1)S(1)}, u32[]{:S(2)}, u32[]{:S(2)}) collective-permute-start(bf16[64,2048]{1,0:T(8,128)(2,1)} %get-tuple-element.18), channel_id=1, source_target_pairs={{0,16},{4,20},{8,24},{12,28},{16,0},{20,4},{24,8},{28,12},{1,17},{... | collective-permute-start | bytes 786440 | tf_op jit(solution)/shard_map/ppermute | solution.py:413
  14.8 0.1 collective-permute-start.2
  15.0 1.3 %collective-permute-start.3 = (bf16[16,4608]{1,0:T(8,128)(2,1)}, bf16[16,4608]{1,0:T(8,128)(2,1)S(1)}, u32[]{:S(2)}, u32[]{:S(2)}) collective-permute-start(bf16[16,4608]{1,0:T(8,128)(2,1)} %get-tuple-element.27), channel_id=1, source_target_pairs={{2,0},{3,1},{6,4},{7,5},{10,8},{11,9},{14,12},{15,13},{18,16},{19,... | collective-permute-start | bytes 442376 | tf_op jit(solution)/shard_map/ppermute | solution.py:409
  16.3 1.3 %collective-permute-start.4 = (bf16[16,4608]{1,0:T(8,128)(2,1)}, bf16[16,4608]{1,0:T(8,128)(2,1)S(1)}, u32[]{:S(2)}, u32[]{:S(2)}) collective-permute-start(bf16[16,4608]{1,0:T(8,128)(2,1)} %get-tuple-element.27), channel_id=1, source_target_pairs={{3,0},{7,4},{11,8},{15,12},{19,16},{23,20},{27,24},{31,28}} | collective-permute-start | bytes 442376 | tf_op jit(solution)/shard_map/ppermute | solution.py:409
  17.6 1.6 %copy-done = f32[128,4096]{1,0:T(8,128)S(1)} copy-done((f32[128,4096]{1,0:T(8,128)S(1)}, f32[128,4096]{1,0:T(8,128)}, u32[]{:S(2)}) %copy-start) | copy-done | bytes 2097176
  19.2 11.7 %local_pass.1.local_ref = f32[128,4096]{1,0:T(8,128)S(1)} custom-call(f32[8,16,4096]{2,1,0:T(8,128)S(1)} %bitcast.16, f32[16,4096]{1,0:T(8,128)S(1)} %copy-done.3, f32[16,128]{1,0:T(8,128)S(1)} %bitcast.20, f32[16,128]{1,0:T(8,128)S(1)} %bitcast.21, f32[1,4096]{1,0:T(1,128)S(1)} %bitcast.23, bf16[128,4096]{1,0:T(8,128)(2,1)S(1)} %bitcast.18), custom_call_target="tpu_custom_call" | custom-call | flops 130000000 | bytes 130000 | tf_op jit(solution)/shard_map/local_pass/pallas_call | solution.py:214
  30.9 0.0 collective-permute-done.3.rest_1_
  30.9 0.0 copy-done.4
  31.0 0.1 collective-permute-start.5
  31.0 0.0 collective-permute-done.4.rest_2_
  31.0 0.0 collective-permute-done.rest_1_
  31.1 0.0 collective-permute-done.1.rest_2_
  31.1 0.0 collective-permute-done.2.rest_3_
  31.1 0.5 %collective-permute-start.6 = (bf16[64,2048]{1,0:T(8,128)(2,1)S(1)}, bf16[64,2048]{1,0:T(8,128)(2,1)S(1)}, u32[]{:S(2)}, u32[]{:S(2)}) collective-permute-start(bf16[64,2048]{1,0:T(8,128)(2,1)S(1)} %collective-permute-done.rest_1_), channel_id=1, source_target_pairs={{0,4},{4,0},{8,12},{12,8},{16,20},{20,16},{24,28},{28,24},{1,5},{5... | collective-permute-start | bytes 786440 | tf_op jit(solution)/shard_map/ppermute | solution.py:413
  31.6 0.1 collective-permute-start.7
  31.7 0.4 collective-permute-start.8
  32.1 1.5 %collective-permute-start.12 = (bf16[16,4608]{1,0:T(8,128)(2,1)S(1)}, bf16[16,4608]{1,0:T(8,128)(2,1)S(1)}, u32[]{:S(2)}, u32[]{:S(2)}) collective-permute-start(bf16[16,4608]{1,0:T(8,128)(2,1)S(1)} %copy-done.9), channel_id=1, source_target_pairs={{1,0},{2,1},{3,2},{5,4},{6,5},{7,6},{9,8},{10,9},{11,10},{13,12},{... | collective-permute-start | bytes 442376 | tf_op jit(solution)/shard_map/ppermute | solution.py:409
  33.6 0.0 collective-permute-done.5.rest_4_
  33.6 0.0 collective-permute-done.6.rest_5_
  33.6 0.0 collective-permute-done.7.rest_6_
  33.6 0.0 collective-permute-done.8.rest_7_
  33.7 3.6 %collective-permute-start.10 = (bf16[128,256]{1,0:T(8,128)(2,1)S(1)}, bf16[128,256]{1,0:T(8,128)(2,1)S(1)}, u32[]{:S(2)}, u32[]{:S(2)}) collective-permute-start(bf16[128,256]{1,0:T(8,128)(2,1)S(1)} %own_columns.1.rest_8_), channel_id=1, source_target_pairs={{0,2},{1,3},{2,0},{3,1},{4,6},{5,7},{6,4},{7,5},{8,10},{9,11},{10,... | collective-permute-start | bytes 196616 | tf_op jit(solution)/shard_map/ppermute | solution.py:413
  37.3 1.5 %collective-permute-start.11 = (bf16[128,256]{1,0:T(8,128)(2,1)S(1)}, bf16[128,256]{1,0:T(8,128)(2,1)S(1)}, u32[]{:S(2)}, u32[]{:S(2)}) collective-permute-start(bf16[128,256]{1,0:T(8,128)(2,1)S(1)} %own_columns.1.rest_8_), channel_id=1, source_target_pairs={{0,3},{1,2},{2,1},{3,0},{4,7},{5,6},{6,5},{7,4},{8,11},{9,10},{10,... | collective-permute-start | bytes 196616 | tf_op jit(solution)/shard_map/ppermute | solution.py:413
  38.8 0.5 %collective-permute-start.9 = (bf16[128,256]{1,0:T(8,128)(2,1)S(1)}, bf16[128,256]{1,0:T(8,128)(2,1)S(1)}, u32[]{:S(2)}, u32[]{:S(2)}) collective-permute-start(bf16[128,256]{1,0:T(8,128)(2,1)S(1)} %own_columns.1.rest_8_), channel_id=1, source_target_pairs={{0,1},{1,0},{2,3},{3,2},{4,5},{5,4},{6,7},{7,6},{8,9},{9,8},{10,11... | collective-permute-start | bytes 196616 | tf_op jit(solution)/shard_map/ppermute | solution.py:413
  39.3 0.5 %collective-permute-done.12.rest_0_ = bf16[16,4608]{1,0:T(8,128)(2,1)S(1)} collective-permute-done((bf16[16,4608]{1,0:T(8,128)(2,1)S(1)}, bf16[16,4608]{1,0:T(8,128)(2,1)S(1)}, u32[]{:S(2)}, u32[]{:S(2)}) %collective-permute-start.12) | collective-permute-done | bytes 147488 | tf_op jit(solution)/shard_map/ppermute | solution.py:409
  39.9 5.6 %carry_pass.1 = bf16[128,4096]{1,0:T(8,128)(2,1)} custom-call(f32[128,4096]{1,0:T(8,128)S(1)} %local_pass.1.local_ref, f32[128,4096]{1,0:T(8,128)S(1)} %copy-done.1, bf16[128,4096]{1,0:T(8,128)(2,1)S(1)} %copy-done.5, f32[16,4096]{1,0:T(8,128)S(1)} %copy-done.3, f32[16,128]{1,0:T(8,128)S(1)} %bitcast.22, ...), custom_call_target="tpu_custom_call" | custom-call | flops 60000000 | bytes 60000 | tf_op jit(solution)/shard_map/carry_pass/pallas_call | solution.py:286
  45.5 0.2 collective-permute-done.10.rest_10_
  45.7 0.2 collective-permute-done.11.rest_11_
  45.9 0.0 collective-permute-done.9.rest_9_
  45.9 1.9 %weight_grad.1 = f32[256,1792]{1,0:T(8,128)} custom-call(bf16[64,2048]{1,0:T(8,128)(2,1)S(1)} %copy-done.4, bf16[64,2048]{1,0:T(8,128)(2,1)S(1)} %collective-permute-done.rest_1_, bf16[64,2048]{1,0:T(8,128)(2,1)S(1)} %collective-permute-done.1.rest_2_, bf16[64,2048]{1,0:T(8,128)(2,1)S(1)} %collective-permute-done.2.rest_3_, ...), custom_call_target="tpu_custom_call" | custom-call | flops 30000000 | bytes 30000 | tf_op jit(solution)/shard_map/weight_grad/pallas_call | solution.py:380
  (19 shorter events, 0.0 us)
Async XLA Ops:
  0.6 16.9 %copy-start.2 = (bf16[1,128,4096]{2,1,0:T(8,128)(2,1)S(1)}, bf16[1,128,4096]{2,1,0:T(8,128)(2,1)}, u32[]{:S(2)}) copy-start(bf16[1,128,4096]{2,1,0:T(8,128)(2,1)} %param.22) | copy-start | bytes 3145732
  0.6 16.9 %copy-start.3 = (f32[16,4096]{1,0:T(8,128)S(1)}, f32[16,4096]{1,0:T(8,128)}, u32[]{:S(2)}) copy-start(f32[16,4096]{1,0:T(8,128)} %decay_ref.3) | copy-start | bytes 786436
  0.7 16.9 %copy-start.6 = (f32[1,16,128]{2,1,0:T(8,128)S(1)}, f32[1,16,128]{2,1,0:T(8,128)}, u32[]{:S(2)}) copy-start(f32[1,16,128]{2,1,0:T(8,128)} %param.21) | copy-start | bytes 24580
  0.7 16.9 %copy-start.7 = (f32[1,16,128]{2,1,0:T(8,128)S(1)}, f32[1,16,128]{2,1,0:T(8,128)}, u32[]{:S(2)}) copy-start(f32[1,16,128]{2,1,0:T(8,128)} %param.20) | copy-start | bytes 24580
  0.7 16.9 %copy-start.8 = (f32[4096]{0:T(1024)S(1)}, f32[4096]{0:T(1024)}, u32[]{:S(2)}) copy-start(f32[4096]{0:T(1024)} %param.23) | copy-start | bytes 49156
  10.4 20.7 %collective-permute-start = (bf16[64,2048]{1,0:T(8,128)(2,1)}, bf16[64,2048]{1,0:T(8,128)(2,1)S(1)}, u32[]{:S(2)}, u32[]{:S(2)}) collective-permute-start(bf16[64,2048]{1,0:T(8,128)(2,1)} %get-tuple-element.17), channel_id=1, source_target_pairs={{0,24},{4,28},{8,16},{12,20},{16,8},{20,12},{24,0},{28,4},{1,25},{... | collective-permute-start | bytes 786440 | tf_op jit(solution)/shard_map/ppermute | solution.py:413
  14.3 16.7 %collective-permute-start.1 = (bf16[64,2048]{1,0:T(8,128)(2,1)}, bf16[64,2048]{1,0:T(8,128)(2,1)S(1)}, u32[]{:S(2)}, u32[]{:S(2)}) collective-permute-start(bf16[64,2048]{1,0:T(8,128)(2,1)} %get-tuple-element.18), channel_id=1, source_target_pairs={{0,16},{4,20},{8,24},{12,28},{16,0},{20,4},{24,8},{28,12},{1,17},{... | collective-permute-start | bytes 786440 | tf_op jit(solution)/shard_map/ppermute | solution.py:413
  14.8 16.2 %collective-permute-start.2 = (bf16[64,2048]{1,0:T(8,128)(2,1)}, bf16[64,2048]{1,0:T(8,128)(2,1)S(1)}, u32[]{:S(2)}, u32[]{:S(2)}) collective-permute-start(bf16[64,2048]{1,0:T(8,128)(2,1)} %get-tuple-element.19), channel_id=1, source_target_pairs={{0,8},{4,12},{8,0},{12,4},{16,24},{20,28},{24,16},{28,20},{1,9},{5... | collective-permute-start | bytes 786440 | tf_op jit(solution)/shard_map/ppermute | solution.py:413
  15.0 16.0 %collective-permute-start.3 = (bf16[16,4608]{1,0:T(8,128)(2,1)}, bf16[16,4608]{1,0:T(8,128)(2,1)S(1)}, u32[]{:S(2)}, u32[]{:S(2)}) collective-permute-start(bf16[16,4608]{1,0:T(8,128)(2,1)} %get-tuple-element.27), channel_id=1, source_target_pairs={{2,0},{3,1},{6,4},{7,5},{10,8},{11,9},{14,12},{15,13},{18,16},{19,... | collective-permute-start | bytes 442376 | tf_op jit(solution)/shard_map/ppermute | solution.py:409
  16.3 14.8 %collective-permute-start.4 = (bf16[16,4608]{1,0:T(8,128)(2,1)}, bf16[16,4608]{1,0:T(8,128)(2,1)S(1)}, u32[]{:S(2)}, u32[]{:S(2)}) collective-permute-start(bf16[16,4608]{1,0:T(8,128)(2,1)} %get-tuple-element.27), channel_id=1, source_target_pairs={{3,0},{7,4},{11,8},{15,12},{19,16},{23,20},{27,24},{31,28}} | collective-permute-start | bytes 442376 | tf_op jit(solution)/shard_map/ppermute | solution.py:409
  17.6 1.6 %copy-start = (f32[128,4096]{1,0:T(8,128)S(1)}, f32[128,4096]{1,0:T(8,128)}, u32[]{:S(2)}) copy-start(f32[128,4096]{1,0:T(8,128)} %get-tuple-element.20.step_ref) | copy-start | bytes 6291460
  19.2 11.7 %copy-start.4 = (bf16[64,2048]{1,0:T(8,128)(2,1)S(1)}, bf16[64,2048]{1,0:T(8,128)(2,1)}, u32[]{:S(2)}) copy-start(bf16[64,2048]{1,0:T(8,128)(2,1)} %get-tuple-element.16.rest_0_) | copy-start | bytes 786436
  19.2 12.9 %copy-start.9 = (bf16[16,4608]{1,0:T(8,128)(2,1)S(1)}, bf16[16,4608]{1,0:T(8,128)(2,1)}, u32[]{:S(2)}) copy-start(bf16[16,4608]{1,0:T(8,128)(2,1)} %get-tuple-element.27) | copy-start | bytes 442372
  19.2 20.6 %copy-start.5 = (bf16[128,4096]{1,0:T(8,128)(2,1)S(1)}, bf16[128,4096]{1,0:T(8,128)(2,1)}, u32[]{:S(2)}) copy-start(bf16[128,4096]{1,0:T(8,128)(2,1)} %get-tuple-element.26.later_ref) | copy-start | bytes 3145732
  30.9 8.9 %copy-start.1 = (f32[128,4096]{1,0:T(8,128)S(1)}, f32[128,4096]{1,0:T(8,128)}, u32[]{:S(2)}) copy-start(f32[128,4096]{1,0:T(8,128)} %get-tuple-element.20.step_ref) | copy-start | bytes 6291460
  31.0 2.6 %collective-permute-start.5 = (bf16[64,2048]{1,0:T(8,128)(2,1)S(1)}, bf16[64,2048]{1,0:T(8,128)(2,1)S(1)}, u32[]{:S(2)}, u32[]{:S(2)}) collective-permute-start(bf16[64,2048]{1,0:T(8,128)(2,1)S(1)} %copy-done.4), channel_id=1, source_target_pairs={{0,4},{4,0},{8,12},{12,8},{16,20},{20,16},{24,28},{28,24},{1,5},{5... | collective-permute-start | bytes 786440 | tf_op jit(solution)/shard_map/ppermute | solution.py:413
  31.1 2.5 %collective-permute-start.6 = (bf16[64,2048]{1,0:T(8,128)(2,1)S(1)}, bf16[64,2048]{1,0:T(8,128)(2,1)S(1)}, u32[]{:S(2)}, u32[]{:S(2)}) collective-permute-start(bf16[64,2048]{1,0:T(8,128)(2,1)S(1)} %collective-permute-done.rest_1_), channel_id=1, source_target_pairs={{0,4},{4,0},{8,12},{12,8},{16,20},{20,16},{24,28},{28,24},{1,5},{5... | collective-permute-start | bytes 786440 | tf_op jit(solution)/shard_map/ppermute | solution.py:413
  31.6 2.0 %collective-permute-start.7 = (bf16[64,2048]{1,0:T(8,128)(2,1)S(1)}, bf16[64,2048]{1,0:T(8,128)(2,1)S(1)}, u32[]{:S(2)}, u32[]{:S(2)}) collective-permute-start(bf16[64,2048]{1,0:T(8,128)(2,1)S(1)} %collective-permute-done.1.rest_2_), channel_id=1, source_target_pairs={{0,4},{4,0},{8,12},{12,8},{16,20},{20,16},{24,28},{28,24},{1,5},{5... | collective-permute-start | bytes 786440 | tf_op jit(solution)/shard_map/ppermute | solution.py:413
  31.7 2.0 %collective-permute-start.8 = (bf16[64,2048]{1,0:T(8,128)(2,1)S(1)}, bf16[64,2048]{1,0:T(8,128)(2,1)S(1)}, u32[]{:S(2)}, u32[]{:S(2)}) collective-permute-start(bf16[64,2048]{1,0:T(8,128)(2,1)S(1)} %collective-permute-done.2.rest_3_), channel_id=1, source_target_pairs={{0,4},{4,0},{8,12},{12,8},{16,20},{20,16},{24,28},{28,24},{1,5},{5... | collective-permute-start | bytes 786440 | tf_op jit(solution)/shard_map/ppermute | solution.py:413
  32.1 7.7 %collective-permute-start.12 = (bf16[16,4608]{1,0:T(8,128)(2,1)S(1)}, bf16[16,4608]{1,0:T(8,128)(2,1)S(1)}, u32[]{:S(2)}, u32[]{:S(2)}) collective-permute-start(bf16[16,4608]{1,0:T(8,128)(2,1)S(1)} %copy-done.9), channel_id=1, source_target_pairs={{1,0},{2,1},{3,2},{5,4},{6,5},{7,6},{9,8},{10,9},{11,10},{13,12},{... | collective-permute-start | bytes 442376 | tf_op jit(solution)/shard_map/ppermute | solution.py:409
  33.7 12.0 %collective-permute-start.10 = (bf16[128,256]{1,0:T(8,128)(2,1)S(1)}, bf16[128,256]{1,0:T(8,128)(2,1)S(1)}, u32[]{:S(2)}, u32[]{:S(2)}) collective-permute-start(bf16[128,256]{1,0:T(8,128)(2,1)S(1)} %own_columns.1.rest_8_), channel_id=1, source_target_pairs={{0,2},{1,3},{2,0},{3,1},{4,6},{5,7},{6,4},{7,5},{8,10},{9,11},{10,... | collective-permute-start | bytes 196616 | tf_op jit(solution)/shard_map/ppermute | solution.py:413
  37.3 8.6 %collective-permute-start.11 = (bf16[128,256]{1,0:T(8,128)(2,1)S(1)}, bf16[128,256]{1,0:T(8,128)(2,1)S(1)}, u32[]{:S(2)}, u32[]{:S(2)}) collective-permute-start(bf16[128,256]{1,0:T(8,128)(2,1)S(1)} %own_columns.1.rest_8_), channel_id=1, source_target_pairs={{0,3},{1,2},{2,1},{3,0},{4,7},{5,6},{6,5},{7,4},{8,11},{9,10},{10,... | collective-permute-start | bytes 196616 | tf_op jit(solution)/shard_map/ppermute | solution.py:413
  38.8 7.1 %collective-permute-start.9 = (bf16[128,256]{1,0:T(8,128)(2,1)S(1)}, bf16[128,256]{1,0:T(8,128)(2,1)S(1)}, u32[]{:S(2)}, u32[]{:S(2)}) collective-permute-start(bf16[128,256]{1,0:T(8,128)(2,1)S(1)} %own_columns.1.rest_8_), channel_id=1, source_target_pairs={{0,1},{1,0},{2,3},{3,2},{4,5},{5,4},{6,7},{7,6},{8,9},{9,8},{10,11... | collective-permute-start | bytes 196616 | tf_op jit(solution)/shard_map/ppermute | solution.py:413
